TPU v7x, 512 devices: a whole 4x4x16 slice. The times are simulated.
512 devices in a mesh: inst: 64 (over z, y), tp: 8 (over x, core).
Axes of the slice: x: 4, y: 4, z: 16, core: 2. Of those that a mesh axis runs over, the one named last changes fastest.
Arguments:
- anchor: int32 [1024], P('inst'), may hold values from 0 to 1023, as said below
- target: int32 [1024], P('inst'), may hold values from 0 to 1023, as said below
- ssm_state: float32 [1024, 16, 8192], P('inst', None, 'tp'), may hold values from -0.04 to 0.04
- conv_state: float32 [1024, 3, 8192], P('inst', None, 'tp'), may hold values from -6 to 6
- x_in: bfloat16 [1024, 2, 8192], P('inst', None, 'tp'), may hold values from -6 to 6
- gate_in: bfloat16 [1024, 2, 8192], P('inst', None, 'tp'), may hold values from -6 to 6
- conv_weight: float32 [4, 8192], P(None, 'tp'), may hold values from -3 to 3
- x_weight: bfloat16 [8192, 544], P('tp'), may hold values from -0.0625 to 0.0625
- dt_weight: bfloat16 [512, 8192], P(None, 'tp'), may hold values from -0.25 to 0.25
- dt_bias: float32 [8192], P('tp'), may hold values from -5 to -3
- a_log: float32 [16, 8192], P(None, 'tp'), may hold values from 0 to 2.5
- d_skip: float32 [8192], P('tp'), may hold values from 0.5 to 1.5
- dt_gain: float32 [512], replicated, may hold values from 0.25 to 1.75
Outputs:
- mixed: bfloat16 [1024, 2, 8192], P('inst', None, 'tp')
- ssm_final: float32 [1024, 16, 8192], P('inst', None, 'tp')
Inputs may be any that keep to these rules, and one draw needn't show every extreme that they name: `anchor`: a permutation of the slots; the slots of one instance take states of at most one slot of any other instance, and exactly 12 of them take states from other instances; the offsets, modulo 64, from the sending instance to the receiving one are the same 12 distinct nonzero offsets for every instance. `target`: the inverse permutation of anchor.
All inputs are finite; a program needn't handle non-finite values.
Results may differ from a plain program's by a relative error of at most 0.013.
Values sent between devices are 32-bit elements; how exact they have to be, the bound alone decides.
No kernel may reach another device: no remote copies, remote signals or barrier semaphores. Data moves between devices by JAX's collectives and lax.ppermute only.
A program may use at most 64 MiB of HBM per device.

v0:
```python
import jax
import jax.numpy as jnp
from jax import lax
from jax.sharding import PartitionSpec as P

DTR = 512
GROUPS = 12


def shifted(array, axis, by):
    size = lax.axis_size(axis)
    return lax.ppermute(array, axis, [(i, (i + by) % size) for i in range(size)])


def finish(totals, dt_gain):
    dt_part = totals[:, :DTR]
    inv_rms = lax.rsqrt(jnp.mean(dt_part * dt_part, axis=-1, keepdims=True) + 1e-06)
    return ((dt_part * inv_rms * dt_gain).astype(jnp.bfloat16), totals[:, DTR:])


def combine(partial_sums, dt_gain):
    totals = lax.psum(partial_sums, "tp")
    return finish(totals, dt_gain)


def decode(
    state,
    conv_rows,
    x_in,
    gate_in,
    conv_weight,
    x_weight,
    dt_weight,
    dt_bias,
    a_log,
    d_skip,
    dt_gain,
):
    decay_rates = jnp.exp(a_log)
    state_size = a_log.shape[0]
    results = []
    for step_index in range(x_in.shape[1]):
        window = jnp.concatenate(
            [conv_rows, x_in[:, step_index : step_index + 1].astype(jnp.float32)], axis=1
        )
        conved = jax.nn.silu(jnp.sum(window * conv_weight[None], axis=1)).astype(jnp.bfloat16)
        conv_rows = window[:, 1:]
        dt_low, bc_rest = combine(
            jnp.dot(conved, x_weight, preferred_element_type=jnp.float32), dt_gain
        )
        b_vector = bc_rest[:, :state_size]
        c_vector = bc_rest[:, state_size:]
        step_size = jax.nn.softplus(
            jnp.dot(dt_low, dt_weight, preferred_element_type=jnp.float32) + dt_bias
        )
        x_values = conved.astype(jnp.float32)
        state = (
            jnp.exp(-step_size[:, None, :] * decay_rates[None]) * state
            + (step_size * x_values)[:, None, :] * b_vector[:, :, None]
        )
        y_output = jnp.sum(c_vector[:, :, None] * state, axis=1) + d_skip * x_values
        gate_values = jax.nn.silu(gate_in[:, step_index].astype(jnp.float32))
        results.append((y_output * gate_values).astype(jnp.bfloat16))
    return (jnp.stack(results, axis=1), state)


def offset_rank(offsets):
    active = offsets != 0
    earlier = active[None, :] & active[:, None] & (offsets[None, :] < offsets[:, None])
    return (jnp.sum(earlier.astype(jnp.int32), axis=1), active)


def sectioned_moves(ssm_state, conv_state, target, self_index, peer_count, slot_ids):
    slot_count = target.shape[0]
    leave_offset = (target // slot_count - self_index) % peer_count
    leave_rank, moving = offset_rank(leave_offset)
    group_ids = jnp.arange(GROUPS, dtype=jnp.int32)
    picks = (leave_rank[None, :] == group_ids[:, None]) & moving[None, :]
    picked = jnp.sum(jnp.where(picks, slot_ids[None, :], 0), axis=1)
    row_offset = jnp.take(leave_offset, picked, axis=0)
    held_ssm = jnp.take(ssm_state, picked, axis=0)
    held_conv = jnp.take(conv_state, picked, axis=0)
    for level in range(peer_count.bit_length() - 1):
        moved_ssm, moved_conv = shifted((held_ssm, held_conv), "inst", 1 << level)
        going = row_offset // (1 << level) % 2 == 1
        held_ssm = jnp.where(going[:, None, None], moved_ssm, held_ssm)
        held_conv = jnp.where(going[:, None, None], moved_conv, held_conv)
    return (held_ssm, held_conv)


def local(
    anchor,
    target,
    ssm_state,
    conv_state,
    x_in,
    gate_in,
    conv_weight,
    x_weight,
    dt_weight,
    dt_bias,
    a_log,
    d_skip,
    dt_gain,
):
    slot_count = anchor.shape[0]
    peer_count = lax.axis_size("inst")
    self_index = lax.axis_index("inst")
    weights = (conv_weight, x_weight, dt_weight, dt_bias, a_log, d_skip, dt_gain)
    slot_ids = jnp.arange(slot_count, dtype=jnp.int32)
    from_inst = anchor // slot_count
    is_local = from_inst == self_index
    held_ssm, held_conv = sectioned_moves(
        ssm_state, conv_state, target, self_index, peer_count, slot_ids
    )
    arrive_offset = (self_index - from_inst) % peer_count
    row_of = offset_rank(arrive_offset)[0]
    local_ssm = jnp.take(
        ssm_state,
        jnp.argmax(
            (target[None, :] % slot_count == slot_ids[:, None])
            & (target[None, :] // slot_count == self_index),
            axis=1,
        ),
        axis=0,
    )
    local_conv = jnp.take(conv_state, anchor % slot_count, axis=0)
    arrived_ssm = jnp.take(held_ssm, row_of, axis=0)
    arrived_conv = jnp.take(held_conv, row_of, axis=0)
    new_ssm = jnp.where(is_local[:, None, None], local_ssm, arrived_ssm)
    new_conv = jnp.where(is_local[:, None, None], local_conv, arrived_conv)
    return decode(new_ssm, new_conv, x_in, gate_in, *weights)


def solution(mesh):
    return jax.shard_map(
        local,
        mesh=mesh,
        in_specs=(
            P("inst"),
            P("inst"),
            P("inst", None, "tp"),
            P("inst", None, "tp"),
            P("inst", None, "tp"),
            P("inst", None, "tp"),
            P(None, "tp"),
            P("tp", None),
            P(None, "tp"),
            P("tp"),
            P(None, "tp"),
            P("tp"),
            P(),
        ),
        out_specs=(P("inst", None, "tp"), P("inst", None, "tp")),
        check_vma=False,
    )
```

profile of v0, /device:TPU:16, one launch (start us, length us, event | category | flops | bytes accessed | tf_op | source)
XLA Modules:
  0.0 350.5 jit_solution(18318665899515837666)
XLA Ops:
  9.7 1.8 gather_fusion.5
  11.7 3.3 collective-permute-start.6
  16.0 3.5 collective-permute-start
  21.9 15.3 %collective-permute-done = f32[12,3,1024]{2,0,1:T(8,128)S(1)} collective-permute-done((f32[12,3,1024]{2,0,1:T(8,128)S(1)}, f32[12,3,1024]{2,0,1:T(8,128)S(1)}, u32[]{:S(2)}, u32[]{:S(2)}) %collective-permute-start) | collective-permute-done | bytes 147488 | tf_op jit(solution)/shard_map/ppermute | solution.py:12
  37.3 5.7 %collective-permute-start.1 = (f32[12,3,1024]{2,0,1:T(8,128)S(1)}, f32[12,3,1024]{2,0,1:T(8,128)S(1)}, u32[]{:S(2)}, u32[]{:S(2)}) collective-permute-start(f32[12,3,1024]{2,0,1:T(8,128)S(1)} %broadcast_select_fusion.8), channel_id=1, source_target_pairs={{0,16},{8,24},{16,32},{24,40},{32,48},{40,56},{48,64},{56,72},{64,... | collective-permute-start | bytes 442376 | tf_op jit(solution)/shard_map/ppermute | solution.py:12
  43.0 11.1 %collective-permute-done.1 = f32[12,3,1024]{2,0,1:T(8,128)S(1)} collective-permute-done((f32[12,3,1024]{2,0,1:T(8,128)S(1)}, f32[12,3,1024]{2,0,1:T(8,128)S(1)}, u32[]{:S(2)}, u32[]{:S(2)}) %collective-permute-start.1) | collective-permute-done | bytes 147488 | tf_op jit(solution)/shard_map/ppermute | solution.py:12
  54.2 1.9 collective-permute-start.2
  56.1 1.3 broadcast_select_fusion.1
  57.5 1.9 collective-permute-start.7
  59.4 3.6 %collective-permute-done.2 = f32[12,3,1024]{2,0,1:T(8,128)S(1)} collective-permute-done((f32[12,3,1024]{2,0,1:T(8,128)S(1)}, f32[12,3,1024]{2,0,1:T(8,128)S(1)}, u32[]{:S(2)}, u32[]{:S(2)}) %collective-permute-start.2) | collective-permute-done | bytes 147488 | tf_op jit(solution)/shard_map/ppermute | solution.py:12
  63.1 4.2 %collective-permute-start.3 = (f32[12,3,1024]{2,0,1:T(8,128)S(1)}, f32[12,3,1024]{2,0,1:T(8,128)S(1)}, u32[]{:S(2)}, u32[]{:S(2)}) collective-permute-start(f32[12,3,1024]{2,0,1:T(8,128)S(1)} %broadcast_select_fusion.10), channel_id=1, source_target_pairs={{0,64},{8,72},{16,80},{24,88},{32,96},{40,104},{48,112},{56,120},{... | collective-permute-start | bytes 442376 | tf_op jit(solution)/shard_map/ppermute | solution.py:12
  67.3 28.7 %collective-permute-done.3 = f32[12,3,1024]{2,0,1:T(8,128)S(1)} collective-permute-done((f32[12,3,1024]{2,0,1:T(8,128)S(1)}, f32[12,3,1024]{2,0,1:T(8,128)S(1)}, u32[]{:S(2)}, u32[]{:S(2)}) %collective-permute-start.3) | collective-permute-done | bytes 147488 | tf_op jit(solution)/shard_map/ppermute | solution.py:12
  96.1 1.9 collective-permute-start.4
  98.2 1.9 collective-permute-start.8
  100.2 12.0 %collective-permute-done.4 = f32[12,3,1024]{2,0,1:T(8,128)S(1)} collective-permute-done((f32[12,3,1024]{2,0,1:T(8,128)S(1)}, f32[12,3,1024]{2,0,1:T(8,128)S(1)}, u32[]{:S(2)}, u32[]{:S(2)}) %collective-permute-start.4) | collective-permute-done | bytes 147488 | tf_op jit(solution)/shard_map/ppermute | solution.py:12
  112.3 9.9 %collective-permute-start.5 = (f32[12,3,1024]{2,0,1:T(8,128)S(1)}, f32[12,3,1024]{2,0,1:T(8,128)S(1)}, u32[]{:S(2)}, u32[]{:S(2)}) collective-permute-start(f32[12,3,1024]{2,0,1:T(8,128)S(1)} %broadcast_select_fusion.12), channel_id=1, source_target_pairs={{0,256},{8,264},{16,272},{24,280},{32,288},{40,296},{48,304},{56,3... | collective-permute-start | bytes 442376 | tf_op jit(solution)/shard_map/ppermute | solution.py:12
  123.1 25.4 %collective-permute-done.5 = f32[12,3,1024]{2,0,1:T(8,128)S(1)} collective-permute-done((f32[12,3,1024]{2,0,1:T(8,128)S(1)}, f32[12,3,1024]{2,0,1:T(8,128)S(1)}, u32[]{:S(2)}, u32[]{:S(2)}) %collective-permute-start.5) | collective-permute-done | bytes 147488 | tf_op jit(solution)/shard_map/ppermute | solution.py:12
  149.4 1.0 broadcast_select_fusion.3
  150.4 2.0 collective-permute-start.9
  152.7 1.0 fusion.44
  153.7 1.0 fusion.45
  154.8 25.1 %collective-permute-done.9 = f32[12,16,1024]{2,1,0:T(8,128)S(1)} collective-permute-done((f32[12,16,1024]{2,1,0:T(8,128)}, f32[12,16,1024]{2,1,0:T(8,128)S(1)}, u32[]{:S(2)}, u32[]{:S(2)}) %collective-permute-start.9) | collective-permute-done | bytes 786464 | tf_op jit(solution)/shard_map/ppermute | solution.py:12
  179.9 2.2 broadcast_select_fusion.4
  182.1 44.1 %collective-permute-start.10 = (f32[12,16,1024]{2,1,0:T(8,128)}, f32[12,16,1024]{2,1,0:T(8,128)}, u32[]{:S(2)}, u32[]{:S(2)}) collective-permute-start(f32[12,16,1024]{2,1,0:T(8,128)} %broadcast_select_fusion.4), channel_id=1, source_target_pairs={{0,128},{8,136},{16,144},{24,152},{32,160},{40,168},{48,176},{56,1... | collective-permute-start | bytes 2359304 | tf_op jit(solution)/shard_map/ppermute | solution.py:12
  226.9 5.5 %all-reduce.3.cloned.1.call-done = (f32[16,544]{1,0:T(8,128)}, f32[16,544]{1,0:T(8,128)}) async-done(((f32[16,544]{1,0:T(8,128)}, f32[16,544]{1,0:T(8,128)}), (f32[16,544]{1,0:T(8,128)}, f32[16,544]{1,0:T(8,128)})) %all-reduce.3.cloned.1.call-update) | async-done | bytes 69648 | tf_op jit(solution)/shard_map/psum | solution.py:22
  235.0 20.8 %collective-permute-done.10 = f32[12,16,1024]{2,1,0:T(8,128)} collective-permute-done((f32[12,16,1024]{2,1,0:T(8,128)}, f32[12,16,1024]{2,1,0:T(8,128)}, u32[]{:S(2)}, u32[]{:S(2)}) %collective-permute-start.10) | collective-permute-done | bytes 786464 | tf_op jit(solution)/shard_map/ppermute | solution.py:12
  255.7 1.5 broadcast_select_fusion.5
  257.2 2.6 collective-permute-start.11
  260.6 77.2 %collective-permute-done.11 = f32[12,16,1024]{2,1,0:T(8,128)S(1)} collective-permute-done((f32[12,16,1024]{2,1,0:T(8,128)S(1)}, f32[12,16,1024]{2,1,0:T(8,128)S(1)}, u32[]{:S(2)}, u32[]{:S(2)}) %collective-permute-start.11) | collective-permute-done | bytes 786464 | tf_op jit(solution)/shard_map/ppermute | solution.py:12
  337.9 1.6 gather_fusion.6
  339.5 1.9 multiply_reduce_fusion.1
  341.4 1.5 multiply_reduce_fusion
  (94 shorter events, 13.4 us)
Async XLA Ops:
  7.2 145.5 %copy-start = (bf16[1024,544]{0,1:T(8,128)(2,1)S(1)}, bf16[1024,544]{0,1:T(8,128)(2,1)}, u32[]{:S(2)}) copy-start(bf16[1024,544]{0,1:T(8,128)(2,1)} %param.20) | copy-start | bytes 3342340
  7.2 225.2 %all-reduce.3.cloned.1.call-start = ((), (), s32[]{:S(2)}) async-start(), calls=%async_computation | async-start | bytes 163840 | tf_op jit(solution)/shard_map/psum | solution.py:22
  11.5 3.5 %copy-start.1 = (f32[16,3,1024]{2,0,1:T(8,128)S(1)}, f32[16,3,1024]{2,0,1:T(8,128)}, u32[]{:S(2)}) copy-start(f32[16,3,1024]{2,0,1:T(8,128)} %param.16) | copy-start | bytes 589828
  11.7 7.8 %copy-start.17 = (s32[16]{0:T(128)S(1)}, s32[16]{0:T(128)}, u32[]{:S(2)}) copy-start(s32[16]{0:T(128)} %param.14) | copy-start | bytes 196
  11.7 7.8 %copy-start.5 = (bf16[16,2,1024]{2,1,0:T(2,128)(2,1)S(1)}, bf16[16,2,1024]{2,1,0:T(2,128)(2,1)}, u32[]{:S(2)}) copy-start(bf16[16,2,1024]{2,1,0:T(2,128)(2,1)} %param.17) | copy-start | bytes 196612
  11.7 7.9 %copy-start.6 = (bf16[16,2,1024]{2,1,0:T(2,128)(2,1)S(1)}, bf16[16,2,1024]{2,1,0:T(2,128)(2,1)}, u32[]{:S(2)}) copy-start(bf16[16,2,1024]{2,1,0:T(2,128)(2,1)} %param.18) | copy-start | bytes 196612
  11.7 44.4 %collective-permute-start.6 = (f32[12,16,1024]{2,1,0:T(8,128)S(1)}, f32[12,16,1024]{2,1,0:T(8,128)}, u32[]{:S(2)}, u32[]{:S(2)}) collective-permute-start(f32[12,16,1024]{2,1,0:T(8,128)S(1)} %broadcast_select_fusion), channel_id=1, source_target_pairs={{0,8},{8,16},{16,24},{24,32},{32,40},{40,48},{48,56},{56,64},{64,7... | collective-permute-start | bytes 2359304 | tf_op jit(solution)/shard_map/ppermute | solution.py:12
  16.0 21.2 %collective-permute-start = (f32[12,3,1024]{2,0,1:T(8,128)S(1)}, f32[12,3,1024]{2,0,1:T(8,128)S(1)}, u32[]{:S(2)}, u32[]{:S(2)}) collective-permute-start(f32[12,3,1024]{2,0,1:T(8,128)S(1)} %broadcast_select_fusion.7), channel_id=1, source_target_pairs={{0,8},{8,16},{16,24},{24,32},{32,40},{40,48},{48,56},{56,64},{64,7... | collective-permute-start | bytes 442376 | tf_op jit(solution)/shard_map/ppermute | solution.py:12
  37.3 16.8 %collective-permute-start.1 = (f32[12,3,1024]{2,0,1:T(8,128)S(1)}, f32[12,3,1024]{2,0,1:T(8,128)S(1)}, u32[]{:S(2)}, u32[]{:S(2)}) collective-permute-start(f32[12,3,1024]{2,0,1:T(8,128)S(1)} %broadcast_select_fusion.8), channel_id=1, source_target_pairs={{0,16},{8,24},{16,32},{24,40},{32,48},{40,56},{48,64},{56,72},{64,... | collective-permute-start | bytes 442376 | tf_op jit(solution)/shard_map/ppermute | solution.py:12
  54.2 8.8 %collective-permute-start.2 = (f32[12,3,1024]{2,0,1:T(8,128)S(1)}, f32[12,3,1024]{2,0,1:T(8,128)S(1)}, u32[]{:S(2)}, u32[]{:S(2)}) collective-permute-start(f32[12,3,1024]{2,0,1:T(8,128)S(1)} %broadcast_select_fusion.9), channel_id=1, source_target_pairs={{0,32},{8,40},{16,48},{24,56},{32,64},{40,72},{48,80},{56,88},{64,... | collective-permute-start | bytes 442376 | tf_op jit(solution)/shard_map/ppermute | solution.py:12
  57.5 40.6 %collective-permute-start.7 = (f32[12,16,1024]{2,1,0:T(8,128)S(1)}, f32[12,16,1024]{2,1,0:T(8,128)S(1)}, u32[]{:S(2)}, u32[]{:S(2)}) collective-permute-start(f32[12,16,1024]{2,1,0:T(8,128)S(1)} %broadcast_select_fusion.1), channel_id=1, source_target_pairs={{0,16},{8,24},{16,32},{24,40},{32,48},{40,56},{48,64},{56,72},{64,... | collective-permute-start | bytes 2359304 | tf_op jit(solution)/shard_map/ppermute | solution.py:12
  63.1 33.0 %collective-permute-start.3 = (f32[12,3,1024]{2,0,1:T(8,128)S(1)}, f32[12,3,1024]{2,0,1:T(8,128)S(1)}, u32[]{:S(2)}, u32[]{:S(2)}) collective-permute-start(f32[12,3,1024]{2,0,1:T(8,128)S(1)} %broadcast_select_fusion.10), channel_id=1, source_target_pairs={{0,64},{8,72},{16,80},{24,88},{32,96},{40,104},{48,112},{56,120},{... | collective-permute-start | bytes 442376 | tf_op jit(solution)/shard_map/ppermute | solution.py:12
  96.1 16.1 %collective-permute-start.4 = (f32[12,3,1024]{2,0,1:T(8,128)S(1)}, f32[12,3,1024]{2,0,1:T(8,128)S(1)}, u32[]{:S(2)}, u32[]{:S(2)}) collective-permute-start(f32[12,3,1024]{2,0,1:T(8,128)S(1)} %broadcast_select_fusion.11), channel_id=1, source_target_pairs={{0,128},{8,136},{16,144},{24,152},{32,160},{40,168},{48,176},{56,1... | collective-permute-start | bytes 442376 | tf_op jit(solution)/shard_map/ppermute | solution.py:12
  98.2 51.2 %collective-permute-start.8 = (f32[12,16,1024]{2,1,0:T(8,128)S(1)}, f32[12,16,1024]{2,1,0:T(8,128)S(1)}, u32[]{:S(2)}, u32[]{:S(2)}) collective-permute-start(f32[12,16,1024]{2,1,0:T(8,128)S(1)} %broadcast_select_fusion.2), channel_id=1, source_target_pairs={{0,32},{8,40},{16,48},{24,56},{32,64},{40,72},{48,80},{56,88},{64,... | collective-permute-start | bytes 2359304 | tf_op jit(solution)/shard_map/ppermute | solution.py:12
  112.3 36.2 %collective-permute-start.5 = (f32[12,3,1024]{2,0,1:T(8,128)S(1)}, f32[12,3,1024]{2,0,1:T(8,128)S(1)}, u32[]{:S(2)}, u32[]{:S(2)}) collective-permute-start(f32[12,3,1024]{2,0,1:T(8,128)S(1)} %broadcast_select_fusion.12), channel_id=1, source_target_pairs={{0,256},{8,264},{16,272},{24,280},{32,288},{40,296},{48,304},{56,3... | collective-permute-start | bytes 442376 | tf_op jit(solution)/shard_map/ppermute | solution.py:12
  149.4 3.2 copy-start.4
  150.4 2.2 copy-start.9
  150.4 2.2 copy-start.14
  150.4 29.5 %collective-permute-start.9 = (f32[12,16,1024]{2,1,0:T(8,128)}, f32[12,16,1024]{2,1,0:T(8,128)S(1)}, u32[]{:S(2)}, u32[]{:S(2)}) collective-permute-start(f32[12,16,1024]{2,1,0:T(8,128)} %broadcast_select_fusion.3), channel_id=1, source_target_pairs={{0,64},{8,72},{16,80},{24,88},{32,96},{40,104},{48,112},{56,120},{... | collective-permute-start | bytes 2359304 | tf_op jit(solution)/shard_map/ppermute | solution.py:12
  154.8 71.4 %copy-start.3 = (f32[16,16,1024]{2,1,0:T(8,128)S(1)}, f32[16,16,1024]{2,1,0:T(8,128)}, u32[]{:S(2)}) copy-start(f32[16,16,1024]{2,1,0:T(8,128)} %param.15) | copy-start | bytes 3145732
  182.1 44.7 %copy-start.12 = (f32[16,1024]{1,0:T(8,128)S(1)}, f32[16,1024]{1,0:T(8,128)}, u32[]{:S(2)}) copy-start(f32[16,1024]{1,0:T(8,128)} %param.23) | copy-start | bytes 196612
  182.1 73.6 %collective-permute-start.10 = (f32[12,16,1024]{2,1,0:T(8,128)}, f32[12,16,1024]{2,1,0:T(8,128)}, u32[]{:S(2)}, u32[]{:S(2)}) collective-permute-start(f32[12,16,1024]{2,1,0:T(8,128)} %broadcast_select_fusion.4), channel_id=1, source_target_pairs={{0,128},{8,136},{16,144},{24,152},{32,160},{40,168},{48,176},{56,1... | collective-permute-start | bytes 2359304 | tf_op jit(solution)/shard_map/ppermute | solution.py:12
  234.9 24.9 %copy-start.10 = (f32[16,544]{1,0:T(8,128)S(1)}, f32[16,544]{1,0:T(8,128)}, u32[]{:S(2)}) copy-start(f32[16,544]{1,0:T(8,128)} %get-tuple-element.13) | copy-start | bytes 104452
  234.9 25.0 %copy-start.2 = (bf16[512,1024]{1,0:T(8,128)(2,1)S(1)}, bf16[512,1024]{1,0:T(8,128)(2,1)}, u32[]{:S(2)}) copy-start(bf16[512,1024]{1,0:T(8,128)(2,1)} %param.21) | copy-start | bytes 3145732
  234.9 25.0 %copy-start.11 = (f32[16,544]{1,0:T(8,128)S(1)}, f32[16,544]{1,0:T(8,128)}, u32[]{:S(2)}) copy-start(f32[16,544]{1,0:T(8,128)} %get-tuple-element.12) | copy-start | bytes 104452
  234.9 25.0 %copy-start.13 = (f32[1024]{0:T(1024)S(1)}, f32[1024]{0:T(1024)}, u32[]{:S(2)}) copy-start(f32[1024]{0:T(1024)} %param.22) | copy-start | bytes 12292
  235.0 25.0 %copy-start.15 = (f32[512]{0:T(512)S(1)}, f32[512]{0:T(512)}, u32[]{:S(2)}) copy-start(f32[512]{0:T(512)} %param.25) | copy-start | bytes 6148
  257.2 80.5 %collective-permute-start.11 = (f32[12,16,1024]{2,1,0:T(8,128)S(1)}, f32[12,16,1024]{2,1,0:T(8,128)S(1)}, u32[]{:S(2)}, u32[]{:S(2)}) collective-permute-start(f32[12,16,1024]{2,1,0:T(8,128)S(1)} %broadcast_select_fusion.5), channel_id=1, source_target_pairs={{0,256},{8,264},{16,272},{24,280},{32,288},{40,296},{48,304},{56,3... | collective-permute-start | bytes 2359304 | tf_op jit(solution)/shard_map/ppermute | solution.py:12
  341.4 1.5 copy-start.7
  341.4 1.5 copy-start.8
  341.4 1.5 copy-start.16
Sparse Core Ops, SparseCore 0:
  154.9 77.3 all-reduce.2
where the time goes:
time: 351 us
  waiting for transfers between devices  225 us (64%)
  starting transfers between devices  83.1 us (24%)
  other arithmetic  15.7 us (4%)
  between operations  14.6 us (4%)
  local copies, waits for them, and re-layouts  9.74 us (3%)
    ppermute x12, waiting for transfers between devices, shifted(): lax.ppermute(array, axis, [(i, (i + by) % size) for i in range(size)])  219 us
    ppermute x12, starting transfers between devices, shifted(): lax.ppermute(array, axis, [(i, (i + by) % size) for i in range(size)])  83 us
  transfers between devices with their start and end apart: 13, of which 10 were waited for; matrix products, arithmetic and copies ran while one was open for 4% of the time, Pallas kernels for 0%

commit v1 on v0

v1 whole, which is shorter than its diff:
```python
import functools

import jax
import jax.numpy as jnp
import numpy as np
from jax import lax
from jax.experimental import pallas as pl
from jax.experimental.pallas import tpu as pltpu
from jax.sharding import PartitionSpec as P

DTR = 512
GROUPS = 12
VMEM = pl.BlockSpec(memory_space=pltpu.VMEM)
SMEM = pl.BlockSpec(memory_space=pltpu.SMEM)

FIRST = 6
CONV = GROUPS // 4
YS = 4


def pack_kernel(me_ref, anchor_ref, target_ref, state_ref, conv_ref, taps_ref, a_ref, b_ref, offset_ref, row_ref, slot_of, rank_of, source):
    slots = state_ref.shape[0]
    peers = slot_of.shape[0]
    me = me_ref[0]
    for o in range(peers):
        slot_of[o] = -1
    for s in range(slots):
        slot_of[(target_ref[s] // slots - me + peers) % peers] = s
    rank = jnp.int32(0)
    for k in range(16):
        offset_ref[k] = 0
    for o in range(1, peers):
        slot = slot_of[o]
        rank_of[o] = rank
        offset_ref[rank] = o
        source[rank] = slot
        rank = rank + (slot >= 0).astype(jnp.int32)
    for s in range(slots):
        offset = (me - anchor_ref[s] // slots + peers) % peers
        row_ref[s] = jnp.where(offset == 0, GROUPS + anchor_ref[s] % slots, rank_of[offset])

    taps = [taps_ref[i : i + 1, :] for i in range(3)]
    for k in range(GROUPS):
        slot = source[k]
        for t in range(16):
            rows, lanes = 8 * (t // 8), 128 * (t % 8)
            block = state_ref[slot, rows : rows + 8, lanes : lanes + 128]
            for h in range(2):
                if k < FIRST:
                    a_ref[t, CONV + 2 * k + h] = block[4 * h : 4 * h + 4]
                else:
                    b_ref[t, 2 * (k - FIRST) + h] = block[4 * h : 4 * h + 4]
        old = [conv_ref[slot, i : i + 1, :] for i in range(3)]
        sums = (old[0] * taps[0] + old[1] * taps[1] + old[2] * taps[2], old[1] * taps[0] + old[2] * taps[1])
        for t in range(16):
            lanes = 128 * (t % 8)
            a_ref[t, k // 4, k % 4 : k % 4 + 1, :] = sums[t // 8][:, lanes : lanes + 128]


def pack(me, anchor, target, ssm_state, conv_state, conv_weight, peers):
    zs = peers // YS
    return pl.pallas_call(
        pack_kernel,
        out_shape=(
            jax.ShapeDtypeStruct((zs, CONV + 2 * FIRST, 4, 128), jnp.float32),
            jax.ShapeDtypeStruct((zs, 2 * (GROUPS - FIRST), 4, 128), jnp.float32),
            jax.ShapeDtypeStruct((16,), jnp.int32),
            jax.ShapeDtypeStruct((16,), jnp.int32),
        ),
        in_specs=[SMEM, SMEM, SMEM, VMEM, VMEM, VMEM],
        out_specs=(VMEM, VMEM, SMEM, SMEM),
        scratch_shapes=[pltpu.SMEM((peers,), jnp.int32), pltpu.SMEM((peers,), jnp.int32), pltpu.SMEM((16,), jnp.int32)],
        compiler_params=pltpu.CompilerParams(vmem_limit_bytes=32 << 20),
        name="pack",
    )(me, anchor, target, ssm_state, conv_state, conv_weight)


def turn_kernel(conv_groups, first, me_ref, offset_ref, held_ref, came_ref, out_ref):
    zs = held_ref.shape[0]
    y = me_ref[0] % YS
    line = lax.broadcasted_iota(jnp.int32, (4, 128), 0)

    def plan(k):
        offset = offset_ref[k]
        return offset // 2 % 2 == 1, (offset + (y - offset + peers) % YS) // YS

    peers = zs * YS

    def pick(rank_plan, z, group):
        came, hops = rank_plan
        sender = (z - hops + zs) % zs
        return jnp.where(came, came_ref[sender, group], held_ref[sender, group])

    for q in range(conv_groups):
        plans = [plan(4 * q + m) for m in range(4)]
        for z in range(zs):
            rows = [pick(p, z, q) for p in plans]
            out_ref[z, q] = jnp.where(
                line < 2, jnp.where(line == 0, rows[0], rows[1]), jnp.where(line == 2, rows[2], rows[3])
            )
    for k in range((held_ref.shape[1] - conv_groups) // 2):
        rank_plan = plan(first + k)
        for z in range(zs):
            for h in range(2):
                group = conv_groups + 2 * k + h
                out_ref[z, group] = pick(rank_plan, z, group)


def turn(conv_groups, first, me, offset, held, came):
    return pl.pallas_call(
        functools.partial(turn_kernel, conv_groups, first),
        out_shape=jax.ShapeDtypeStruct(held.shape, jnp.float32),
        in_specs=[SMEM, SMEM, VMEM, VMEM],
        out_specs=VMEM,
        compiler_params=pltpu.CompilerParams(vmem_limit_bytes=32 << 20),
        name="turn",
    )(me, offset, held, came)


def along_y(conv_groups, first, me, offset, held):
    peers = lax.axis_size("inst")

    def shift(array, by):
        return lax.ppermute(array, "inst", [(i, i // YS * YS + (i + by) % YS) for i in range(peers)])

    ranks = [[4 * q + m for m in range(4)] for q in range(conv_groups)]
    ranks += [[first + g // 2] * 4 for g in range(held.shape[1] - conv_groups)]
    odd = (offset % 2 == 1)[np.array(ranks)]
    held = jnp.where(odd[None, :, :, None], shift(held, 1), held)
    return turn(conv_groups, first, me, offset, held, shift(held, 2))


def along_z(chunks):
    peers = lax.axis_size("inst")
    groups = [list(range(y, peers, YS)) for y in range(YS)]
    return lax.all_to_all(chunks, "inst", 0, 0, axis_index_groups=groups)


def update_kernel(row_ref, first_ref, second_ref, state_ref, step_ref, x_ref, b_ref, c_ref, decay_ref, skip_ref, gate_ref, mixed_ref, out_ref, held, y_ref):
    slots, state_size, width = state_ref.shape
    steps = step_ref.shape[0]
    for s in range(slots):
        r = row_ref[s]

        def gather(get):
            for t in range(16):
                rows, lanes = 8 * (t // 8), 128 * (t % 8)
                held[s, rows : rows + 8, lanes : lanes + 128] = get(t)

        @pl.when(r < FIRST)
        def _():
            group = CONV + 2 * jnp.minimum(r, FIRST - 1)
            gather(lambda t: jnp.concatenate([first_ref[t, group], first_ref[t, group + 1]]))

        @pl.when((r >= FIRST) & (r < GROUPS))
        def _():
            group = 2 * jnp.clip(r - FIRST, 0, GROUPS - FIRST - 1)
            gather(lambda t: jnp.concatenate([second_ref[t, group], second_ref[t, group + 1]]))

        @pl.when(r >= GROUPS)
        def _():
            held[s] = state_ref[jnp.maximum(r - GROUPS, 0)]

    for s in range(slots):
        b = [b_ref[i, :, s : s + 1] for i in range(steps)]
        c = [c_ref[i, :, s : s + 1] for i in range(steps)]
        for lanes in range(0, width, 128):
            cut = slice(lanes, lanes + 128)
            state = held[s, :, cut]
            decay = decay_ref[:, cut]
            for i in range(steps):
                step = step_ref[i, s : s + 1, cut]
                state = jnp.exp(-step * decay) * state + (step * x_ref[i, s : s + 1, cut]) * b[i]
                y_ref[i, s : s + 1, cut] = jnp.sum(c[i] * state, axis=0, keepdims=True)
            out_ref[s, :, cut] = state
    for i in range(steps):
        gate = gate_ref[i]
        mixed_ref[i] = ((y_ref[i] + skip_ref[...] * x_ref[i]) * jax.nn.silu(gate)).astype(mixed_ref.dtype)


def update(row, first, second, state, step, x, b, c, decay, skip, gate):
    steps, slots, width = step.shape
    return pl.pallas_call(
        update_kernel,
        out_shape=(
            jax.ShapeDtypeStruct(step.shape, jnp.bfloat16),
            jax.ShapeDtypeStruct(state.shape, jnp.float32),
        ),
        in_specs=[SMEM] + [VMEM] * 10,
        out_specs=(VMEM, VMEM),
        scratch_shapes=[pltpu.VMEM(state.shape, jnp.float32), pltpu.VMEM(step.shape, jnp.float32)],
        compiler_params=pltpu.CompilerParams(vmem_limit_bytes=32 << 20),
        name="update",
    )(row, first, second, state, step, x, b, c, decay, skip, gate)


def sum_over_tp(part):
    half = part.shape[0] // 2
    size = lax.axis_size("tp")
    first = lax.axis_index("tp") % 2 == 0

    def swap(array, bit):
        return lax.ppermute(array, "tp", [(i, i ^ bit) for i in range(size)])

    mine = jnp.where(first, part[:half], part[half:]) + swap(jnp.where(first, part[half:], part[:half]), 1)
    bit = 2
    while bit < size:
        mine = mine + swap(mine, bit)
        bit *= 2
    other = swap(mine, 1)
    return jnp.concatenate([jnp.where(first, mine, other), jnp.where(first, other, mine)])


def local(
    anchor,
    target,
    ssm_state,
    conv_state,
    x_in,
    gate_in,
    conv_weight,
    x_weight,
    dt_weight,
    dt_bias,
    a_log,
    d_skip,
    dt_gain,
):
    slots, state_size, width = ssm_state.shape
    steps = x_in.shape[1]
    taps = conv_weight.shape[0]
    peers = lax.axis_size("inst")
    me = lax.axis_index("inst").astype(jnp.int32).reshape(1)

    first, second, offset, row = pack(me, anchor, target, ssm_state, conv_state, conv_weight, peers)
    first = along_z(first)
    second, first = lax.optimization_barrier((second, first))
    second = along_z(second)
    second, first = lax.optimization_barrier((second, along_y(CONV, 0, me, offset, first)))
    first = along_z(first)
    second, first = lax.optimization_barrier((along_y(0, FIRST, me, offset, second), first))
    second = along_z(second)

    stayed = jnp.stack(
        [
            jnp.sum(conv_state[:, i:] * conv_weight[None, : taps - 1 - i], axis=1)
            for i in range(steps)
        ],
        axis=1,
    )
    came = first[:, :CONV].reshape(steps, -1, GROUPS, 128).transpose(2, 0, 1, 3).reshape(GROUPS, steps, width)
    partial = jnp.take(jnp.concatenate([came, stayed]), row, axis=0)
    x_values = x_in.astype(jnp.float32)
    conved = []
    for i in range(steps):
        window = partial[:, i] + jnp.sum(x_values[:, : i + 1] * conv_weight[None, taps - 1 - i :], axis=1)
        conved.append(jax.nn.silu(window).astype(jnp.bfloat16))
    conved = jnp.concatenate(conved, axis=0)
    totals = sum_over_tp(jnp.dot(conved, x_weight, preferred_element_type=jnp.float32))
    dt_part = totals[:, :DTR]
    inv_rms = lax.rsqrt(jnp.mean(dt_part * dt_part, axis=-1, keepdims=True) + 1e-06)
    dt_low = (dt_part * inv_rms * dt_gain).astype(jnp.bfloat16)
    step_size = jax.nn.softplus(jnp.dot(dt_low, dt_weight, preferred_element_type=jnp.float32) + dt_bias)
    rest = totals[:, DTR:].reshape(steps, slots, 2 * state_size).transpose(0, 2, 1)
    mixed, state = update(
        row,
        first,
        second,
        ssm_state,
        step_size.reshape(steps, slots, width),
        conved.astype(jnp.float32).reshape(steps, slots, width),
        rest[:, :state_size],
        rest[:, state_size:],
        jnp.exp(a_log),
        d_skip.reshape(1, width),
        gate_in.astype(jnp.float32).transpose(1, 0, 2),
    )
    return mixed.transpose(1, 0, 2), state


def solution(mesh):
    return jax.shard_map(
        local,
        mesh=mesh,
        in_specs=(
            P("inst"),
            P("inst"),
            P("inst", None, "tp"),
            P("inst", None, "tp"),
            P("inst", None, "tp"),
            P("inst", None, "tp"),
            P(None, "tp"),
            P("tp", None),
            P(None, "tp"),
            P("tp"),
            P(None, "tp"),
            P("tp"),
            P(),
        ),
        out_specs=(P("inst", None, "tp"), P("inst", None, "tp")),
        check_vma=False,
    )
```

time: 351 us -> 171 us (0.49)
  the two profiles are of different devices: /device:TPU:16 before, /device:TPU:6 now
where the time goes in v1:
time: 171 us; the launch traced here: 170 us
  waiting for transfers between devices  54.2 us (32%)
  starting transfers between devices  51.1 us (30%)
  blocking collectives  43.1 us (25%)
  Pallas kernels  8.87 us (5%)
  local copies, waits for them, and re-layouts  8.29 us (5%)
  matrix products  2.06 us (1%)
    all_to_all x1, blocking collectives, along_z(): return lax.all_to_all(chunks, 'inst', 0, 0, axis_index_groups=groups)  43.1 us
    ppermute x4, waiting for transfers between devices, shift(): lax.ppermute(array, 'inst', [(i, i // YS * YS + (i + by) % YS) for i in r...  39.3 us
    all_to_all x3, starting transfers between devices, along_z(): return lax.all_to_all(chunks, 'inst', 0, 0, axis_index_groups=groups)  29.1 us
    ppermute x4, starting transfers between devices, shift(): lax.ppermute(array, 'inst', [(i, i // YS * YS + (i + by) % YS) for i in r...  12.1 us
    ppermute x4, starting transfers between devices, swap(): return lax.ppermute(array, 'tp', [(i, i ^ bit) for i in range(size)])  9.87 us
    ppermute x4, waiting for transfers between devices, swap(): return lax.ppermute(array, 'tp', [(i, i ^ bit) for i in range(size)])  8.29 us
    all_to_all x3, waiting for transfers between devices, along_z(): return lax.all_to_all(chunks, 'inst', 0, 0, axis_index_groups=groups)  6.69 us
    unnamed x38, local copies, waits for them, and re-layouts  5.58 us
  transfers between devices with their start and end apart: 11, of which 8 were waited for; matrix products, arithmetic and copies ran while one was open for 3% of the time, Pallas kernels for 3%

profile of v1, /device:TPU:6, one launch (start us, length us, event | category | flops | bytes accessed | tf_op | source)
XLA Modules:
  0.0 170.2 jit_solution(3074886337435748860)
XLA Ops:
  0.7 1.2 copy.24.conv_ref
  1.8 1.2 copy-done.1
  3.0 0.7 copy-done.3
  5.1 1.8 %pack.1 = (f32[16,15,4,128]{3,2,1,0:T(4,128)S(1)}, f32[16,12,4,128]{3,2,1,0:T(4,128)}, s32[16]{0:T(128)S(1)}, s32[16]{0:T(128)S(1)}) custom-call(s32[1]{0:T(128)} %bitcast.me_ref, s32[16]{0:T(128)S(1)} %copy-done.6, s32[16]{0:T(128)S(1)} %copy-done.7, f32[16,16,1024]{2,1,0:T(8,128)S(1)} %copy-done.1, f32[16,3,1024]{2,1,0:T(4,128)S(1)} %copy.24.conv_ref, ...), custom_call_target="tpu_custom_call" | custom-call | tf_op jit(solution)/shard_map/pack/pallas_call | solution.py:62
  6.8 43.1 %all_to_all.20 = f32[16,15,4,128]{3,2,1,0:T(4,128)S(1)} all-to-all(f32[16,15,4,128]{3,2,1,0:T(4,128)S(1)} %get-tuple-element.17), channel_id=1, replica_groups={{0,32,64,96,128,160,192,224,256,288,320,352,384,416,448,480},{8,40,72,1..., dimensions={0} | all-to-all | bytes 983040 | tf_op jit(solution)/shard_map/all_to_all | solution.py:136
  50.0 5.8 %all-to-all-start.1 = ((f32[16,12,4,128]{3,2,1,0:T(4,128)}), f32[16,12,4,128]{3,2,1,0:T(4,128)S(1)}, u32[]{:S(2)}, u32[]{:S(2)}) async-start(f32[16,12,4,128]{3,2,1,0:T(4,128)} %get-tuple-element.18), calls=%async_computation.1 | async-start | bytes 786432 | tf_op jit(solution)/shard_map/all_to_all | solution.py:136
  55.8 3.5 %collective-permute-start = (f32[16,15,4,128]{3,2,1,0:T(4,128)S(1)}, f32[16,15,4,128]{3,2,1,0:T(4,128)S(1)}, u32[]{:S(2)}, u32[]{:S(2)}) collective-permute-start(f32[16,15,4,128]{3,2,1,0:T(4,128)S(1)} %all_to_all.20), channel_id=1, source_target_pairs={{0,8},{8,16},{16,24},{24,0},{32,40},{40,48},{48,56},{56,32},{64,72... | collective-permute-start | bytes 1474568 | tf_op jit(solution)/shard_map/ppermute | solution.py:124
  59.4 0.8 gather_fusion.1
  60.2 11.4 %collective-permute-done = f32[16,15,4,128]{3,2,1,0:T(4,128)S(1)} collective-permute-done((f32[16,15,4,128]{3,2,1,0:T(4,128)S(1)}, f32[16,15,4,128]{3,2,1,0:T(4,128)S(1)}, u32[]{:S(2)}, u32[]{:S(2)}) %collective-permute-start) | collective-permute-done | bytes 491552 | tf_op jit(solution)/shard_map/ppermute | solution.py:124
  71.9 4.0 %collective-permute-start.1 = (f32[16,15,4,128]{3,2,1,0:T(4,128)S(1)}, f32[16,15,4,128]{3,2,1,0:T(4,128)S(1)}, u32[]{:S(2)}, u32[]{:S(2)}) collective-permute-start(f32[16,15,4,128]{3,2,1,0:T(4,128)S(1)} %broadcast_select_fusion.held_ref), channel_id=1, source_target_pairs={{0,16},{8,24},{16,0},{24,8},{32,48},{40,56},{48,32},{56,40},{64,80... | collective-permute-start | bytes 1474568 | tf_op jit(solution)/shard_map/ppermute | solution.py:124
  75.8 11.4 %collective-permute-done.1.came_ref = f32[16,15,4,128]{3,2,1,0:T(4,128)S(1)} collective-permute-done((f32[16,15,4,128]{3,2,1,0:T(4,128)S(1)}, f32[16,15,4,128]{3,2,1,0:T(4,128)S(1)}, u32[]{:S(2)}, u32[]{:S(2)}) %collective-permute-start.1) | collective-permute-done | bytes 491552 | tf_op jit(solution)/shard_map/ppermute | solution.py:124
  87.2 2.6 %turn.2 = f32[16,15,4,128]{3,2,1,0:T(4,128)} custom-call(s32[1]{0:T(128)} %bitcast.me_ref, s32[16]{0:T(128)S(1)} %get-tuple-element.15.offset_ref, f32[16,15,4,128]{3,2,1,0:T(4,128)S(1)} %broadcast_select_fusion.held_ref, f32[16,15,4,128]{3,2,1,0:T(4,128)S(1)} %collective-permute-done.1.came_ref), custom_call_target="tpu_custom_call" | custom-call | tf_op jit(solution)/shard_map/turn/pallas_call | solution.py:110
  89.8 11.6 %all-to-all-start.2 = ((f32[16,15,4,128]{3,2,1,0:T(4,128)}), f32[16,15,4,128]{3,2,1,0:T(4,128)S(1)}, u32[]{:S(2)}, u32[]{:S(2)}) async-start(f32[16,15,4,128]{3,2,1,0:T(4,128)} %turn.2), calls=%async_computation.2 | async-start | bytes 983040 | tf_op jit(solution)/shard_map/all_to_all | solution.py:136
  101.4 2.1 %collective-permute-start.2 = (f32[16,12,4,128]{3,2,1,0:T(4,128)S(1)}, f32[16,12,4,128]{3,2,1,0:T(4,128)S(1)}, u32[]{:S(2)}, u32[]{:S(2)}) collective-permute-start(f32[16,12,4,128]{3,2,1,0:T(4,128)S(1)} %all-to-all-done.1), channel_id=1, source_target_pairs={{0,8},{8,16},{16,24},{24,0},{32,40},{40,48},{48,56},{56,32},{64,72... | collective-permute-start | bytes 1179656 | tf_op jit(solution)/shard_map/ppermute | solution.py:124
  103.9 0.8 gather_fusion
  104.7 8.0 %collective-permute-done.2 = f32[16,12,4,128]{3,2,1,0:T(4,128)S(1)} collective-permute-done((f32[16,12,4,128]{3,2,1,0:T(4,128)S(1)}, f32[16,12,4,128]{3,2,1,0:T(4,128)S(1)}, u32[]{:S(2)}, u32[]{:S(2)}) %collective-permute-start.2) | collective-permute-done | bytes 393248 | tf_op jit(solution)/shard_map/ppermute | solution.py:124
  112.9 2.5 %collective-permute-start.3 = (f32[16,12,4,128]{3,2,1,0:T(4,128)S(1)}, f32[16,12,4,128]{3,2,1,0:T(4,128)S(1)}, u32[]{:S(2)}, u32[]{:S(2)}) collective-permute-start(f32[16,12,4,128]{3,2,1,0:T(4,128)S(1)} %broadcast_select_fusion.1.held_ref), channel_id=1, source_target_pairs={{0,16},{8,24},{16,0},{24,8},{32,48},{40,56},{48,32},{56,40},{64,80... | collective-permute-start | bytes 1179656 | tf_op jit(solution)/shard_map/ppermute | solution.py:124
  115.6 8.5 %collective-permute-done.3.came_ref = f32[16,12,4,128]{3,2,1,0:T(4,128)S(1)} collective-permute-done((f32[16,12,4,128]{3,2,1,0:T(4,128)S(1)}, f32[16,12,4,128]{3,2,1,0:T(4,128)S(1)}, u32[]{:S(2)}, u32[]{:S(2)}) %collective-permute-start.3) | collective-permute-done | bytes 393248 | tf_op jit(solution)/shard_map/ppermute | solution.py:124
  124.1 1.7 %turn.3 = f32[16,12,4,128]{3,2,1,0:T(4,128)} custom-call(s32[1]{0:T(128)} %bitcast.me_ref, s32[16]{0:T(128)S(1)} %get-tuple-element.15.offset_ref, f32[16,12,4,128]{3,2,1,0:T(4,128)S(1)} %broadcast_select_fusion.1.held_ref, f32[16,12,4,128]{3,2,1,0:T(4,128)S(1)} %collective-permute-done.3.came_ref), custom_call_target="tpu_custom_call" | custom-call | tf_op jit(solution)/shard_map/turn/pallas_call | solution.py:110
  126.1 0.7 gather_fusion.2
  127.6 1.9 %collective-permute-start.4 = (f32[16,544]{1,0:T(8,128)S(1)}, f32[16,544]{1,0:T(8,128)S(1)}, u32[]{:S(2)}, u32[]{:S(2)}) collective-permute-start(f32[16,544]{1,0:T(8,128)S(1)} %slice_select_fusion), channel_id=1, source_target_pairs={{0,1},{1,0},{2,3},{3,2},{4,5},{5,4},{6,7},{7,6},{8,9},{9,8},{10,11... | collective-permute-start | bytes 104456 | tf_op jit(solution)/shard_map/ppermute | solution.py:203
  129.5 11.7 %all-to-all-start.3 = ((f32[16,12,4,128]{3,2,1,0:T(4,128)}), f32[16,12,4,128]{3,2,1,0:T(4,128)S(1)}, u32[]{:S(2)}, u32[]{:S(2)}) async-start(f32[16,12,4,128]{3,2,1,0:T(4,128)} %turn.3), calls=%async_computation.3 | async-start | bytes 786432 | tf_op jit(solution)/shard_map/all_to_all | solution.py:136
  141.3 2.7 %collective-permute-start.5 = (f32[16,544]{1,0:T(8,128)S(1)}, f32[16,544]{1,0:T(8,128)S(1)}, u32[]{:S(2)}, u32[]{:S(2)}) collective-permute-start(f32[16,544]{1,0:T(8,128)S(1)} %select_add_fusion), channel_id=1, source_target_pairs={{0,2},{1,3},{2,0},{3,1},{4,6},{5,7},{6,4},{7,5},{8,10},{9,11},{10,... | collective-permute-start | bytes 104456 | tf_op jit(solution)/shard_map/ppermute | solution.py:203
  144.1 3.1 %collective-permute-done.5 = f32[16,544]{1,0:T(8,128)S(1)} collective-permute-done((f32[16,544]{1,0:T(8,128)S(1)}, f32[16,544]{1,0:T(8,128)S(1)}, u32[]{:S(2)}, u32[]{:S(2)}) %collective-permute-start.5) | collective-permute-done | bytes 34848 | tf_op jit(solution)/shard_map/ppermute | solution.py:203
  147.2 3.3 %collective-permute-start.6 = (f32[16,544]{1,0:T(8,128)S(1)}, f32[16,544]{1,0:T(8,128)S(1)}, u32[]{:S(2)}, u32[]{:S(2)}) collective-permute-start(f32[16,544]{1,0:T(8,128)S(1)} %add.89), channel_id=1, source_target_pairs={{0,4},{1,5},{2,6},{3,7},{4,0},{5,1},{6,2},{7,3},{8,12},{9,13},{10,... | collective-permute-start | bytes 104456 | tf_op jit(solution)/shard_map/ppermute | solution.py:203
  150.6 4.0 %collective-permute-done.6 = f32[16,544]{1,0:T(8,128)S(1)} collective-permute-done((f32[16,544]{1,0:T(8,128)S(1)}, f32[16,544]{1,0:T(8,128)S(1)}, u32[]{:S(2)}, u32[]{:S(2)}) %collective-permute-start.6) | collective-permute-done | bytes 34848 | tf_op jit(solution)/shard_map/ppermute | solution.py:203
  154.6 1.9 %collective-permute-start.7 = (f32[16,544]{1,0:T(8,128)S(1)}, f32[16,544]{1,0:T(8,128)S(1)}, u32[]{:S(2)}, u32[]{:S(2)}) collective-permute-start(f32[16,544]{1,0:T(8,128)S(1)} %add.90), channel_id=1, source_target_pairs={{0,1},{1,0},{2,3},{3,2},{4,5},{5,4},{6,7},{7,6},{8,9},{9,8},{10,11... | collective-permute-start | bytes 104456 | tf_op jit(solution)/shard_map/ppermute | solution.py:203
  156.6 1.2 collective-permute-done.7
  158.4 1.6 compare_select_fusion
  160.0 6.7 %all-to-all-done.3.second_ref = f32[16,12,4,128]{3,2,1,0:T(4,128)S(1)} async-done(((f32[16,12,4,128]{3,2,1,0:T(4,128)}), f32[16,12,4,128]{3,2,1,0:T(4,128)S(1)}, u32[]{:S(2)}, u32[]{:S(2)}) %all-to-all-start.3) | async-done | bytes 393248 | tf_op jit(solution)/shard_map/all_to_all | solution.py:136
  166.7 2.8 %update.1 = (bf16[2,16,1024]{2,1,0:T(8,128)(2,1)S(1)}, f32[16,16,1024]{2,1,0:T(8,128)}) custom-call(s32[16]{0:T(128)S(1)} %get-tuple-element.14.row_ref, f32[16,15,4,128]{3,2,1,0:T(4,128)S(1)} %all-to-all-done.2.first_ref, f32[16,12,4,128]{3,2,1,0:T(4,128)S(1)} %all-to-all-done.3.second_ref, f32[16,16,1024]{2,1,0:T(8,128)S(1)} %copy-done.2, ...), custom_call_target="tpu_custom_call" | custom-call | tf_op jit(solution)/shard_map/update/pallas_call | solution.py:183
  169.5 0.7 copy.28
  (77 shorter events, 4.0 us)
Async XLA Ops:
  0.6 126.5 %copy-start = (bf16[1024,544]{0,1:T(8,128)(2,1)S(1)}, bf16[1024,544]{0,1:T(8,128)(2,1)}, u32[]{:S(2)}) copy-start(bf16[1024,544]{0,1:T(8,128)(2,1)} %param.24) | copy-start | bytes 3342340
  1.8 1.2 copy-start.1
  3.0 0.7 copy-start.3
  3.8 0.7 copy-start.6
  4.4 0.7 copy-start.7
  6.8 52.5 %copy-start.17 = (s32[60]{0:T(128)S(1)}, s32[60]{0:T(128)}, u32[]{:S(2)}) copy-start(s32[60]{0:T(128)} %constant.86) | copy-start | bytes 724
  50.0 39.8 %all-to-all-start.1 = ((f32[16,12,4,128]{3,2,1,0:T(4,128)}), f32[16,12,4,128]{3,2,1,0:T(4,128)S(1)}, u32[]{:S(2)}, u32[]{:S(2)}) async-start(f32[16,12,4,128]{3,2,1,0:T(4,128)} %get-tuple-element.18), calls=%async_computation.1 | async-start | bytes 786432 | tf_op jit(solution)/shard_map/all_to_all | solution.py:136
  55.8 15.8 %collective-permute-start = (f32[16,15,4,128]{3,2,1,0:T(4,128)S(1)}, f32[16,15,4,128]{3,2,1,0:T(4,128)S(1)}, u32[]{:S(2)}, u32[]{:S(2)}) collective-permute-start(f32[16,15,4,128]{3,2,1,0:T(4,128)S(1)} %all_to_all.20), channel_id=1, source_target_pairs={{0,8},{8,16},{16,24},{24,0},{32,40},{40,48},{48,56},{56,32},{64,72... | collective-permute-start | bytes 1474568 | tf_op jit(solution)/shard_map/ppermute | solution.py:124
  71.9 31.7 %copy-start.4 = (f32[4,1024]{1,0:T(4,128)S(1)}, f32[4,1024]{1,0:T(4,128)}, u32[]{:S(2)}) copy-start(f32[4,1024]{1,0:T(4,128)} %taps_ref.1) | copy-start | bytes 49156
  71.9 31.7 %copy-start.8 = (f32[16,3,1024]{2,0,1:T(8,128)S(1)}, f32[16,3,1024]{2,0,1:T(8,128)}, u32[]{:S(2)}) copy-start(f32[16,3,1024]{2,0,1:T(8,128)} %param.20) | copy-start | bytes 589828
  71.9 15.4 %collective-permute-start.1 = (f32[16,15,4,128]{3,2,1,0:T(4,128)S(1)}, f32[16,15,4,128]{3,2,1,0:T(4,128)S(1)}, u32[]{:S(2)}, u32[]{:S(2)}) collective-permute-start(f32[16,15,4,128]{3,2,1,0:T(4,128)S(1)} %broadcast_select_fusion.held_ref), channel_id=1, source_target_pairs={{0,16},{8,24},{16,0},{24,8},{32,48},{40,56},{48,32},{56,40},{64,80... | collective-permute-start | bytes 1474568 | tf_op jit(solution)/shard_map/ppermute | solution.py:124
  89.8 14.0 %copy-start.11 = (bf16[16,2,1024]{2,1,0:T(2,128)(2,1)S(1)}, bf16[16,2,1024]{2,1,0:T(2,128)(2,1)}, u32[]{:S(2)}) copy-start(bf16[16,2,1024]{2,1,0:T(2,128)(2,1)} %param.21) | copy-start | bytes 196612
  89.8 14.0 %copy-start.16 = (s32[48]{0:T(128)S(1)}, s32[48]{0:T(128)}, u32[]{:S(2)}) copy-start(s32[48]{0:T(128)} %constant.85) | copy-start | bytes 580
  89.8 36.0 %all-to-all-start.2 = ((f32[16,15,4,128]{3,2,1,0:T(4,128)}), f32[16,15,4,128]{3,2,1,0:T(4,128)S(1)}, u32[]{:S(2)}, u32[]{:S(2)}) async-start(f32[16,15,4,128]{3,2,1,0:T(4,128)} %turn.2), calls=%async_computation.2 | async-start | bytes 983040 | tf_op jit(solution)/shard_map/all_to_all | solution.py:136
  101.4 11.3 %collective-permute-start.2 = (f32[16,12,4,128]{3,2,1,0:T(4,128)S(1)}, f32[16,12,4,128]{3,2,1,0:T(4,128)S(1)}, u32[]{:S(2)}, u32[]{:S(2)}) collective-permute-start(f32[16,12,4,128]{3,2,1,0:T(4,128)S(1)} %all-to-all-done.1), channel_id=1, source_target_pairs={{0,8},{8,16},{16,24},{24,0},{32,40},{40,48},{48,56},{56,32},{64,72... | collective-permute-start | bytes 1179656 | tf_op jit(solution)/shard_map/ppermute | solution.py:124
  112.9 11.2 %collective-permute-start.3 = (f32[16,12,4,128]{3,2,1,0:T(4,128)S(1)}, f32[16,12,4,128]{3,2,1,0:T(4,128)S(1)}, u32[]{:S(2)}, u32[]{:S(2)}) collective-permute-start(f32[16,12,4,128]{3,2,1,0:T(4,128)S(1)} %broadcast_select_fusion.1.held_ref), channel_id=1, source_target_pairs={{0,16},{8,24},{16,0},{24,8},{32,48},{40,56},{48,32},{56,40},{64,80... | collective-permute-start | bytes 1179656 | tf_op jit(solution)/shard_map/ppermute | solution.py:124
  127.1 23.4 %copy-start.12 = (bf16[16,2,1024]{2,1,0:T(2,128)(2,1)S(1)}, bf16[16,2,1024]{2,1,0:T(2,128)(2,1)}, u32[]{:S(2)}) copy-start(bf16[16,2,1024]{2,1,0:T(2,128)(2,1)} %param.22) | copy-start | bytes 196612
  127.1 23.4 %copy-start.13 = (f32[16,1024]{1,0:T(8,128)S(1)}, f32[16,1024]{1,0:T(8,128)}, u32[]{:S(2)}) copy-start(f32[16,1024]{1,0:T(8,128)} %param.27) | copy-start | bytes 196612
  127.6 30.8 %copy-start.14 = (f32[1024]{0:T(1024)S(1)}, f32[1024]{0:T(1024)}, u32[]{:S(2)}) copy-start(f32[1024]{0:T(1024)} %param.26) | copy-start | bytes 12292
  127.6 30.8 %copy-start.15 = (f32[512]{0:T(512)S(1)}, f32[512]{0:T(512)}, u32[]{:S(2)}) copy-start(f32[512]{0:T(512)} %param.29) | copy-start | bytes 6148
  127.6 13.7 %collective-permute-start.4 = (f32[16,544]{1,0:T(8,128)S(1)}, f32[16,544]{1,0:T(8,128)S(1)}, u32[]{:S(2)}, u32[]{:S(2)}) collective-permute-start(f32[16,544]{1,0:T(8,128)S(1)} %slice_select_fusion), channel_id=1, source_target_pairs={{0,1},{1,0},{2,3},{3,2},{4,5},{5,4},{6,7},{7,6},{8,9},{9,8},{10,11... | collective-permute-start | bytes 104456 | tf_op jit(solution)/shard_map/ppermute | solution.py:203
  129.5 37.1 %all-to-all-start.3 = ((f32[16,12,4,128]{3,2,1,0:T(4,128)}), f32[16,12,4,128]{3,2,1,0:T(4,128)S(1)}, u32[]{:S(2)}, u32[]{:S(2)}) async-start(f32[16,12,4,128]{3,2,1,0:T(4,128)} %turn.3), calls=%async_computation.3 | async-start | bytes 786432 | tf_op jit(solution)/shard_map/all_to_all | solution.py:136
  141.3 5.9 %collective-permute-start.5 = (f32[16,544]{1,0:T(8,128)S(1)}, f32[16,544]{1,0:T(8,128)S(1)}, u32[]{:S(2)}, u32[]{:S(2)}) collective-permute-start(f32[16,544]{1,0:T(8,128)S(1)} %select_add_fusion), channel_id=1, source_target_pairs={{0,2},{1,3},{2,0},{3,1},{4,6},{5,7},{6,4},{7,5},{8,10},{9,11},{10,... | collective-permute-start | bytes 104456 | tf_op jit(solution)/shard_map/ppermute | solution.py:203
  147.2 7.4 %collective-permute-start.6 = (f32[16,544]{1,0:T(8,128)S(1)}, f32[16,544]{1,0:T(8,128)S(1)}, u32[]{:S(2)}, u32[]{:S(2)}) collective-permute-start(f32[16,544]{1,0:T(8,128)S(1)} %add.89), channel_id=1, source_target_pairs={{0,4},{1,5},{2,6},{3,7},{4,0},{5,1},{6,2},{7,3},{8,12},{9,13},{10,... | collective-permute-start | bytes 104456 | tf_op jit(solution)/shard_map/ppermute | solution.py:203
  150.6 16.1 %copy-start.2 = (f32[16,16,1024]{2,1,0:T(8,128)S(1)}, f32[16,16,1024]{2,1,0:T(8,128)}, u32[]{:S(2)}) copy-start(f32[16,16,1024]{2,1,0:T(8,128)} %state_ref.3) | copy-start | bytes 3145732
  150.6 16.1 %copy-start.5 = (f32[1024]{0:T(1024)S(1)}, f32[1024]{0:T(1024)}, u32[]{:S(2)}) copy-start(f32[1024]{0:T(1024)} %param.28) | copy-start | bytes 12292
  154.6 3.1 %collective-permute-start.7 = (f32[16,544]{1,0:T(8,128)S(1)}, f32[16,544]{1,0:T(8,128)S(1)}, u32[]{:S(2)}, u32[]{:S(2)}) collective-permute-start(f32[16,544]{1,0:T(8,128)S(1)} %add.90), channel_id=1, source_target_pairs={{0,1},{1,0},{2,3},{3,2},{4,5},{5,4},{6,7},{7,6},{8,9},{9,8},{10,11... | collective-permute-start | bytes 104456 | tf_op jit(solution)/shard_map/ppermute | solution.py:203
  157.7 0.6 copy-start.9
  157.7 0.6 copy-start.10

commit v2 on v1

--- a/solution.py
+++ b/solution.py
@@ -13,14 +13,20 @@
 VMEM = pl.BlockSpec(memory_space=pltpu.VMEM)
 SMEM = pl.BlockSpec(memory_space=pltpu.SMEM)
 
-FIRST = 6
-CONV = GROUPS // 4
-YS = 4
-
-
-def pack_kernel(me_ref, anchor_ref, target_ref, state_ref, conv_ref, taps_ref, a_ref, b_ref, offset_ref, row_ref, slot_of, rank_of, source):
-    slots = state_ref.shape[0]
-    peers = slot_of.shape[0]
+def peer_order(peers):
+    zs = peers // 4
+    bits = zs.bit_length() - 1
+    order = []
+    for place in range(peers):
+        low = place % zs
+        z = sum((low >> i & 1) << (bits - 1 - i) for i in range(bits))
+        order.append(4 * z + (place // zs + place) % 4)
+    return order
+
+
+def pack_kernel(me_ref, anchor_ref, target_ref, state_ref, conv_ref, taps_ref, leaving_ref, offset_ref, row_ref, slot_of, rank_of, source):
+    slots, state_size, width = state_ref.shape
+    peers = leaving_ref.shape[0]
     me = me_ref[0]
     for o in range(peers):
         slot_of[o] = -1
@@ -43,97 +49,65 @@
     for k in range(GROUPS):
         slot = source[k]
         for t in range(16):
+            tile = 16 * k + t
             rows, lanes = 8 * (t // 8), 128 * (t % 8)
             block = state_ref[slot, rows : rows + 8, lanes : lanes + 128]
             for h in range(2):
-                if k < FIRST:
-                    a_ref[t, CONV + 2 * k + h] = block[4 * h : 4 * h + 4]
-                else:
-                    b_ref[t, 2 * (k - FIRST) + h] = block[4 * h : 4 * h + 4]
+                leaving_ref[tile % peers, 2 * (tile // peers) + h] = block[4 * h : 4 * h + 4]
         old = [conv_ref[slot, i : i + 1, :] for i in range(3)]
         sums = (old[0] * taps[0] + old[1] * taps[1] + old[2] * taps[2], old[1] * taps[0] + old[2] * taps[1])
-        for t in range(16):
-            lanes = 128 * (t % 8)
-            a_ref[t, k // 4, k % 4 : k % 4 + 1, :] = sums[t // 8][:, lanes : lanes + 128]
+        for i in range(2):
+            for c in range(8):
+                r = 16 * k + 8 * i + c
+                leaving_ref[r // 3, 6, r % 3 : r % 3 + 1, :] = sums[i][:, 128 * c : 128 * c + 128]
 
 
 def pack(me, anchor, target, ssm_state, conv_state, conv_weight, peers):
-    zs = peers // YS
     return pl.pallas_call(
         pack_kernel,
         out_shape=(
-            jax.ShapeDtypeStruct((zs, CONV + 2 * FIRST, 4, 128), jnp.float32),
-            jax.ShapeDtypeStruct((zs, 2 * (GROUPS - FIRST), 4, 128), jnp.float32),
+            jax.ShapeDtypeStruct((peers, 7, 4, 128), jnp.float32),
             jax.ShapeDtypeStruct((16,), jnp.int32),
             jax.ShapeDtypeStruct((16,), jnp.int32),
         ),
         in_specs=[SMEM, SMEM, SMEM, VMEM, VMEM, VMEM],
-        out_specs=(VMEM, VMEM, SMEM, SMEM),
+        out_specs=(VMEM, SMEM, SMEM),
         scratch_shapes=[pltpu.SMEM((peers,), jnp.int32), pltpu.SMEM((peers,), jnp.int32), pltpu.SMEM((16,), jnp.int32)],
         compiler_params=pltpu.CompilerParams(vmem_limit_bytes=32 << 20),
         name="pack",
     )(me, anchor, target, ssm_state, conv_state, conv_weight)
 
 
-def turn_kernel(conv_groups, first, me_ref, offset_ref, held_ref, came_ref, out_ref):
-    zs = held_ref.shape[0]
-    y = me_ref[0] % YS
+def roll_kernel(order, me_ref, place_ref, offset_ref, held_ref, first_ref, second_ref):
+    peers = held_ref.shape[0]
+    place = place_ref[me_ref[0]]
+    state_shift = [offset_ref[4 * u + place // 16] for u in range(3)]
+    conv_shift = [offset_ref[(3 * place + m) // 16] for m in range(3)]
     line = lax.broadcasted_iota(jnp.int32, (4, 128), 0)
-
-    def plan(k):
-        offset = offset_ref[k]
-        return offset // 2 % 2 == 1, (offset + (y - offset + peers) % YS) // YS
-
-    peers = zs * YS
-
-    def pick(rank_plan, z, group):
-        came, hops = rank_plan
-        sender = (z - hops + zs) % zs
-        return jnp.where(came, came_ref[sender, group], held_ref[sender, group])
-
-    for q in range(conv_groups):
-        plans = [plan(4 * q + m) for m in range(4)]
-        for z in range(zs):
-            rows = [pick(p, z, q) for p in plans]
-            out_ref[z, q] = jnp.where(
-                line < 2, jnp.where(line == 0, rows[0], rows[1]), jnp.where(line == 2, rows[2], rows[3])
-            )
-    for k in range((held_ref.shape[1] - conv_groups) // 2):
-        rank_plan = plan(first + k)
-        for z in range(zs):
-            for h in range(2):
-                group = conv_groups + 2 * k + h
-                out_ref[z, group] = pick(rank_plan, z, group)
-
-
-def turn(conv_groups, first, me, offset, held, came):
+    for d in range(peers):
+        sender = [place_ref[(order[d] - shift + peers) % peers] for shift in state_shift]
+        rows = [held_ref[place_ref[(order[d] - shift + peers) % peers], 6] for shift in conv_shift]
+        first_ref[d, 0] = jnp.where(line == 0, rows[0], jnp.where(line == 1, rows[1], rows[2]))
+        for h in range(2):
+            first_ref[d, 1 + h] = held_ref[sender[0], h]
+            second_ref[d, h] = held_ref[sender[1], 2 + h]
+            second_ref[d, 2 + h] = held_ref[sender[2], 4 + h]
+
+
+def roll(me, offset, held):
+    peers = held.shape[0]
+    order = peer_order(peers)
     return pl.pallas_call(
-        functools.partial(turn_kernel, conv_groups, first),
-        out_shape=jax.ShapeDtypeStruct(held.shape, jnp.float32),
-        in_specs=[SMEM, SMEM, VMEM, VMEM],
-        out_specs=VMEM,
+        functools.partial(roll_kernel, order),
+        out_shape=(
+            jax.ShapeDtypeStruct((peers, 3, 4, 128), jnp.float32),
+            jax.ShapeDtypeStruct((peers, 4, 4, 128), jnp.float32),
+        ),
+        in_specs=[SMEM, SMEM, SMEM, VMEM],
+        out_specs=(VMEM, VMEM),
         compiler_params=pltpu.CompilerParams(vmem_limit_bytes=32 << 20),
-        name="turn",
-    )(me, offset, held, came)
-
-
-def along_y(conv_groups, first, me, offset, held):
-    peers = lax.axis_size("inst")
-
-    def shift(array, by):
-        return lax.ppermute(array, "inst", [(i, i // YS * YS + (i + by) % YS) for i in range(peers)])
-
-    ranks = [[4 * q + m for m in range(4)] for q in range(conv_groups)]
-    ranks += [[first + g // 2] * 4 for g in range(held.shape[1] - conv_groups)]
-    odd = (offset % 2 == 1)[np.array(ranks)]
-    held = jnp.where(odd[None, :, :, None], shift(held, 1), held)
-    return turn(conv_groups, first, me, offset, held, shift(held, 2))
-
-
-def along_z(chunks):
-    peers = lax.axis_size("inst")
-    groups = [list(range(y, peers, YS)) for y in range(YS)]
-    return lax.all_to_all(chunks, "inst", 0, 0, axis_index_groups=groups)
+        name="roll",
+    )(me, jnp.array(np.argsort(order), jnp.int32), offset, held)
 
 
 def update_kernel(row_ref, first_ref, second_ref, state_ref, step_ref, x_ref, b_ref, c_ref, decay_ref, skip_ref, gate_ref, mixed_ref, out_ref, held, y_ref):
@@ -147,15 +121,17 @@
                 rows, lanes = 8 * (t // 8), 128 * (t % 8)
                 held[s, rows : rows + 8, lanes : lanes + 128] = get(t)
 
-        @pl.when(r < FIRST)
+        @pl.when(r < 4)
         def _():
-            group = CONV + 2 * jnp.minimum(r, FIRST - 1)
-            gather(lambda t: jnp.concatenate([first_ref[t, group], first_ref[t, group + 1]]))
-
-        @pl.when((r >= FIRST) & (r < GROUPS))
+            base = jnp.minimum(r, 3) * 16
+            gather(lambda t: jnp.concatenate([first_ref[base + t, 1], first_ref[base + t, 2]]))
+
+        @pl.when((r >= 4) & (r < GROUPS))
         def _():
-            group = 2 * jnp.clip(r - FIRST, 0, GROUPS - FIRST - 1)
-            gather(lambda t: jnp.concatenate([second_ref[t, group], second_ref[t, group + 1]]))
+            place = jnp.clip(r - 4, 0, 7)
+            base = place % 4 * 16
+            half = place // 4 * 2
+            gather(lambda t: jnp.concatenate([second_ref[base + t, half], second_ref[base + t, half + 1]]))
 
         @pl.when(r >= GROUPS)
         def _():
@@ -192,6 +168,10 @@
         compiler_params=pltpu.CompilerParams(vmem_limit_bytes=32 << 20),
         name="update",
     )(row, first, second, state, step, x, b, c, decay, skip, gate)
+
+
+def exchange(chunks):
+    return lax.all_to_all(chunks, "inst", 0, 0, axis_index_groups=[peer_order(chunks.shape[0])])
 
 
 def sum_over_tp(part):
@@ -232,14 +212,11 @@
     peers = lax.axis_size("inst")
     me = lax.axis_index("inst").astype(jnp.int32).reshape(1)
 
-    first, second, offset, row = pack(me, anchor, target, ssm_state, conv_state, conv_weight, peers)
-    first = along_z(first)
+    leaving, offset, row = pack(me, anchor, target, ssm_state, conv_state, conv_weight, peers)
+    first, second = roll(me, offset, exchange(leaving))
+    first = exchange(first)
     second, first = lax.optimization_barrier((second, first))
-    second = along_z(second)
-    second, first = lax.optimization_barrier((second, along_y(CONV, 0, me, offset, first)))
-    first = along_z(first)
-    second, first = lax.optimization_barrier((along_y(0, FIRST, me, offset, second), first))
-    second = along_z(second)
+    second = exchange(second)
 
     stayed = jnp.stack(
         [
@@ -248,7 +225,7 @@
         ],
         axis=1,
     )
-    came = first[:, :CONV].reshape(steps, -1, GROUPS, 128).transpose(2, 0, 1, 3).reshape(GROUPS, steps, width)
+    came = first[:, 0, :3].reshape(GROUPS, steps, width)
     partial = jnp.take(jnp.concatenate([came, stayed]), row, axis=0)
     x_values = x_in.astype(jnp.float32)
     conved = []

time: 171 us -> 155 us (0.906)
  starting transfers between devices: 51.1 us -> 19.6 us
  blocking collectives: 43.1 us -> 68.5 us
  waiting for transfers between devices: 54.2 us -> 45.7 us
    ppermute x4 -> x0, waiting for transfers between devices: 39.3 us -> none  [shift(): lax.ppermute(array, 'inst', [(i, i // YS * YS + (i + by) % YS) for i in r...]
    all_to_all x3 -> x2, waiting for transfers between devices: 6.69 us -> 36.3 us  [exchange(): lax.all_to_all(chunks, 'inst', 0, 0, axis_index_groups=[peer_order(chunks...]
    all_to_all x1, blocking collectives: 43.1 us -> 68.5 us  [exchange(): lax.all_to_all(chunks, 'inst', 0, 0, axis_index_groups=[peer_order(chunks...]
    all_to_all x3 -> x2, starting transfers between devices: 29.1 us -> 9.77 us  [exchange(): lax.all_to_all(chunks, 'inst', 0, 0, axis_index_groups=[peer_order(chunks...]
    ppermute x4 -> x0, starting transfers between devices: 12.1 us -> none  [shift(): lax.ppermute(array, 'inst', [(i, i // YS * YS + (i + by) % YS) for i in r...]
    unnamed x38, local copies, waits for them, and re-layouts: 5.58 us -> 7.52 us
    gather x4 -> x0, local copies, waits for them, and re-layouts: 1.75 us -> none  [along_y(): odd = (offset % 2 == 1)[np.array(ranks)]]
    pallas_call x3 -> x2, Pallas kernels: 6.06 us -> 4.57 us  [the longest x1 2.8 us: roll(): pl.pallas_call(functools.partial(roll_kernel, order), out_shape=(jax.Shap...]
  transfers between devices with their start and end apart: 11 -> 6, of which waited for: 8 -> 6; matrix products, arithmetic and copies ran while one was open for 3% -> 3% of each run, Pallas kernels for 3% -> 0%
where the time goes in v2:
time: 155 us
  blocking collectives  68.5 us (44%)
  waiting for transfers between devices  45.7 us (29%)
  starting transfers between devices  19.6 us (13%)
  local copies, waits for them, and re-layouts  9.13 us (6%)
  Pallas kernels  7.39 us (5%)
  matrix products  2.05 us (1%)
    all_to_all x1, blocking collectives, exchange(): lax.all_to_all(chunks, 'inst', 0, 0, axis_index_groups=[peer_order(chunks...  68.5 us
    all_to_all x2, waiting for transfers between devices, exchange(): lax.all_to_all(chunks, 'inst', 0, 0, axis_index_groups=[peer_order(chunks...  36.3 us
    ppermute x4, starting transfers between devices, swap(): return lax.ppermute(array, 'tp', [(i, i ^ bit) for i in range(size)])  9.87 us
    all_to_all x2, starting transfers between devices, exchange(): lax.all_to_all(chunks, 'inst', 0, 0, axis_index_groups=[peer_order(chunks...  9.77 us
    ppermute x4, waiting for transfers between devices, swap(): return lax.ppermute(array, 'tp', [(i, i ^ bit) for i in range(size)])  9.48 us
    unnamed x38, local copies, waits for them, and re-layouts  7.52 us
  transfers between devices with their start and end apart: 6, of which 6 were waited for; matrix products, arithmetic and copies ran while one was open for 3% of the time, Pallas kernels for 0%

profile of v2, /device:TPU:6, one launch (start us, length us, event | category | flops | bytes accessed | tf_op | source)
XLA Modules:
  0.0 154.5 jit_solution(9891865035494767614)
XLA Ops:
  0.7 1.2 copy.21.conv_ref
  1.8 1.2 copy-done.1
  3.0 0.7 copy-done.3
  3.8 0.7 copy-done.7
  4.4 0.7 copy-done.8
  5.1 1.8 %pack.1 = (f32[64,7,4,128]{3,2,1,0:T(4,128)S(1)}, s32[16]{0:T(128)S(1)}, s32[16]{0:T(128)S(1)}) custom-call(s32[1]{0:T(128)} %bitcast.me_ref, s32[16]{0:T(128)S(1)} %copy-done.7, s32[16]{0:T(128)S(1)} %copy-done.8, f32[16,16,1024]{2,1,0:T(8,128)S(1)} %copy-done.1, f32[16,3,1024]{2,1,0:T(4,128)S(1)} %copy.21.conv_ref, f32[4,1024]{1,0:T(4,128)S(1)} %copy-done.3), custom_call_target="tpu_custom_call" | custom-call | tf_op jit(solution)/shard_map/pack/pallas_call | solution.py:66
  6.9 68.5 %all_to_all.15.held_ref = f32[64,7,4,128]{3,2,1,0:T(4,128)S(1)} all-to-all(f32[64,7,4,128]{3,2,1,0:T(4,128)S(1)} %get-tuple-element.13), channel_id=1, replica_groups={{0,264,144,408,64,328,208,472,32,296,176,440,96,360,240,504,8,272,152,3..., dimensions={0} | all-to-all | bytes 1835008 | tf_op jit(solution)/shard_map/all_to_all | solution.py:174
  75.4 2.8 %roll.1 = (f32[64,3,4,128]{3,2,1,0:T(4,128)}, f32[64,4,4,128]{3,2,1,0:T(4,128)}) custom-call(s32[1]{0:T(128)} %bitcast.me_ref, s32[64]{0:T(128)S(1)} %copy-done.9, s32[16]{0:T(128)S(1)} %get-tuple-element.12.offset_ref, f32[64,7,4,128]{3,2,1,0:T(4,128)S(1)} %all_to_all.15.held_ref), custom_call_target="tpu_custom_call" | custom-call | tf_op jit(solution)/shard_map/roll/pallas_call | solution.py:100
  78.2 5.1 %all-to-all-start.1 = ((f32[64,3,4,128]{3,2,1,0:T(4,128)}), f32[64,3,4,128]{3,2,1,0:T(4,128)S(1)}, u32[]{:S(2)}, u32[]{:S(2)}) async-start(f32[64,3,4,128]{3,2,1,0:T(4,128)} %get-tuple-element.15), calls=%async_computation.1 | async-start | bytes 786432 | tf_op jit(solution)/shard_map/all_to_all | solution.py:174
  83.7 0.2 multiply_reduce_fusion.1
  83.9 27.9 %all-to-all-done.1.first_ref = f32[64,3,4,128]{3,2,1,0:T(4,128)S(1)} async-done(((f32[64,3,4,128]{3,2,1,0:T(4,128)}), f32[64,3,4,128]{3,2,1,0:T(4,128)S(1)}, u32[]{:S(2)}, u32[]{:S(2)}) %all-to-all-start.1) | async-done | bytes 393248 | tf_op jit(solution)/shard_map/all_to_all | solution.py:174
  111.8 4.6 %all-to-all-start.2 = ((f32[64,4,4,128]{3,2,1,0:T(4,128)}), f32[64,4,4,128]{3,2,1,0:T(4,128)S(1)}, u32[]{:S(2)}, u32[]{:S(2)}) async-start(f32[64,4,4,128]{3,2,1,0:T(4,128)} %get-tuple-element.17), calls=%async_computation.2 | async-start | bytes 1048576 | tf_op jit(solution)/shard_map/all_to_all | solution.py:174
  116.5 0.2 maximum_maximum_fusion
  116.7 0.7 gather_fusion
  117.8 0.4 fusion.10
  118.2 1.9 %collective-permute-start = (f32[16,544]{1,0:T(8,128)S(1)}, f32[16,544]{1,0:T(8,128)S(1)}, u32[]{:S(2)}, u32[]{:S(2)}) collective-permute-start(f32[16,544]{1,0:T(8,128)S(1)} %slice_select_fusion), channel_id=1, source_target_pairs={{0,1},{1,0},{2,3},{3,2},{4,5},{5,4},{6,7},{7,6},{8,9},{9,8},{10,11... | collective-permute-start | bytes 104456 | tf_op jit(solution)/shard_map/ppermute | solution.py:183
  120.1 1.2 collective-permute-done
  121.3 2.7 %collective-permute-start.1 = (f32[16,544]{1,0:T(8,128)S(1)}, f32[16,544]{1,0:T(8,128)S(1)}, u32[]{:S(2)}, u32[]{:S(2)}) collective-permute-start(f32[16,544]{1,0:T(8,128)S(1)} %select_add_fusion), channel_id=1, source_target_pairs={{0,2},{1,3},{2,0},{3,1},{4,6},{5,7},{6,4},{7,5},{8,10},{9,11},{10,... | collective-permute-start | bytes 104456 | tf_op jit(solution)/shard_map/ppermute | solution.py:183
  124.1 3.2 %collective-permute-done.1 = f32[16,544]{1,0:T(8,128)S(1)} collective-permute-done((f32[16,544]{1,0:T(8,128)S(1)}, f32[16,544]{1,0:T(8,128)S(1)}, u32[]{:S(2)}, u32[]{:S(2)}) %collective-permute-start.1) | collective-permute-done | bytes 34848 | tf_op jit(solution)/shard_map/ppermute | solution.py:183
  127.2 3.3 %collective-permute-start.2 = (f32[16,544]{1,0:T(8,128)S(1)}, f32[16,544]{1,0:T(8,128)S(1)}, u32[]{:S(2)}, u32[]{:S(2)}) collective-permute-start(f32[16,544]{1,0:T(8,128)S(1)} %add.64), channel_id=1, source_target_pairs={{0,4},{1,5},{2,6},{3,7},{4,0},{5,1},{6,2},{7,3},{8,12},{9,13},{10,... | collective-permute-start | bytes 104456 | tf_op jit(solution)/shard_map/ppermute | solution.py:183
  130.6 4.0 %collective-permute-done.2 = f32[16,544]{1,0:T(8,128)S(1)} collective-permute-done((f32[16,544]{1,0:T(8,128)S(1)}, f32[16,544]{1,0:T(8,128)S(1)}, u32[]{:S(2)}, u32[]{:S(2)}) %collective-permute-start.2) | collective-permute-done | bytes 34848 | tf_op jit(solution)/shard_map/ppermute | solution.py:183
  134.6 1.9 %collective-permute-start.3 = (f32[16,544]{1,0:T(8,128)S(1)}, f32[16,544]{1,0:T(8,128)S(1)}, u32[]{:S(2)}, u32[]{:S(2)}) collective-permute-start(f32[16,544]{1,0:T(8,128)S(1)} %add.65), channel_id=1, source_target_pairs={{0,1},{1,0},{2,3},{3,2},{4,5},{5,4},{6,7},{7,6},{8,9},{9,8},{10,11... | collective-permute-start | bytes 104456 | tf_op jit(solution)/shard_map/ppermute | solution.py:183
  136.6 1.2 collective-permute-done.3
  138.0 0.4 copy-done.13
  138.4 0.6 fusion.11
  139.0 1.6 %compare_select_fusion = f32[32,1024]{1,0:T(8,128)S(1)} fusion(bf16[512,1024]{1,0:T(8,128)(2,1)} %param.22, f32[1024]{0:T(1024)} %param.23, f32[512]{0:T(512)} %param.26, f32[32]{0:T(128)S(1)} %add_rsqrt_fusion, f32[16,544]{1,0:T(8,128)} %copy-done.13, f32[16,544]{1,0:T(8,128)} %copy-done.14), kind=kOutput, calls=%fused_computation.2 | convolution fusion | flops 33849344 | bytes 1255552 | tf_op jit(solution)/shard_map/dot_general | solution.py:240
  140.6 8.4 %all-to-all-done.2.second_ref = f32[64,4,4,128]{3,2,1,0:T(4,128)S(1)} async-done(((f32[64,4,4,128]{3,2,1,0:T(4,128)}), f32[64,4,4,128]{3,2,1,0:T(4,128)S(1)}, u32[]{:S(2)}, u32[]{:S(2)}) %all-to-all-start.2) | async-done | bytes 524320 | tf_op jit(solution)/shard_map/all_to_all | solution.py:174
  149.0 0.7 copy-done.5
  149.7 0.7 copy-done.6
  150.4 0.6 copy-done.11
  151.0 2.8 %update.1 = (bf16[2,16,1024]{2,1,0:T(8,128)(2,1)S(1)}, f32[16,16,1024]{2,1,0:T(8,128)}) custom-call(s32[16]{0:T(128)S(1)} %copy-done.11, f32[64,3,4,128]{3,2,1,0:T(4,128)S(1)} %all-to-all-done.1.first_ref, f32[64,4,4,128]{3,2,1,0:T(4,128)S(1)} %all-to-all-done.2.second_ref, f32[16,16,1024]{2,1,0:T(8,128)S(1)} %copy-done.2, f32[2,16,1024]{2,1,0:T(8,128)S(1)} %bitcast.31, ...), custom_call_target="tpu_custom_call" | custom-call | tf_op jit(solution)/shard_map/update/pallas_call | solution.py:159
  153.8 0.7 copy.24
  (56 shorter events, 1.0 us)
Async XLA Ops:
  0.6 117.1 %copy-start = (bf16[1024,544]{0,1:T(8,128)(2,1)S(1)}, bf16[1024,544]{0,1:T(8,128)(2,1)}, u32[]{:S(2)}) copy-start(bf16[1024,544]{0,1:T(8,128)(2,1)} %param.21) | copy-start | bytes 3342340
  1.8 1.2 copy-start.1
  3.0 0.7 copy-start.3
  3.8 0.7 copy-start.7
  4.4 0.7 copy-start.8
  6.8 77.0 %copy-start.10 = (s32[16]{0:T(128)}, s32[16]{0:T(128)S(1)}, u32[]{:S(2)}) copy-start(s32[16]{0:T(128)S(1)} %get-tuple-element.11.row_ref) | copy-start | bytes 196
  6.8 68.6 %copy-start.9 = (s32[64]{0:T(128)S(1)}, s32[64]{0:T(128)}, u32[]{:S(2)}) copy-start(s32[64]{0:T(128)} %constant.53.clone.place_ref) | copy-start | bytes 772
  75.4 8.0 %copy-start.4 = (f32[4,1024]{1,0:T(4,128)S(1)}, f32[4,1024]{1,0:T(4,128)}, u32[]{:S(2)}) copy-start(f32[4,1024]{1,0:T(4,128)} %taps_ref.1) | copy-start | bytes 49156
  75.4 8.0 %copy-start.12 = (f32[16,3,1024]{2,0,1:T(8,128)S(1)}, f32[16,3,1024]{2,0,1:T(8,128)}, u32[]{:S(2)}) copy-start(f32[16,3,1024]{2,0,1:T(8,128)} %param.17) | copy-start | bytes 589828
  75.4 8.2 %copy-start.15 = (bf16[16,2,1024]{2,1,0:T(2,128)(2,1)S(1)}, bf16[16,2,1024]{2,1,0:T(2,128)(2,1)}, u32[]{:S(2)}) copy-start(bf16[16,2,1024]{2,1,0:T(2,128)(2,1)} %param.18) | copy-start | bytes 196612
  78.2 33.5 %all-to-all-start.1 = ((f32[64,3,4,128]{3,2,1,0:T(4,128)}), f32[64,3,4,128]{3,2,1,0:T(4,128)S(1)}, u32[]{:S(2)}, u32[]{:S(2)}) async-start(f32[64,3,4,128]{3,2,1,0:T(4,128)} %get-tuple-element.15), calls=%async_computation.1 | async-start | bytes 786432 | tf_op jit(solution)/shard_map/all_to_all | solution.py:174
  111.8 37.2 %all-to-all-start.2 = ((f32[64,4,4,128]{3,2,1,0:T(4,128)}), f32[64,4,4,128]{3,2,1,0:T(4,128)S(1)}, u32[]{:S(2)}, u32[]{:S(2)}) async-start(f32[64,4,4,128]{3,2,1,0:T(4,128)} %get-tuple-element.17), calls=%async_computation.2 | async-start | bytes 1048576 | tf_op jit(solution)/shard_map/all_to_all | solution.py:174
  117.5 13.0 %copy-start.16 = (bf16[16,2,1024]{2,1,0:T(2,128)(2,1)S(1)}, bf16[16,2,1024]{2,1,0:T(2,128)(2,1)}, u32[]{:S(2)}) copy-start(bf16[16,2,1024]{2,1,0:T(2,128)(2,1)} %param.19) | copy-start | bytes 196612
  117.7 12.9 %copy-start.17 = (f32[16,1024]{1,0:T(8,128)S(1)}, f32[16,1024]{1,0:T(8,128)}, u32[]{:S(2)}) copy-start(f32[16,1024]{1,0:T(8,128)} %param.24) | copy-start | bytes 196612
  118.2 3.1 %collective-permute-start = (f32[16,544]{1,0:T(8,128)S(1)}, f32[16,544]{1,0:T(8,128)S(1)}, u32[]{:S(2)}, u32[]{:S(2)}) collective-permute-start(f32[16,544]{1,0:T(8,128)S(1)} %slice_select_fusion), channel_id=1, source_target_pairs={{0,1},{1,0},{2,3},{3,2},{4,5},{5,4},{6,7},{7,6},{8,9},{9,8},{10,11... | collective-permute-start | bytes 104456 | tf_op jit(solution)/shard_map/ppermute | solution.py:183
  121.3 5.9 %collective-permute-start.1 = (f32[16,544]{1,0:T(8,128)S(1)}, f32[16,544]{1,0:T(8,128)S(1)}, u32[]{:S(2)}, u32[]{:S(2)}) collective-permute-start(f32[16,544]{1,0:T(8,128)S(1)} %select_add_fusion), channel_id=1, source_target_pairs={{0,2},{1,3},{2,0},{3,1},{4,6},{5,7},{6,4},{7,5},{8,10},{9,11},{10,... | collective-permute-start | bytes 104456 | tf_op jit(solution)/shard_map/ppermute | solution.py:183
  127.2 7.4 %collective-permute-start.2 = (f32[16,544]{1,0:T(8,128)S(1)}, f32[16,544]{1,0:T(8,128)S(1)}, u32[]{:S(2)}, u32[]{:S(2)}) collective-permute-start(f32[16,544]{1,0:T(8,128)S(1)} %add.64), channel_id=1, source_target_pairs={{0,4},{1,5},{2,6},{3,7},{4,0},{5,1},{6,2},{7,3},{8,12},{9,13},{10,... | collective-permute-start | bytes 104456 | tf_op jit(solution)/shard_map/ppermute | solution.py:183
  130.6 18.4 %copy-start.2 = (f32[16,16,1024]{2,1,0:T(8,128)S(1)}, f32[16,16,1024]{2,1,0:T(8,128)}, u32[]{:S(2)}) copy-start(f32[16,16,1024]{2,1,0:T(8,128)} %state_ref.3) | copy-start | bytes 3145732
  134.6 3.1 %collective-permute-start.3 = (f32[16,544]{1,0:T(8,128)S(1)}, f32[16,544]{1,0:T(8,128)S(1)}, u32[]{:S(2)}, u32[]{:S(2)}) collective-permute-start(f32[16,544]{1,0:T(8,128)S(1)} %add.65), channel_id=1, source_target_pairs={{0,1},{1,0},{2,3},{3,2},{4,5},{5,4},{6,7},{7,6},{8,9},{9,8},{10,11... | collective-permute-start | bytes 104456 | tf_op jit(solution)/shard_map/ppermute | solution.py:183
  137.8 0.6 copy-start.13
  137.8 0.6 copy-start.14
  149.0 0.7 copy-start.5
  149.7 0.7 copy-start.6
  150.4 0.6 copy-start.11

commit v3 on v2

v3 whole, which is shorter than its diff:
```python
import jax
import jax.numpy as jnp
from jax import lax
from jax.experimental import pallas as pl
from jax.experimental.pallas import tpu as pltpu
from jax.sharding import PartitionSpec as P

DTR = 512
GROUPS = 12
VMEM = pl.BlockSpec(memory_space=pltpu.VMEM)
SMEM = pl.BlockSpec(memory_space=pltpu.SMEM)

ANY = pl.BlockSpec(memory_space=pl.ANY)

TILES = 3
CONV = 4


def fetch(pairs, sems):
    copies = [pltpu.make_async_copy(src, dst, sems.at[i]) for i, (src, dst) in enumerate(pairs)]
    for copy in copies:
        copy.start()
    for copy in copies:
        copy.wait()


def pack_kernel(
    me_ref, anchor_hbm, target_hbm, state_hbm, conv_hbm, taps_hbm,
    leaving_ref, offset_ref, row_ref, sums_ref,
    anchor_ref, target_ref, state_ref, conv_ref, taps_ref, slot_of, rank_of, source, sems,
):
    fetch(
        [
            (anchor_hbm, anchor_ref),
            (target_hbm, target_ref),
            (conv_hbm, conv_ref),
            (taps_hbm, taps_ref),
            (state_hbm, state_ref),
        ],
        sems,
    )
    slots = state_ref.shape[0]
    peers = leaving_ref.shape[0]
    me = me_ref[0]
    for o in range(peers):
        slot_of[o] = -1
    for s in range(slots):
        slot_of[(target_ref[s] // slots - me + peers) % peers] = s
    rank = jnp.int32(0)
    for k in range(16):
        offset_ref[k] = 0
    for o in range(1, peers):
        slot = slot_of[o]
        rank_of[o] = rank
        offset_ref[rank] = o
        source[rank] = slot
        rank = rank + (slot >= 0).astype(jnp.int32)
    for s in range(slots):
        offset = (me - anchor_ref[s] // slots + peers) % peers
        row_ref[s] = jnp.where(offset == 0, GROUPS + anchor_ref[s] % slots, rank_of[offset])

    old = [conv_ref[i] for i in range(3)]
    taps = [taps_ref[i : i + 1, :] for i in range(3)]
    sums_ref[0] = old[0] * taps[0] + old[1] * taps[1] + old[2] * taps[2]
    sums_ref[1] = old[1] * taps[0] + old[2] * taps[1]
    for d in range(peers):
        for q in range(CONV):
            leaving_ref[d, 2 * TILES + q] = jnp.zeros((4, 128), jnp.float32)
    for k in range(GROUPS):
        slot = source[k]
        for t in range(16):
            tile = 16 * k + t
            rows, lanes = 8 * (t // 8), 128 * (t % 8)
            block = state_ref[slot, rows : rows + 8, lanes : lanes + 128]
            for h in range(2):
                leaving_ref[tile % peers, 2 * (tile // peers) + h] = block[4 * h : 4 * h + 4]
        receiver = (me + offset_ref[k]) % peers
        for i in range(2):
            sums = sums_ref[i, pl.ds(slot, 1), :]
            for c in range(8):
                r = 8 * i + c
                leaving_ref[receiver, 2 * TILES + r // 4, r % 4 : r % 4 + 1, :] = sums[:, 128 * c : 128 * c + 128]


def pack(me, anchor, target, ssm_state, conv_state, conv_weight, peers):
    slots, _, width = ssm_state.shape
    return pl.pallas_call(
        pack_kernel,
        out_shape=(
            jax.ShapeDtypeStruct((peers, 2 * TILES + CONV, 4, 128), jnp.float32),
            jax.ShapeDtypeStruct((16,), jnp.int32),
            jax.ShapeDtypeStruct((16,), jnp.int32),
            jax.ShapeDtypeStruct((2, slots, width), jnp.float32),
        ),
        in_specs=[SMEM] + [ANY] * 5,
        out_specs=(VMEM, SMEM, SMEM, VMEM),
        scratch_shapes=[
            pltpu.SMEM(anchor.shape, jnp.int32),
            pltpu.SMEM(target.shape, jnp.int32),
            pltpu.VMEM(ssm_state.shape, jnp.float32),
            pltpu.VMEM(conv_state.shape, jnp.float32),
            pltpu.VMEM(conv_weight.shape, jnp.float32),
            pltpu.SMEM((peers,), jnp.int32),
            pltpu.SMEM((peers,), jnp.int32),
            pltpu.SMEM((16,), jnp.int32),
            pltpu.SemaphoreType.DMA((5,)),
        ],
        compiler_params=pltpu.CompilerParams(vmem_limit_bytes=56 << 20),
        name="pack",
    )(me, anchor, target, ssm_state, conv_state, conv_weight)


def roll_kernel(me_ref, offset_ref, held_ref, due_ref):
    peers = held_ref.shape[0]
    shifts = [offset_ref[4 * u + me_ref[0] // 16] for u in range(TILES)]

    def body(d, carry):
        for u, shift in enumerate(shifts):
            sender = (d - shift + peers) % peers
            for h in range(2):
                due_ref[d, 2 * u + h] = held_ref[sender, 2 * u + h]
        return carry

    lax.fori_loop(0, peers, body, 0, unroll=8)


def roll(me, offset, held):
    peers = held.shape[0]
    return pl.pallas_call(
        roll_kernel,
        out_shape=jax.ShapeDtypeStruct((peers, 2 * TILES, 4, 128), jnp.float32),
        in_specs=[SMEM, SMEM, VMEM],
        out_specs=VMEM,
        compiler_params=pltpu.CompilerParams(vmem_limit_bytes=32 << 20),
        name="roll",
    )(me, offset, held)


def update_kernel(
    row_hbm, rest_hbm, moved_ref, state_ref, step_ref, x_ref, skip_ref, decay_ref, gate_ref,
    mixed_ref, out_ref,
    row_ref, rest_ref, held, y_ref, sems,
):
    fetch([(row_hbm, row_ref), (rest_hbm, rest_ref)], sems)
    slots, state_size, width = state_ref.shape
    steps = step_ref.shape[0]
    for s in range(slots):
        r = row_ref[s]

        @pl.when(r < GROUPS)
        def _():
            rank = jnp.minimum(r, GROUPS - 1)
            base, group = rank % 4 * 16, rank // 4 * 2
            for t in range(16):
                rows, lanes = 8 * (t // 8), 128 * (t % 8)
                held[s, rows : rows + 8, lanes : lanes + 128] = jnp.concatenate(
                    [moved_ref[base + t, group], moved_ref[base + t, group + 1]]
                )

        @pl.when(r >= GROUPS)
        def _():
            held[s] = state_ref[jnp.maximum(r - GROUPS, 0)]

    for s in range(slots):
        b = [rest_ref[i, :state_size, s : s + 1] for i in range(steps)]
        c = [rest_ref[i, state_size:, s : s + 1] for i in range(steps)]
        for lanes in range(0, width, 128):
            cut = slice(lanes, lanes + 128)
            state = held[s, :, cut]
            decay = decay_ref[:, cut]
            for i in range(steps):
                step = step_ref[i, s : s + 1, cut]
                state = jnp.exp(-step * decay) * state + (step * x_ref[i, s : s + 1, cut]) * b[i]
                y_ref[s, i : i + 1, cut] = jnp.sum(c[i] * state, axis=0, keepdims=True)
            out_ref[s, :, cut] = state
        gate = gate_ref[s].astype(jnp.float32)
        mixed_ref[s] = ((y_ref[s] + skip_ref[s]) * jax.nn.silu(gate)).astype(mixed_ref.dtype)


def update(row, rest, moved, state, step, x, skip, decay, gate):
    return pl.pallas_call(
        update_kernel,
        out_shape=(
            jax.ShapeDtypeStruct(gate.shape, jnp.bfloat16),
            jax.ShapeDtypeStruct(state.shape, jnp.float32),
        ),
        in_specs=[ANY, ANY] + [VMEM] * 7,
        out_specs=(VMEM, VMEM),
        scratch_shapes=[
            pltpu.SMEM(row.shape, jnp.int32),
            pltpu.VMEM(rest.shape, jnp.float32),
            pltpu.VMEM(state.shape, jnp.float32),
            pltpu.VMEM(gate.shape, jnp.float32),
            pltpu.SemaphoreType.DMA((2,)),
        ],
        compiler_params=pltpu.CompilerParams(vmem_limit_bytes=32 << 20),
        name="update",
    )(row, rest, moved, state, step, x, skip, decay, gate)


def exchange(chunks):
    return lax.all_to_all(chunks, "inst", 0, 0)


def sum_over_tp(part):
    half = part.shape[0] // 2
    size = lax.axis_size("tp")
    first = lax.axis_index("tp") % 2 == 0

    def swap(array, bit):
        return lax.ppermute(array, "tp", [(i, i ^ bit) for i in range(size)])

    mine = jnp.where(first, part[:half], part[half:]) + swap(jnp.where(first, part[half:], part[:half]), 1)
    bit = 2
    while bit < size:
        mine = mine + swap(mine, bit)
        bit *= 2
    other = swap(mine, 1)
    return jnp.concatenate([jnp.where(first, mine, other), jnp.where(first, other, mine)])


def local(
    anchor,
    target,
    ssm_state,
    conv_state,
    x_in,
    gate_in,
    conv_weight,
    x_weight,
    dt_weight,
    dt_bias,
    a_log,
    d_skip,
    dt_gain,
):
    slots, state_size, width = ssm_state.shape
    steps = x_in.shape[1]
    taps = conv_weight.shape[0]
    peers = lax.axis_size("inst")
    me = lax.axis_index("inst").astype(jnp.int32).reshape(1)

    leaving, offset, row, sums = pack(me, anchor, target, ssm_state, conv_state.transpose(1, 0, 2), conv_weight, peers)
    spread = exchange(leaving)
    moved = exchange(roll(me, offset, spread))

    came = spread[:, 2 * TILES :].reshape(peers, steps, width)
    partial = jnp.where(
        (anchor // slots == me)[:, None, None],
        jnp.take(sums.transpose(1, 0, 2), anchor % slots, axis=0),
        jnp.take(came, anchor // slots, axis=0),
    )
    x_values = x_in.astype(jnp.float32)
    conved = []
    for i in range(steps):
        window = partial[:, i] + jnp.sum(x_values[:, : i + 1] * conv_weight[None, taps - 1 - i :], axis=1)
        conved.append(jax.nn.silu(window).astype(jnp.bfloat16))
    conved = jnp.concatenate(conved, axis=0)
    totals = sum_over_tp(jnp.dot(conved, x_weight, preferred_element_type=jnp.float32))
    dt_part = totals[:, :DTR]
    inv_rms = lax.rsqrt(jnp.mean(dt_part * dt_part, axis=-1, keepdims=True) + 1e-06)
    dt_low = (dt_part * inv_rms * dt_gain).astype(jnp.bfloat16)
    step_size = jax.nn.softplus(jnp.dot(dt_low, dt_weight, preferred_element_type=jnp.float32) + dt_bias)
    rest = totals[:, DTR:].reshape(steps, slots, 2 * state_size).transpose(0, 2, 1)
    x_rows = conved.astype(jnp.float32).reshape(steps, slots, width)
    return update(
        row,
        rest,
        moved,
        ssm_state,
        step_size.reshape(steps, slots, width),
        x_rows,
        (d_skip * x_rows).transpose(1, 0, 2),
        jnp.exp(a_log),
        gate_in,
    )


def solution(mesh):
    return jax.shard_map(
        local,
        mesh=mesh,
        in_specs=(
            P("inst"),
            P("inst"),
            P("inst", None, "tp"),
            P("inst", None, "tp"),
            P("inst", None, "tp"),
            P("inst", None, "tp"),
            P(None, "tp"),
            P("tp", None),
            P(None, "tp"),
            P("tp"),
            P(None, "tp"),
            P("tp"),
            P(),
        ),
        out_specs=(P("inst", None, "tp"), P("inst", None, "tp")),
        check_vma=False,
    )
```

time: 155 us -> 144 us (0.929)
  blocking collectives: 68.5 us -> 0 us
  waiting for transfers between devices: 45.7 us -> 89.6 us
  starting transfers between devices: 19.6 us -> 34.7 us
  local copies, waits for them, and re-layouts: 9.13 us -> 5.84 us
  other arithmetic: 0.94 us -> 2.94 us
    all_to_all x1 -> x0, blocking collectives: 68.5 us -> none  [exchange(): lax.all_to_all(chunks, 'inst', 0, 0, axis_index_groups=[peer_order(chunks...]
    all_to_all x2, waiting for transfers between devices: 36.3 us -> 80.2 us  [exchange(): return lax.all_to_all(chunks, 'inst', 0, 0)]
    all_to_all x2, starting transfers between devices: 9.77 us -> 24.8 us  [exchange(): return lax.all_to_all(chunks, 'inst', 0, 0)]
    unnamed x38 -> x36, local copies, waits for them, and re-layouts: 7.52 us -> 1.85 us
    and x1 -> x2, other arithmetic: 0.01 us -> 1.73 us  [the longest x1 1.15 us: local(): jnp.take(came, anchor // slots, axis=0)]
  transfers between devices with their start and end apart: 6 -> 6, of which waited for: 6 -> 6; matrix products, arithmetic and copies ran while one was open for 3% -> 6% of each run, Pallas kernels for 0% -> 0%
where the time goes in v3:
time: 144 us
  waiting for transfers between devices  89.6 us (62%)
  starting transfers between devices  34.7 us (24%)
  Pallas kernels  7.46 us (5%)
  local copies, waits for them, and re-layouts  5.84 us (4%)
  other arithmetic  2.94 us (2%)
  matrix products  2.06 us (1%)
    all_to_all x2, waiting for transfers between devices, exchange(): return lax.all_to_all(chunks, 'inst', 0, 0)  80.2 us
    all_to_all x2, starting transfers between devices, exchange(): return lax.all_to_all(chunks, 'inst', 0, 0)  24.8 us
    ppermute x4, starting transfers between devices, swap(): return lax.ppermute(array, 'tp', [(i, i ^ bit) for i in range(size)])  9.87 us
    ppermute x4, waiting for transfers between devices, swap(): return lax.ppermute(array, 'tp', [(i, i ^ bit) for i in range(size)])  9.37 us
    pallas_call x1, Pallas kernels, pack(): pl.pallas_call(pack_kernel, out_shape=(jax.ShapeDtypeStruct((peers, 2 * T...  3.27 us
    pallas_call x1, Pallas kernels, update(): pl.pallas_call(update_kernel, out_shape=(jax.ShapeDtypeStruct(gate.shape,...  2.92 us
  transfers between devices with their start and end apart: 6, of which 6 were waited for; matrix products, arithmetic and copies ran while one was open for 6% of the time, Pallas kernels for 0%

profile of v3, /device:TPU:6, one launch (start us, length us, event | category | flops | bytes accessed | tf_op | source)
XLA Modules:
  0.0 143.6 jit_solution(17179967268083898691)
XLA Ops:
  0.7 3.3 %pack.1 = (f32[64,10,4,128]{3,2,1,0:T(4,128)}, s32[16]{0:T(128)}, s32[16]{0:T(128)}, f32[2,16,1024]{2,1,0:T(8,128)}) custom-call(s32[1]{0:T(128)} %bitcast.me_ref, s32[16]{0:T(128)} %anchor_hbm.1, s32[16]{0:T(128)} %target_hbm.1, f32[16,16,1024]{2,1,0:T(8,128)} %state_ref.1, f32[3,16,1024]{2,1,0:T(8,128)} %bitcast.24, f32[4,1024]{1,0:T(4,128)} %taps_hbm.1), custom_call_target="tpu_custom_call" | custom-call | tf_op jit(solution)/shard_map/pack/pallas_call | solution.py:87
  4.0 18.9 %all-to-all-start = ((f32[64,10,4,128]{3,2,1,0:T(4,128)}), f32[64,10,4,128]{3,2,1,0:T(4,128)S(1)}, u32[]{:S(2)}, u32[]{:S(2)}) async-start(f32[64,10,4,128]{3,2,1,0:T(4,128)} %get-tuple-element.8), calls=%async_computation | async-start | bytes 2621440 | tf_op jit(solution)/shard_map/all_to_all | solution.py:202
  22.9 0.6 compare_and_fusion.1
  23.5 0.5 copy-done.17
  24.0 0.6 multiply_reduce_fusion
  24.6 64.8 %all-to-all-done.held_ref = f32[64,10,4,128]{3,2,1,0:T(4,128)S(1)} async-done(((f32[64,10,4,128]{3,2,1,0:T(4,128)}), f32[64,10,4,128]{3,2,1,0:T(4,128)S(1)}, u32[]{:S(2)}, u32[]{:S(2)}) %all-to-all-start) | async-done | bytes 1310752 | tf_op jit(solution)/shard_map/all_to_all | solution.py:202
  89.4 1.3 roll.1
  90.7 0.9 copy-done.2
  91.5 6.0 %all-to-all-start.1 = ((f32[64,6,4,128]{3,2,1,0:T(4,128)}), f32[64,6,4,128]{3,2,1,0:T(4,128)S(1)}, u32[]{:S(2)}, u32[]{:S(2)}) async-start(f32[64,6,4,128]{3,2,1,0:T(4,128)} %copy-done.2), calls=%async_computation.1 | async-start | bytes 1572864 | tf_op jit(solution)/shard_map/all_to_all | solution.py:202
  97.6 0.1 copy.22
  97.7 0.7 gather_fusion
  98.4 1.2 compare_and_fusion
  99.6 0.8 slice.46
  100.4 1.5 %reshape.50 = f32[64,2,1024]{2,1,0:T(2,128)S(1)} reshape(f32[64,4,4,128]{3,2,1,0:T(4,128)} %slice.46) | data formatting | bytes 1048576 | tf_op jit(solution)/shard_map/reshape | solution.py:247
  101.9 0.7 gather_fusion.1
  102.6 0.2 select_select_fusion
  102.8 0.1 fusion.7
  103.0 0.4 fusion.6
  103.5 1.9 %collective-permute-start = (f32[16,544]{1,0:T(8,128)S(1)}, f32[16,544]{1,0:T(8,128)S(1)}, u32[]{:S(2)}, u32[]{:S(2)}) collective-permute-start(f32[16,544]{1,0:T(8,128)S(1)} %slice_select_fusion), channel_id=1, source_target_pairs={{0,1},{1,0},{2,3},{3,2},{4,5},{5,4},{6,7},{7,6},{8,9},{9,8},{10,11... | collective-permute-start | bytes 104456 | tf_op jit(solution)/shard_map/ppermute | solution.py:211
  105.4 1.2 collective-permute-done
  106.6 2.7 %collective-permute-start.1 = (f32[16,544]{1,0:T(8,128)S(1)}, f32[16,544]{1,0:T(8,128)S(1)}, u32[]{:S(2)}, u32[]{:S(2)}) collective-permute-start(f32[16,544]{1,0:T(8,128)S(1)} %select_add_fusion), channel_id=1, source_target_pairs={{0,2},{1,3},{2,0},{3,1},{4,6},{5,7},{6,4},{7,5},{8,10},{9,11},{10,... | collective-permute-start | bytes 104456 | tf_op jit(solution)/shard_map/ppermute | solution.py:211
  109.4 3.1 %collective-permute-done.1 = f32[16,544]{1,0:T(8,128)S(1)} collective-permute-done((f32[16,544]{1,0:T(8,128)S(1)}, f32[16,544]{1,0:T(8,128)S(1)}, u32[]{:S(2)}, u32[]{:S(2)}) %collective-permute-start.1) | collective-permute-done | bytes 34848 | tf_op jit(solution)/shard_map/ppermute | solution.py:211
  112.5 3.3 %collective-permute-start.2 = (f32[16,544]{1,0:T(8,128)S(1)}, f32[16,544]{1,0:T(8,128)S(1)}, u32[]{:S(2)}, u32[]{:S(2)}) collective-permute-start(f32[16,544]{1,0:T(8,128)S(1)} %add.77), channel_id=1, source_target_pairs={{0,4},{1,5},{2,6},{3,7},{4,0},{5,1},{6,2},{7,3},{8,12},{9,13},{10,... | collective-permute-start | bytes 104456 | tf_op jit(solution)/shard_map/ppermute | solution.py:211
  115.9 4.0 %collective-permute-done.2 = f32[16,544]{1,0:T(8,128)S(1)} collective-permute-done((f32[16,544]{1,0:T(8,128)S(1)}, f32[16,544]{1,0:T(8,128)S(1)}, u32[]{:S(2)}, u32[]{:S(2)}) %collective-permute-start.2) | collective-permute-done | bytes 34848 | tf_op jit(solution)/shard_map/ppermute | solution.py:211
  119.9 1.9 %collective-permute-start.3 = (f32[16,544]{1,0:T(8,128)S(1)}, f32[16,544]{1,0:T(8,128)S(1)}, u32[]{:S(2)}, u32[]{:S(2)}) collective-permute-start(f32[16,544]{1,0:T(8,128)S(1)} %add.78), channel_id=1, source_target_pairs={{0,1},{1,0},{2,3},{3,2},{4,5},{5,4},{6,7},{7,6},{8,9},{9,8},{10,11... | collective-permute-start | bytes 104456 | tf_op jit(solution)/shard_map/ppermute | solution.py:211
  121.8 0.1 fusion.skip_ref
  121.9 1.1 collective-permute-done.3
  123.1 0.1 multiply_reduce_fusion.1
  123.2 0.4 copy-done.6
  123.6 1.6 %compare_select_fusion = f32[32,1024]{1,0:T(8,128)S(1)} fusion(bf16[512,1024]{1,0:T(8,128)(2,1)} %param.21, f32[1024]{0:T(1024)S(1)} %copy-done.13, f32[16,544]{1,0:T(8,128)} %copy-done.6, f32[16,544]{1,0:T(8,128)S(1)} %get-tuple-element.16, f32[512]{0:T(512)} %param.25, f32[32]{0:T(128)S(1)} %add_rsqrt_fusion), kind=kOutput, calls=%fused_computation.3 | convolution fusion | flops 33849344 | bytes 1255552 | tf_op jit(solution)/shard_map/dot_general | solution.py:263
  125.3 15.4 %all-to-all-done.1.moved_ref = f32[64,6,4,128]{3,2,1,0:T(4,128)S(1)} async-done(((f32[64,6,4,128]{3,2,1,0:T(4,128)}), f32[64,6,4,128]{3,2,1,0:T(4,128)S(1)}, u32[]{:S(2)}, u32[]{:S(2)}) %all-to-all-start.1) | async-done | bytes 786464 | tf_op jit(solution)/shard_map/all_to_all | solution.py:202
  140.7 2.9 %update.1 = (bf16[16,2,1024]{2,1,0:T(2,128)(2,1)}, f32[16,16,1024]{2,1,0:T(8,128)}) custom-call(s32[16]{0:T(128)S(1)} %copy-done.4, f32[2,32,16]{2,1,0:T(8,128)S(1)} %bitcast.22, f32[64,6,4,128]{3,2,1,0:T(4,128)S(1)} %all-to-all-done.1.moved_ref, f32[16,16,1024]{2,1,0:T(8,128)S(1)} %copy-done.1, f32[2,16,1024]{2,1,0:T(8,128)S(1)} %bitcast.21, ...), custom_call_target="tpu_custom_call" | custom-call | tf_op jit(solution)/shard_map/update/pallas_call | solution.py:181
  (51 shorter events, 0.4 us)
Async XLA Ops:
  0.6 102.4 %copy-start = (bf16[1024,544]{0,1:T(8,128)(2,1)S(1)}, bf16[1024,544]{0,1:T(8,128)(2,1)}, u32[]{:S(2)}) copy-start(bf16[1024,544]{0,1:T(8,128)(2,1)} %param.20) | copy-start | bytes 3342340
  3.9 18.9 %copy-start.11 = (f32[4,1024]{1,0:T(4,128)S(1)}, f32[4,1024]{1,0:T(4,128)}, u32[]{:S(2)}) copy-start(f32[4,1024]{1,0:T(4,128)} %taps_hbm.1) | copy-start | bytes 49156
  3.9 18.9 %copy-start.14 = (s32[16]{0:T(128)S(1)}, s32[16]{0:T(128)}, u32[]{:S(2)}) copy-start(s32[16]{0:T(128)} %anchor_hbm.1) | copy-start | bytes 196
  4.0 20.0 %copy-start.7 = (bf16[16,2,1024]{2,1,0:T(2,128)(2,1)S(1)}, bf16[16,2,1024]{2,1,0:T(2,128)(2,1)}, u32[]{:S(2)}) copy-start(bf16[16,2,1024]{2,1,0:T(2,128)(2,1)} %param.17) | copy-start | bytes 196612
  4.0 85.4 %copy-start.5 = (s32[16]{0:T(128)S(1)}, s32[16]{0:T(128)}, u32[]{:S(2)}) copy-start(s32[16]{0:T(128)} %get-tuple-element.9.offset_ref) | copy-start | bytes 196
  4.0 85.4 %all-to-all-start = ((f32[64,10,4,128]{3,2,1,0:T(4,128)}), f32[64,10,4,128]{3,2,1,0:T(4,128)S(1)}, u32[]{:S(2)}, u32[]{:S(2)}) async-start(f32[64,10,4,128]{3,2,1,0:T(4,128)} %get-tuple-element.8), calls=%async_computation | async-start | bytes 2621440 | tf_op jit(solution)/shard_map/all_to_all | solution.py:202
  23.5 0.5 copy-start.17
  90.7 0.9 copy-start.2
  91.5 6.0 %copy-start.9 = (f32[2,16,1024]{2,1,0:T(8,128)S(1)}, f32[2,16,1024]{2,1,0:T(8,128)}, u32[]{:S(2)}) copy-start(f32[2,16,1024]{2,1,0:T(8,128)} %get-tuple-element.7) | copy-start | bytes 393220
  91.5 49.2 %all-to-all-start.1 = ((f32[64,6,4,128]{3,2,1,0:T(4,128)}), f32[64,6,4,128]{3,2,1,0:T(4,128)S(1)}, u32[]{:S(2)}, u32[]{:S(2)}) async-start(f32[64,6,4,128]{3,2,1,0:T(4,128)} %copy-done.2), calls=%async_computation.1 | async-start | bytes 1572864 | tf_op jit(solution)/shard_map/all_to_all | solution.py:202
  99.6 3.0 %copy-start.15 = (pred[16]{0:T(512)(128)(4,1)S(1)}, pred[16]{0:T(512)(128)(4,1)}, u32[]{:S(2)}) copy-start(pred[16]{0:T(512)(128)(4,1)} %get-tuple-element.18) | copy-start | bytes 52
  99.6 3.0 %copy-start.16 = (pred[16]{0:T(512)(128)(4,1)S(1)}, pred[16]{0:T(512)(128)(4,1)}, u32[]{:S(2)}) copy-start(pred[16]{0:T(512)(128)(4,1)} %compare_and_fusion) | copy-start | bytes 52
  100.4 2.5 %copy-start.8 = (f32[16,1024]{1,0:T(8,128)S(1)}, f32[16,1024]{1,0:T(8,128)}, u32[]{:S(2)}) copy-start(f32[16,1024]{1,0:T(8,128)} %multiply_reduce_fusion) | copy-start | bytes 196612
  102.8 6.6 %copy-start.10 = (f32[16,1024]{1,0:T(8,128)S(1)}, f32[16,1024]{1,0:T(8,128)}, u32[]{:S(2)}) copy-start(f32[16,1024]{1,0:T(8,128)} %param.23) | copy-start | bytes 196612
  103.0 18.8 %copy-start.12 = (f32[1024]{0:T(1024)S(1)}, f32[1024]{0:T(1024)}, u32[]{:S(2)}) copy-start(f32[1024]{0:T(1024)} %param.24) | copy-start | bytes 12292
  103.4 20.2 %copy-start.13 = (f32[1024]{0:T(1024)S(1)}, f32[1024]{0:T(1024)}, u32[]{:S(2)}) copy-start(f32[1024]{0:T(1024)} %param.22) | copy-start | bytes 12292
  103.5 3.1 %collective-permute-start = (f32[16,544]{1,0:T(8,128)S(1)}, f32[16,544]{1,0:T(8,128)S(1)}, u32[]{:S(2)}, u32[]{:S(2)}) collective-permute-start(f32[16,544]{1,0:T(8,128)S(1)} %slice_select_fusion), channel_id=1, source_target_pairs={{0,1},{1,0},{2,3},{3,2},{4,5},{5,4},{6,7},{7,6},{8,9},{9,8},{10,11... | collective-permute-start | bytes 104456 | tf_op jit(solution)/shard_map/ppermute | solution.py:211
  106.6 5.9 %collective-permute-start.1 = (f32[16,544]{1,0:T(8,128)S(1)}, f32[16,544]{1,0:T(8,128)S(1)}, u32[]{:S(2)}, u32[]{:S(2)}) collective-permute-start(f32[16,544]{1,0:T(8,128)S(1)} %select_add_fusion), channel_id=1, source_target_pairs={{0,2},{1,3},{2,0},{3,1},{4,6},{5,7},{6,4},{7,5},{8,10},{9,11},{10,... | collective-permute-start | bytes 104456 | tf_op jit(solution)/shard_map/ppermute | solution.py:211
  112.5 7.4 %collective-permute-start.2 = (f32[16,544]{1,0:T(8,128)S(1)}, f32[16,544]{1,0:T(8,128)S(1)}, u32[]{:S(2)}, u32[]{:S(2)}) collective-permute-start(f32[16,544]{1,0:T(8,128)S(1)} %add.77), channel_id=1, source_target_pairs={{0,4},{1,5},{2,6},{3,7},{4,0},{5,1},{6,2},{7,3},{8,12},{9,13},{10,... | collective-permute-start | bytes 104456 | tf_op jit(solution)/shard_map/ppermute | solution.py:211
  115.8 24.9 %copy-start.1 = (f32[16,16,1024]{2,1,0:T(8,128)S(1)}, f32[16,16,1024]{2,1,0:T(8,128)}, u32[]{:S(2)}) copy-start(f32[16,16,1024]{2,1,0:T(8,128)} %state_ref.1) | copy-start | bytes 3145732
  115.8 24.9 %copy-start.3 = (bf16[16,2,1024]{2,1,0:T(2,128)(2,1)S(1)}, bf16[16,2,1024]{2,1,0:T(2,128)(2,1)}, u32[]{:S(2)}) copy-start(bf16[16,2,1024]{2,1,0:T(2,128)(2,1)} %gate_ref.1) | copy-start | bytes 196612
  115.9 24.9 %copy-start.4 = (s32[16]{0:T(128)S(1)}, s32[16]{0:T(128)}, u32[]{:S(2)}) copy-start(s32[16]{0:T(128)} %get-tuple-element.6.row_hbm) | copy-start | bytes 196
  119.9 3.1 %collective-permute-start.3 = (f32[16,544]{1,0:T(8,128)S(1)}, f32[16,544]{1,0:T(8,128)S(1)}, u32[]{:S(2)}, u32[]{:S(2)}) collective-permute-start(f32[16,544]{1,0:T(8,128)S(1)} %add.78), channel_id=1, source_target_pairs={{0,1},{1,0},{2,3},{3,2},{4,5},{5,4},{6,7},{7,6},{8,9},{9,8},{10,11... | collective-permute-start | bytes 104456 | tf_op jit(solution)/shard_map/ppermute | solution.py:211
  123.0 0.6 copy-start.6

commit v4 on v3

--- a/solution.py
+++ b/solution.py
@@ -16,12 +16,11 @@
 CONV = 4
 
 
-def fetch(pairs, sems):
+def begin(pairs, sems):
     copies = [pltpu.make_async_copy(src, dst, sems.at[i]) for i, (src, dst) in enumerate(pairs)]
     for copy in copies:
         copy.start()
-    for copy in copies:
-        copy.wait()
+    return copies
 
 
 def pack_kernel(
@@ -29,7 +28,7 @@
     leaving_ref, offset_ref, row_ref, sums_ref,
     anchor_ref, target_ref, state_ref, conv_ref, taps_ref, slot_of, rank_of, source, sems,
 ):
-    fetch(
+    copies = begin(
         [
             (anchor_hbm, anchor_ref),
             (target_hbm, target_ref),
@@ -42,8 +41,13 @@
     slots = state_ref.shape[0]
     peers = leaving_ref.shape[0]
     me = me_ref[0]
+    for d in range(peers):
+        for q in range(CONV):
+            leaving_ref[d, 2 * TILES + q] = jnp.zeros((4, 128), jnp.float32)
     for o in range(peers):
         slot_of[o] = -1
+    for copy in copies[:2]:
+        copy.wait()
     for s in range(slots):
         slot_of[(target_ref[s] // slots - me + peers) % peers] = s
     rank = jnp.int32(0)
@@ -59,13 +63,13 @@
         offset = (me - anchor_ref[s] // slots + peers) % peers
         row_ref[s] = jnp.where(offset == 0, GROUPS + anchor_ref[s] % slots, rank_of[offset])
 
+    for copy in copies[2:4]:
+        copy.wait()
     old = [conv_ref[i] for i in range(3)]
     taps = [taps_ref[i : i + 1, :] for i in range(3)]
     sums_ref[0] = old[0] * taps[0] + old[1] * taps[1] + old[2] * taps[2]
     sums_ref[1] = old[1] * taps[0] + old[2] * taps[1]
-    for d in range(peers):
-        for q in range(CONV):
-            leaving_ref[d, 2 * TILES + q] = jnp.zeros((4, 128), jnp.float32)
+    copies[4].wait()
     for k in range(GROUPS):
         slot = source[k]
         for t in range(16):
@@ -136,66 +140,103 @@
     )(me, offset, held)
 
 
-def update_kernel(
-    row_hbm, rest_hbm, moved_ref, state_ref, step_ref, x_ref, skip_ref, decay_ref, gate_ref,
-    mixed_ref, out_ref,
-    row_ref, rest_ref, held, y_ref, sems,
-):
-    fetch([(row_hbm, row_ref), (rest_hbm, rest_ref)], sems)
-    slots, state_size, width = state_ref.shape
-    steps = step_ref.shape[0]
-    for s in range(slots):
-        r = row_ref[s]
-
-        @pl.when(r < GROUPS)
-        def _():
-            rank = jnp.minimum(r, GROUPS - 1)
-            base, group = rank % 4 * 16, rank // 4 * 2
-            for t in range(16):
-                rows, lanes = 8 * (t // 8), 128 * (t % 8)
-                held[s, rows : rows + 8, lanes : lanes + 128] = jnp.concatenate(
-                    [moved_ref[base + t, group], moved_ref[base + t, group + 1]]
-                )
-
-        @pl.when(r >= GROUPS)
-        def _():
-            held[s] = state_ref[jnp.maximum(r - GROUPS, 0)]
-
+def plan_kernel(step_ref, x_ref, rest_ref, skip_ref, decay_ref, p_ref, q_ref, g_ref, y_ref):
+    steps, slots, width = step_ref.shape
+    state_size = decay_ref.shape[0]
     for s in range(slots):
         b = [rest_ref[i, :state_size, s : s + 1] for i in range(steps)]
         c = [rest_ref[i, state_size:, s : s + 1] for i in range(steps)]
         for lanes in range(0, width, 128):
             cut = slice(lanes, lanes + 128)
-            state = held[s, :, cut]
             decay = decay_ref[:, cut]
+            p, q = None, None
             for i in range(steps):
                 step = step_ref[i, s : s + 1, cut]
-                state = jnp.exp(-step * decay) * state + (step * x_ref[i, s : s + 1, cut]) * b[i]
-                y_ref[s, i : i + 1, cut] = jnp.sum(c[i] * state, axis=0, keepdims=True)
-            out_ref[s, :, cut] = state
+                x = x_ref[i, s : s + 1, cut]
+                kept = jnp.exp(-step * decay)
+                added = (step * x) * b[i]
+                p, q = (kept, added) if p is None else (kept * p, kept * q + added)
+                g_ref[i, s, :, cut] = c[i] * p
+                y_ref[s, i : i + 1, cut] = jnp.sum(c[i] * q, axis=0, keepdims=True) + skip_ref[:, cut] * x
+            p_ref[s, :, cut] = p
+            q_ref[s, :, cut] = q
+
+
+def plan(step, x, rest, skip, decay):
+    steps, slots, width = step.shape
+    whole = jax.ShapeDtypeStruct((slots, *decay.shape), jnp.float32)
+    return pl.pallas_call(
+        plan_kernel,
+        out_shape=(
+            whole,
+            whole,
+            jax.ShapeDtypeStruct((steps, *whole.shape), jnp.float32),
+            jax.ShapeDtypeStruct((slots, steps, width), jnp.float32),
+        ),
+        in_specs=[VMEM] * 5,
+        out_specs=(VMEM,) * 4,
+        compiler_params=pltpu.CompilerParams(vmem_limit_bytes=32 << 20),
+        name="plan",
+    )(step, x, rest, skip, decay)
+
+
+def update_kernel(row_hbm, moved_ref, state_ref, p_ref, q_ref, g_ref, plus_ref, gate_ref, mixed_ref, out_ref, row_ref, y_ref, sems):
+    for copy in begin([(row_hbm, row_ref)], sems):
+        copy.wait()
+    slots, state_size, width = state_ref.shape
+    steps = g_ref.shape[0]
+    for s in range(slots):
+        r = row_ref[s]
+
+        def advance(get):
+            for t in range(width // 128):
+                cut = slice(128 * t, 128 * t + 128)
+                sums = [0.0] * steps
+                for n in range(state_size // 8):
+                    rows = slice(8 * n, 8 * n + 8)
+                    state = get(n, t)
+                    out_ref[s, rows, cut] = p_ref[s, rows, cut] * state + q_ref[s, rows, cut]
+                    for i in range(steps):
+                        sums[i] = sums[i] + g_ref[i, s, rows, cut] * state
+                for i in range(steps):
+                    y_ref[s, i : i + 1, cut] = jnp.sum(sums[i], axis=0, keepdims=True)
+
+        @pl.when(r < GROUPS)
+        def _():
+            rank = jnp.minimum(r, GROUPS - 1)
+            base, group = rank % 4 * 16, rank // 4 * 2
+            advance(
+                lambda n, t: jnp.concatenate(
+                    [moved_ref[base + 8 * n + t, group], moved_ref[base + 8 * n + t, group + 1]]
+                )
+            )
+
+        @pl.when(r >= GROUPS)
+        def _():
+            slot = jnp.maximum(r - GROUPS, 0)
+            advance(lambda n, t: state_ref[slot, 8 * n : 8 * n + 8, 128 * t : 128 * t + 128])
+
         gate = gate_ref[s].astype(jnp.float32)
-        mixed_ref[s] = ((y_ref[s] + skip_ref[s]) * jax.nn.silu(gate)).astype(mixed_ref.dtype)
-
-
-def update(row, rest, moved, state, step, x, skip, decay, gate):
+        mixed_ref[s] = ((y_ref[s] + plus_ref[s]) * jax.nn.silu(gate)).astype(mixed_ref.dtype)
+
+
+def update(row, moved, state, p, q, g, plus, gate):
     return pl.pallas_call(
         update_kernel,
         out_shape=(
             jax.ShapeDtypeStruct(gate.shape, jnp.bfloat16),
             jax.ShapeDtypeStruct(state.shape, jnp.float32),
         ),
-        in_specs=[ANY, ANY] + [VMEM] * 7,
+        in_specs=[ANY] + [VMEM] * 7,
         out_specs=(VMEM, VMEM),
         scratch_shapes=[
             pltpu.SMEM(row.shape, jnp.int32),
-            pltpu.VMEM(rest.shape, jnp.float32),
-            pltpu.VMEM(state.shape, jnp.float32),
             pltpu.VMEM(gate.shape, jnp.float32),
-            pltpu.SemaphoreType.DMA((2,)),
+            pltpu.SemaphoreType.DMA((1,)),
         ],
         compiler_params=pltpu.CompilerParams(vmem_limit_bytes=32 << 20),
         name="update",
-    )(row, rest, moved, state, step, x, skip, decay, gate)
+    )(row, moved, state, p, q, g, plus, gate)
 
 
 def exchange(chunks):
@@ -203,20 +244,12 @@
 
 
 def sum_over_tp(part):
-    half = part.shape[0] // 2
     size = lax.axis_size("tp")
-    first = lax.axis_index("tp") % 2 == 0
-
-    def swap(array, bit):
-        return lax.ppermute(array, "tp", [(i, i ^ bit) for i in range(size)])
-
-    mine = jnp.where(first, part[:half], part[half:]) + swap(jnp.where(first, part[half:], part[:half]), 1)
-    bit = 2
+    bit = 1
     while bit < size:
-        mine = mine + swap(mine, bit)
+        part = part + lax.ppermute(part, "tp", [(i, i ^ bit) for i in range(size)])
         bit *= 2
-    other = swap(mine, 1)
-    return jnp.concatenate([jnp.where(first, mine, other), jnp.where(first, other, mine)])
+    return part
 
 
 def local(
@@ -262,18 +295,14 @@
     dt_low = (dt_part * inv_rms * dt_gain).astype(jnp.bfloat16)
     step_size = jax.nn.softplus(jnp.dot(dt_low, dt_weight, preferred_element_type=jnp.float32) + dt_bias)
     rest = totals[:, DTR:].reshape(steps, slots, 2 * state_size).transpose(0, 2, 1)
-    x_rows = conved.astype(jnp.float32).reshape(steps, slots, width)
-    return update(
-        row,
+    p, q, g, plus = plan(
+        step_size.reshape(steps, slots, width),
+        conved.astype(jnp.float32).reshape(steps, slots, width),
         rest,
-        moved,
-        ssm_state,
-        step_size.reshape(steps, slots, width),
-        x_rows,
-        (d_skip * x_rows).transpose(1, 0, 2),
+        d_skip.reshape(1, width),
         jnp.exp(a_log),
-        gate_in,
     )
+    return update(row, moved, ssm_state, p, q, g, plus, gate_in)
 
 
 def solution(mesh):

time: 144 us -> 147 us (1.021)
  blocking collectives: 0 us -> 85.3 us
  waiting for transfers between devices: 89.6 us -> 21.5 us
  starting transfers between devices: 34.7 us -> 14 us
  local copies, waits for them, and re-layouts: 5.84 us -> 12.3 us
    all_to_all x0 -> x1, blocking collectives: none -> 85.3 us  [exchange(): return lax.all_to_all(chunks, 'inst', 0, 0)]
    all_to_all x2 -> x1, waiting for transfers between devices: 80.2 us -> 12.2 us  [exchange(): return lax.all_to_all(chunks, 'inst', 0, 0)]
    all_to_all x2 -> x1, starting transfers between devices: 24.8 us -> 5.98 us  [exchange(): return lax.all_to_all(chunks, 'inst', 0, 0)]
    unnamed x36 -> x46, local copies, waits for them, and re-layouts: 1.85 us -> 8.3 us
    ppermute x4 -> x3, starting transfers between devices: 9.87 us -> 7.97 us  [sum_over_tp(): part = part + lax.ppermute(part, 'tp', [(i, i ^ bit) for i in range(size)])]
    ppermute x4 -> x3, waiting for transfers between devices: 9.37 us -> 9.3 us  [sum_over_tp(): part = part + lax.ppermute(part, 'tp', [(i, i ^ bit) for i in range(size)])]
  transfers between devices with their start and end apart: 6 -> 4, of which waited for: 6 -> 4; matrix products, arithmetic and copies ran while one was open for 6% -> 6% of each run, Pallas kernels for 0% -> 1%
where the time goes in v4:
time: 147 us
  blocking collectives  85.3 us (58%)
  waiting for transfers between devices  21.5 us (15%)
  starting transfers between devices  14 us (10%)
  local copies, waits for them, and re-layouts  12.3 us (8%)
  Pallas kernels  7.55 us (5%)
  other arithmetic  3.02 us (2%)
  matrix products  2.02 us (1%)
    all_to_all x1, blocking collectives, exchange(): return lax.all_to_all(chunks, 'inst', 0, 0)  85.3 us
    all_to_all x1, waiting for transfers between devices, exchange(): return lax.all_to_all(chunks, 'inst', 0, 0)  12.2 us
    ppermute x3, waiting for transfers between devices, sum_over_tp(): part = part + lax.ppermute(part, 'tp', [(i, i ^ bit) for i in range(size)])  9.3 us
    unnamed x46, local copies, waits for them, and re-layouts  8.3 us
    ppermute x3, starting transfers between devices, sum_over_tp(): part = part + lax.ppermute(part, 'tp', [(i, i ^ bit) for i in range(size)])  7.97 us
    all_to_all x1, starting transfers between devices, exchange(): return lax.all_to_all(chunks, 'inst', 0, 0)  5.98 us
  transfers between devices with their start and end apart: 4, of which 4 were waited for; matrix products, arithmetic and copies ran while one was open for 6% of the time, Pallas kernels for 1%

profile of v4, /device:TPU:6, one launch (start us, length us, event | category | flops | bytes accessed | tf_op | source)
XLA Modules:
  0.0 146.6 jit_solution(6336717680992540987)
XLA Ops:
  0.7 2.8 %pack.1 = (f32[64,10,4,128]{3,2,1,0:T(4,128)}, s32[16]{0:T(128)}, s32[16]{0:T(128)}, f32[2,16,1024]{2,1,0:T(8,128)}) custom-call(s32[1]{0:T(128)} %bitcast.me_ref, s32[16]{0:T(128)} %anchor_hbm.1, s32[16]{0:T(128)} %target_hbm.1, f32[16,16,1024]{2,1,0:T(8,128)} %state_ref.1, f32[3,16,1024]{2,1,0:T(8,128)} %bitcast.24, f32[4,1024]{1,0:T(4,128)} %taps_hbm.1), custom_call_target="tpu_custom_call" | custom-call | tf_op jit(solution)/shard_map/pack/pallas_call | solution.py:91
  3.4 85.3 %all_to_all.10.held_ref = f32[64,10,4,128]{3,2,1,0:T(4,128)S(1)} all-to-all(f32[64,10,4,128]{3,2,1,0:T(4,128)} %get-tuple-element.12), channel_id=1, replica_groups=mesh['inst'=64,'tp'=8] {'inst'}, dimensions={0} | all-to-all | bytes 2621440 | tf_op jit(solution)/shard_map/all_to_all | solution.py:243
  88.7 1.3 roll.1
  90.0 0.9 copy-done.2
  90.9 6.0 %all-to-all-start.1 = ((f32[64,6,4,128]{3,2,1,0:T(4,128)}), f32[64,6,4,128]{3,2,1,0:T(4,128)S(1)}, u32[]{:S(2)}, u32[]{:S(2)}) async-start(f32[64,6,4,128]{3,2,1,0:T(4,128)} %copy-done.2), calls=%async_computation.1 | async-start | bytes 1572864 | tf_op jit(solution)/shard_map/all_to_all | solution.py:243
  97.0 0.6 compare_and_fusion.1
  97.7 0.7 gather_fusion
  98.3 0.7 compare_select_fusion.1
  99.0 0.6 multiply_reduce_fusion
  99.7 0.7 compare_and_fusion
  100.4 0.8 slice.36
  101.2 1.5 reshape.52
  102.7 0.7 gather_fusion.1
  103.4 0.2 select_select_fusion
  103.8 0.4 fusion.4
  104.2 1.9 %collective-permute-start = (f32[32,544]{1,0:T(8,128)S(1)}, f32[32,544]{1,0:T(8,128)S(1)}, u32[]{:S(2)}, u32[]{:S(2)}) collective-permute-start(f32[32,544]{1,0:T(8,128)S(1)} %fusion.4), channel_id=1, source_target_pairs={{0,1},{1,0},{2,3},{3,2},{4,5},{5,4},{6,7},{7,6},{8,9},{9,8},{10,11... | collective-permute-start | bytes 208904 | tf_op jit(solution)/shard_map/ppermute | solution.py:250
  106.2 1.2 collective-permute-done
  107.4 2.7 %collective-permute-start.1 = (f32[32,544]{1,0:T(8,128)S(1)}, f32[32,544]{1,0:T(8,128)S(1)}, u32[]{:S(2)}, u32[]{:S(2)}) collective-permute-start(f32[32,544]{1,0:T(8,128)S(1)} %add.71), channel_id=1, source_target_pairs={{0,2},{1,3},{2,0},{3,1},{4,6},{5,7},{6,4},{7,5},{8,10},{9,11},{10,... | collective-permute-start | bytes 208904 | tf_op jit(solution)/shard_map/ppermute | solution.py:250
  110.2 3.6 %collective-permute-done.1 = f32[32,544]{1,0:T(8,128)S(1)} collective-permute-done((f32[32,544]{1,0:T(8,128)S(1)}, f32[32,544]{1,0:T(8,128)S(1)}, u32[]{:S(2)}, u32[]{:S(2)}) %collective-permute-start.1) | collective-permute-done | bytes 69664 | tf_op jit(solution)/shard_map/ppermute | solution.py:250
  113.8 3.3 %collective-permute-start.2 = (f32[32,544]{1,0:T(8,128)S(1)}, f32[32,544]{1,0:T(8,128)S(1)}, u32[]{:S(2)}, u32[]{:S(2)}) collective-permute-start(f32[32,544]{1,0:T(8,128)S(1)} %add.72), channel_id=1, source_target_pairs={{0,4},{1,5},{2,6},{3,7},{4,0},{5,1},{6,2},{7,3},{8,12},{9,13},{10,... | collective-permute-start | bytes 208904 | tf_op jit(solution)/shard_map/ppermute | solution.py:250
  117.2 4.5 %collective-permute-done.2 = f32[32,544]{1,0:T(8,128)S(1)} collective-permute-done((f32[32,544]{1,0:T(8,128)S(1)}, f32[32,544]{1,0:T(8,128)S(1)}, u32[]{:S(2)}, u32[]{:S(2)}) %collective-permute-start.2) | collective-permute-done | bytes 69664 | tf_op jit(solution)/shard_map/ppermute | solution.py:250
  121.8 0.1 multiply_reduce_fusion.1
  121.9 1.6 %compare_select_fusion = f32[32,1024]{1,0:T(8,128)S(1)} fusion(bf16[512,1024]{1,0:T(8,128)(2,1)} %param.21, f32[1024]{0:T(1024)S(1)} %copy-done.18, f32[32,544]{1,0:T(8,128)S(1)} %add.73, f32[512]{0:T(512)S(1)} %copy-done.19, f32[32]{0:T(128)S(1)} %add_rsqrt_fusion), kind=kOutput, calls=%fused_computation.3 | convolution fusion | flops 33832960 | bytes 1251840 | tf_op jit(solution)/shard_map/dot_general | solution.py:296
  123.5 1.0 plan.1
  124.6 1.3 copy-done.3
  125.9 1.0 copy-done.5
  126.8 1.0 copy-done.7
  127.8 12.2 %all-to-all-done.1.moved_ref = f32[64,6,4,128]{3,2,1,0:T(4,128)S(1)} async-done(((f32[64,6,4,128]{3,2,1,0:T(4,128)}), f32[64,6,4,128]{3,2,1,0:T(4,128)S(1)}, u32[]{:S(2)}, u32[]{:S(2)}) %all-to-all-start.1) | async-done | bytes 786464 | tf_op jit(solution)/shard_map/all_to_all | solution.py:243
  140.1 1.6 %copy-done.4 = f32[2,16,16,1024]{3,2,1,0:T(8,128)S(1)} copy-done((f32[2,16,16,1024]{3,2,1,0:T(8,128)S(1)}, f32[2,16,16,1024]{3,2,1,0:T(8,128)}, u32[]{:S(2)}) %copy-start.4) | copy-done | bytes 2097176
  141.7 1.2 copy-done.6
  142.9 1.2 copy-done.8
  144.1 2.5 %update.1 = (bf16[16,2,1024]{2,1,0:T(2,128)(2,1)}, f32[16,16,1024]{2,1,0:T(8,128)}) custom-call(s32[16]{0:T(128)S(1)} %copy-done.11, f32[64,6,4,128]{3,2,1,0:T(4,128)S(1)} %all-to-all-done.1.moved_ref, f32[16,16,1024]{2,1,0:T(8,128)S(1)} %copy-done.1, f32[16,16,1024]{2,1,0:T(8,128)S(1)} %copy-done.6, f32[16,16,1024]{2,1,0:T(8,128)S(1)} %copy-done.8, ...), custom_call_target="tpu_custom_call" | custom-call | tf_op jit(solution)/shard_map/update/pallas_call | solution.py:224
  (56 shorter events, 0.6 us)
Async XLA Ops:
  0.6 103.1 %copy-start = (bf16[1024,544]{0,1:T(8,128)(2,1)S(1)}, bf16[1024,544]{0,1:T(8,128)(2,1)}, u32[]{:S(2)}) copy-start(bf16[1024,544]{0,1:T(8,128)(2,1)} %param.20) | copy-start | bytes 3342340
  3.4 85.3 %copy-start.12 = (s32[16]{0:T(128)S(1)}, s32[16]{0:T(128)}, u32[]{:S(2)}) copy-start(s32[16]{0:T(128)} %get-tuple-element.11.offset_ref) | copy-start | bytes 196
  90.0 0.9 copy-start.2
  90.9 6.0 %copy-start.17 = (f32[4,1024]{1,0:T(4,128)S(1)}, f32[4,1024]{1,0:T(4,128)}, u32[]{:S(2)}) copy-start(f32[4,1024]{1,0:T(4,128)} %taps_hbm.1) | copy-start | bytes 49156
  90.9 6.0 %copy-start.15 = (f32[2,16,1024]{2,1,0:T(8,128)S(1)}, f32[2,16,1024]{2,1,0:T(8,128)}, u32[]{:S(2)}) copy-start(f32[2,16,1024]{2,1,0:T(8,128)} %get-tuple-element.13) | copy-start | bytes 393220
  90.9 6.2 %copy-start.20 = (s32[16]{0:T(128)S(1)}, s32[16]{0:T(128)}, u32[]{:S(2)}) copy-start(s32[16]{0:T(128)} %anchor_hbm.1) | copy-start | bytes 196
  90.9 8.1 %copy-start.13 = (bf16[16,2,1024]{2,1,0:T(2,128)(2,1)S(1)}, bf16[16,2,1024]{2,1,0:T(2,128)(2,1)}, u32[]{:S(2)}) copy-start(bf16[16,2,1024]{2,1,0:T(2,128)(2,1)} %param.17) | copy-start | bytes 196612
  90.9 49.2 %all-to-all-start.1 = ((f32[64,6,4,128]{3,2,1,0:T(4,128)}), f32[64,6,4,128]{3,2,1,0:T(4,128)S(1)}, u32[]{:S(2)}, u32[]{:S(2)}) async-start(f32[64,6,4,128]{3,2,1,0:T(4,128)} %copy-done.2), calls=%async_computation.1 | async-start | bytes 1572864 | tf_op jit(solution)/shard_map/all_to_all | solution.py:243
  100.3 3.0 %copy-start.21 = (pred[16]{0:T(512)(128)(4,1)S(1)}, pred[16]{0:T(512)(128)(4,1)}, u32[]{:S(2)}) copy-start(pred[16]{0:T(512)(128)(4,1)} %get-tuple-element.20) | copy-start | bytes 52
  100.4 3.0 %copy-start.22 = (pred[16]{0:T(512)(128)(4,1)S(1)}, pred[16]{0:T(512)(128)(4,1)}, u32[]{:S(2)}) copy-start(pred[16]{0:T(512)(128)(4,1)} %get-tuple-element.24) | copy-start | bytes 52
  101.2 2.5 %copy-start.14 = (f32[16,1024]{1,0:T(8,128)S(1)}, f32[16,1024]{1,0:T(8,128)}, u32[]{:S(2)}) copy-start(f32[16,1024]{1,0:T(8,128)} %multiply_reduce_fusion) | copy-start | bytes 196612
  103.6 6.6 %copy-start.16 = (f32[16,1024]{1,0:T(8,128)S(1)}, f32[16,1024]{1,0:T(8,128)}, u32[]{:S(2)}) copy-start(f32[16,1024]{1,0:T(8,128)} %param.23) | copy-start | bytes 196612
  103.8 18.1 %copy-start.18 = (f32[1024]{0:T(1024)S(1)}, f32[1024]{0:T(1024)}, u32[]{:S(2)}) copy-start(f32[1024]{0:T(1024)} %param.22) | copy-start | bytes 12292
  103.8 18.1 %copy-start.19 = (f32[512]{0:T(512)S(1)}, f32[512]{0:T(512)}, u32[]{:S(2)}) copy-start(f32[512]{0:T(512)} %param.25) | copy-start | bytes 6148
  104.2 3.2 %collective-permute-start = (f32[32,544]{1,0:T(8,128)S(1)}, f32[32,544]{1,0:T(8,128)S(1)}, u32[]{:S(2)}, u32[]{:S(2)}) collective-permute-start(f32[32,544]{1,0:T(8,128)S(1)} %fusion.4), channel_id=1, source_target_pairs={{0,1},{1,0},{2,3},{3,2},{4,5},{5,4},{6,7},{7,6},{8,9},{9,8},{10,11... | collective-permute-start | bytes 208904 | tf_op jit(solution)/shard_map/ppermute | solution.py:250
  107.4 6.4 %collective-permute-start.1 = (f32[32,544]{1,0:T(8,128)S(1)}, f32[32,544]{1,0:T(8,128)S(1)}, u32[]{:S(2)}, u32[]{:S(2)}) collective-permute-start(f32[32,544]{1,0:T(8,128)S(1)} %add.71), channel_id=1, source_target_pairs={{0,2},{1,3},{2,0},{3,1},{4,6},{5,7},{6,4},{7,5},{8,10},{9,11},{10,... | collective-permute-start | bytes 208904 | tf_op jit(solution)/shard_map/ppermute | solution.py:250
  110.2 13.3 %copy-start.10 = (f32[1024]{0:T(1024)S(1)}, f32[1024]{0:T(1024)}, u32[]{:S(2)}) copy-start(f32[1024]{0:T(1024)} %param.24) | copy-start | bytes 12292
  113.8 7.8 %collective-permute-start.2 = (f32[32,544]{1,0:T(8,128)S(1)}, f32[32,544]{1,0:T(8,128)S(1)}, u32[]{:S(2)}, u32[]{:S(2)}) collective-permute-start(f32[32,544]{1,0:T(8,128)S(1)} %add.72), channel_id=1, source_target_pairs={{0,4},{1,5},{2,6},{3,7},{4,0},{5,1},{6,2},{7,3},{8,12},{9,13},{10,... | collective-permute-start | bytes 208904 | tf_op jit(solution)/shard_map/ppermute | solution.py:250
  117.2 22.9 %copy-start.1 = (f32[16,16,1024]{2,1,0:T(8,128)S(1)}, f32[16,16,1024]{2,1,0:T(8,128)}, u32[]{:S(2)}) copy-start(f32[16,16,1024]{2,1,0:T(8,128)} %state_ref.1) | copy-start | bytes 3145732
  117.2 22.9 %copy-start.9 = (bf16[16,2,1024]{2,1,0:T(2,128)(2,1)S(1)}, bf16[16,2,1024]{2,1,0:T(2,128)(2,1)}, u32[]{:S(2)}) copy-start(bf16[16,2,1024]{2,1,0:T(2,128)(2,1)} %gate_ref.1) | copy-start | bytes 196612
  117.2 22.9 %copy-start.11 = (s32[16]{0:T(128)S(1)}, s32[16]{0:T(128)}, u32[]{:S(2)}) copy-start(s32[16]{0:T(128)} %get-tuple-element.10.row_hbm) | copy-start | bytes 196
  124.5 1.3 copy-start.3
  125.9 1.0 copy-start.5
  126.8 1.0 copy-start.7
  140.1 1.6 %copy-start.4 = (f32[2,16,16,1024]{3,2,1,0:T(8,128)S(1)}, f32[2,16,16,1024]{3,2,1,0:T(8,128)}, u32[]{:S(2)}) copy-start(f32[2,16,16,1024]{3,2,1,0:T(8,128)} %copy-done.3) | copy-start | bytes 6291460
  141.7 1.2 copy-start.6
  142.9 1.2 copy-start.8

commit v5 on v4

--- a/solution.py
+++ b/solution.py
@@ -135,7 +135,7 @@
         out_shape=jax.ShapeDtypeStruct((peers, 2 * TILES, 4, 128), jnp.float32),
         in_specs=[SMEM, SMEM, VMEM],
         out_specs=VMEM,
-        compiler_params=pltpu.CompilerParams(vmem_limit_bytes=32 << 20),
+        compiler_params=pltpu.CompilerParams(vmem_limit_bytes=12 << 20),
         name="roll",
     )(me, offset, held)
 
@@ -175,7 +175,7 @@
         ),
         in_specs=[VMEM] * 5,
         out_specs=(VMEM,) * 4,
-        compiler_params=pltpu.CompilerParams(vmem_limit_bytes=32 << 20),
+        compiler_params=pltpu.CompilerParams(vmem_limit_bytes=12 << 20),
         name="plan",
     )(step, x, rest, skip, decay)
 
@@ -234,7 +234,7 @@
             pltpu.VMEM(gate.shape, jnp.float32),
             pltpu.SemaphoreType.DMA((1,)),
         ],
-        compiler_params=pltpu.CompilerParams(vmem_limit_bytes=32 << 20),
+        compiler_params=pltpu.CompilerParams(vmem_limit_bytes=12 << 20),
         name="update",
     )(row, moved, state, p, q, g, plus, gate)
 

time: 147 us -> 147 us (level)
  no operation moved by 1% of the time
where the time goes in v5:
time: 147 us
  blocking collectives  85.3 us (58%)
  waiting for transfers between devices  21.5 us (15%)
  starting transfers between devices  14 us (10%)
  local copies, waits for them, and re-layouts  12.3 us (8%)
  Pallas kernels  7.55 us (5%)
  other arithmetic  3.02 us (2%)
  matrix products  2.02 us (1%)
    all_to_all x1, blocking collectives, exchange(): return lax.all_to_all(chunks, 'inst', 0, 0)  85.3 us
    all_to_all x1, waiting for transfers between devices, exchange(): return lax.all_to_all(chunks, 'inst', 0, 0)  12.2 us
    ppermute x3, waiting for transfers between devices, sum_over_tp(): part = part + lax.ppermute(part, 'tp', [(i, i ^ bit) for i in range(size)])  9.3 us
    unnamed x46, local copies, waits for them, and re-layouts  8.3 us
    ppermute x3, starting transfers between devices, sum_over_tp(): part = part + lax.ppermute(part, 'tp', [(i, i ^ bit) for i in range(size)])  7.97 us
    all_to_all x1, starting transfers between devices, exchange(): return lax.all_to_all(chunks, 'inst', 0, 0)  5.98 us
  transfers between devices with their start and end apart: 4, of which 4 were waited for; matrix products, arithmetic and copies ran while one was open for 6% of the time, Pallas kernels for 1%

profile of v5, /device:TPU:6, one launch (start us, length us, event | category | flops | bytes accessed | tf_op | source)
XLA Modules:
  0.0 146.6 jit_solution(16270644418640746884)
XLA Ops:
  0.7 2.8 %pack.1 = (f32[64,10,4,128]{3,2,1,0:T(4,128)}, s32[16]{0:T(128)}, s32[16]{0:T(128)}, f32[2,16,1024]{2,1,0:T(8,128)}) custom-call(s32[1]{0:T(128)} %bitcast.me_ref, s32[16]{0:T(128)} %anchor_hbm.1, s32[16]{0:T(128)} %target_hbm.1, f32[16,16,1024]{2,1,0:T(8,128)} %state_ref.1, f32[3,16,1024]{2,1,0:T(8,128)} %bitcast.24, f32[4,1024]{1,0:T(4,128)} %taps_hbm.1), custom_call_target="tpu_custom_call" | custom-call | tf_op jit(solution)/shard_map/pack/pallas_call | solution.py:91
  3.4 85.3 %all_to_all.10.held_ref = f32[64,10,4,128]{3,2,1,0:T(4,128)S(1)} all-to-all(f32[64,10,4,128]{3,2,1,0:T(4,128)} %get-tuple-element.12), channel_id=1, replica_groups=mesh['inst'=64,'tp'=8] {'inst'}, dimensions={0} | all-to-all | bytes 2621440 | tf_op jit(solution)/shard_map/all_to_all | solution.py:243
  88.7 1.3 roll.1
  90.0 0.9 copy-done.2
  90.9 6.0 %all-to-all-start.1 = ((f32[64,6,4,128]{3,2,1,0:T(4,128)}), f32[64,6,4,128]{3,2,1,0:T(4,128)S(1)}, u32[]{:S(2)}, u32[]{:S(2)}) async-start(f32[64,6,4,128]{3,2,1,0:T(4,128)} %copy-done.2), calls=%async_computation.1 | async-start | bytes 1572864 | tf_op jit(solution)/shard_map/all_to_all | solution.py:243
  97.0 0.6 compare_and_fusion.1
  97.7 0.7 gather_fusion
  98.3 0.7 compare_select_fusion.1
  99.0 0.6 multiply_reduce_fusion
  99.7 0.7 compare_and_fusion
  100.4 0.8 slice.36
  101.2 1.5 reshape.52
  102.7 0.7 gather_fusion.1
  103.4 0.2 select_select_fusion
  103.8 0.4 fusion.4
  104.2 1.9 %collective-permute-start = (f32[32,544]{1,0:T(8,128)S(1)}, f32[32,544]{1,0:T(8,128)S(1)}, u32[]{:S(2)}, u32[]{:S(2)}) collective-permute-start(f32[32,544]{1,0:T(8,128)S(1)} %fusion.4), channel_id=1, source_target_pairs={{0,1},{1,0},{2,3},{3,2},{4,5},{5,4},{6,7},{7,6},{8,9},{9,8},{10,11... | collective-permute-start | bytes 208904 | tf_op jit(solution)/shard_map/ppermute | solution.py:250
  106.2 1.2 collective-permute-done
  107.4 2.7 %collective-permute-start.1 = (f32[32,544]{1,0:T(8,128)S(1)}, f32[32,544]{1,0:T(8,128)S(1)}, u32[]{:S(2)}, u32[]{:S(2)}) collective-permute-start(f32[32,544]{1,0:T(8,128)S(1)} %add.71), channel_id=1, source_target_pairs={{0,2},{1,3},{2,0},{3,1},{4,6},{5,7},{6,4},{7,5},{8,10},{9,11},{10,... | collective-permute-start | bytes 208904 | tf_op jit(solution)/shard_map/ppermute | solution.py:250
  110.2 3.6 %collective-permute-done.1 = f32[32,544]{1,0:T(8,128)S(1)} collective-permute-done((f32[32,544]{1,0:T(8,128)S(1)}, f32[32,544]{1,0:T(8,128)S(1)}, u32[]{:S(2)}, u32[]{:S(2)}) %collective-permute-start.1) | collective-permute-done | bytes 69664 | tf_op jit(solution)/shard_map/ppermute | solution.py:250
  113.8 3.3 %collective-permute-start.2 = (f32[32,544]{1,0:T(8,128)S(1)}, f32[32,544]{1,0:T(8,128)S(1)}, u32[]{:S(2)}, u32[]{:S(2)}) collective-permute-start(f32[32,544]{1,0:T(8,128)S(1)} %add.72), channel_id=1, source_target_pairs={{0,4},{1,5},{2,6},{3,7},{4,0},{5,1},{6,2},{7,3},{8,12},{9,13},{10,... | collective-permute-start | bytes 208904 | tf_op jit(solution)/shard_map/ppermute | solution.py:250
  117.2 4.5 %collective-permute-done.2 = f32[32,544]{1,0:T(8,128)S(1)} collective-permute-done((f32[32,544]{1,0:T(8,128)S(1)}, f32[32,544]{1,0:T(8,128)S(1)}, u32[]{:S(2)}, u32[]{:S(2)}) %collective-permute-start.2) | collective-permute-done | bytes 69664 | tf_op jit(solution)/shard_map/ppermute | solution.py:250
  121.8 0.1 multiply_reduce_fusion.1
  121.9 1.6 %compare_select_fusion = f32[32,1024]{1,0:T(8,128)S(1)} fusion(bf16[512,1024]{1,0:T(8,128)(2,1)} %param.21, f32[1024]{0:T(1024)S(1)} %copy-done.18, f32[32,544]{1,0:T(8,128)S(1)} %add.73, f32[512]{0:T(512)S(1)} %copy-done.19, f32[32]{0:T(128)S(1)} %add_rsqrt_fusion), kind=kOutput, calls=%fused_computation.3 | convolution fusion | flops 33832960 | bytes 1251840 | tf_op jit(solution)/shard_map/dot_general | solution.py:296
  123.5 1.0 plan.1
  124.6 1.3 copy-done.3
  125.9 1.0 copy-done.5
  126.8 1.0 copy-done.7
  127.8 12.2 %all-to-all-done.1.moved_ref = f32[64,6,4,128]{3,2,1,0:T(4,128)S(1)} async-done(((f32[64,6,4,128]{3,2,1,0:T(4,128)}), f32[64,6,4,128]{3,2,1,0:T(4,128)S(1)}, u32[]{:S(2)}, u32[]{:S(2)}) %all-to-all-start.1) | async-done | bytes 786464 | tf_op jit(solution)/shard_map/all_to_all | solution.py:243
  140.1 1.6 %copy-done.4 = f32[2,16,16,1024]{3,2,1,0:T(8,128)S(1)} copy-done((f32[2,16,16,1024]{3,2,1,0:T(8,128)S(1)}, f32[2,16,16,1024]{3,2,1,0:T(8,128)}, u32[]{:S(2)}) %copy-start.4) | copy-done | bytes 2097176
  141.7 1.2 copy-done.6
  142.9 1.2 copy-done.8
  144.1 2.5 %update.1 = (bf16[16,2,1024]{2,1,0:T(2,128)(2,1)}, f32[16,16,1024]{2,1,0:T(8,128)}) custom-call(s32[16]{0:T(128)S(1)} %copy-done.11, f32[64,6,4,128]{3,2,1,0:T(4,128)S(1)} %all-to-all-done.1.moved_ref, f32[16,16,1024]{2,1,0:T(8,128)S(1)} %copy-done.1, f32[16,16,1024]{2,1,0:T(8,128)S(1)} %copy-done.6, f32[16,16,1024]{2,1,0:T(8,128)S(1)} %copy-done.8, ...), custom_call_target="tpu_custom_call" | custom-call | tf_op jit(solution)/shard_map/update/pallas_call | solution.py:224
  (56 shorter events, 0.6 us)
Async XLA Ops:
  0.6 103.1 %copy-start = (bf16[1024,544]{0,1:T(8,128)(2,1)S(1)}, bf16[1024,544]{0,1:T(8,128)(2,1)}, u32[]{:S(2)}) copy-start(bf16[1024,544]{0,1:T(8,128)(2,1)} %param.20) | copy-start | bytes 3342340
  3.4 85.3 %copy-start.12 = (s32[16]{0:T(128)S(1)}, s32[16]{0:T(128)}, u32[]{:S(2)}) copy-start(s32[16]{0:T(128)} %get-tuple-element.11.offset_ref) | copy-start | bytes 196
  90.0 0.9 copy-start.2
  90.9 6.0 %copy-start.17 = (f32[4,1024]{1,0:T(4,128)S(1)}, f32[4,1024]{1,0:T(4,128)}, u32[]{:S(2)}) copy-start(f32[4,1024]{1,0:T(4,128)} %taps_hbm.1) | copy-start | bytes 49156
  90.9 6.0 %copy-start.15 = (f32[2,16,1024]{2,1,0:T(8,128)S(1)}, f32[2,16,1024]{2,1,0:T(8,128)}, u32[]{:S(2)}) copy-start(f32[2,16,1024]{2,1,0:T(8,128)} %get-tuple-element.13) | copy-start | bytes 393220
  90.9 6.2 %copy-start.20 = (s32[16]{0:T(128)S(1)}, s32[16]{0:T(128)}, u32[]{:S(2)}) copy-start(s32[16]{0:T(128)} %anchor_hbm.1) | copy-start | bytes 196
  90.9 8.1 %copy-start.13 = (bf16[16,2,1024]{2,1,0:T(2,128)(2,1)S(1)}, bf16[16,2,1024]{2,1,0:T(2,128)(2,1)}, u32[]{:S(2)}) copy-start(bf16[16,2,1024]{2,1,0:T(2,128)(2,1)} %param.17) | copy-start | bytes 196612
  90.9 49.2 %all-to-all-start.1 = ((f32[64,6,4,128]{3,2,1,0:T(4,128)}), f32[64,6,4,128]{3,2,1,0:T(4,128)S(1)}, u32[]{:S(2)}, u32[]{:S(2)}) async-start(f32[64,6,4,128]{3,2,1,0:T(4,128)} %copy-done.2), calls=%async_computation.1 | async-start | bytes 1572864 | tf_op jit(solution)/shard_map/all_to_all | solution.py:243
  100.3 3.0 %copy-start.21 = (pred[16]{0:T(512)(128)(4,1)S(1)}, pred[16]{0:T(512)(128)(4,1)}, u32[]{:S(2)}) copy-start(pred[16]{0:T(512)(128)(4,1)} %get-tuple-element.20) | copy-start | bytes 52
  100.4 3.0 %copy-start.22 = (pred[16]{0:T(512)(128)(4,1)S(1)}, pred[16]{0:T(512)(128)(4,1)}, u32[]{:S(2)}) copy-start(pred[16]{0:T(512)(128)(4,1)} %get-tuple-element.24) | copy-start | bytes 52
  101.2 2.5 %copy-start.14 = (f32[16,1024]{1,0:T(8,128)S(1)}, f32[16,1024]{1,0:T(8,128)}, u32[]{:S(2)}) copy-start(f32[16,1024]{1,0:T(8,128)} %multiply_reduce_fusion) | copy-start | bytes 196612
  103.6 6.6 %copy-start.16 = (f32[16,1024]{1,0:T(8,128)S(1)}, f32[16,1024]{1,0:T(8,128)}, u32[]{:S(2)}) copy-start(f32[16,1024]{1,0:T(8,128)} %param.23) | copy-start | bytes 196612
  103.8 18.1 %copy-start.18 = (f32[1024]{0:T(1024)S(1)}, f32[1024]{0:T(1024)}, u32[]{:S(2)}) copy-start(f32[1024]{0:T(1024)} %param.22) | copy-start | bytes 12292
  103.8 18.1 %copy-start.19 = (f32[512]{0:T(512)S(1)}, f32[512]{0:T(512)}, u32[]{:S(2)}) copy-start(f32[512]{0:T(512)} %param.25) | copy-start | bytes 6148
  104.2 3.2 %collective-permute-start = (f32[32,544]{1,0:T(8,128)S(1)}, f32[32,544]{1,0:T(8,128)S(1)}, u32[]{:S(2)}, u32[]{:S(2)}) collective-permute-start(f32[32,544]{1,0:T(8,128)S(1)} %fusion.4), channel_id=1, source_target_pairs={{0,1},{1,0},{2,3},{3,2},{4,5},{5,4},{6,7},{7,6},{8,9},{9,8},{10,11... | collective-permute-start | bytes 208904 | tf_op jit(solution)/shard_map/ppermute | solution.py:250
  107.4 6.4 %collective-permute-start.1 = (f32[32,544]{1,0:T(8,128)S(1)}, f32[32,544]{1,0:T(8,128)S(1)}, u32[]{:S(2)}, u32[]{:S(2)}) collective-permute-start(f32[32,544]{1,0:T(8,128)S(1)} %add.71), channel_id=1, source_target_pairs={{0,2},{1,3},{2,0},{3,1},{4,6},{5,7},{6,4},{7,5},{8,10},{9,11},{10,... | collective-permute-start | bytes 208904 | tf_op jit(solution)/shard_map/ppermute | solution.py:250
  110.2 13.3 %copy-start.10 = (f32[1024]{0:T(1024)S(1)}, f32[1024]{0:T(1024)}, u32[]{:S(2)}) copy-start(f32[1024]{0:T(1024)} %param.24) | copy-start | bytes 12292
  113.8 7.8 %collective-permute-start.2 = (f32[32,544]{1,0:T(8,128)S(1)}, f32[32,544]{1,0:T(8,128)S(1)}, u32[]{:S(2)}, u32[]{:S(2)}) collective-permute-start(f32[32,544]{1,0:T(8,128)S(1)} %add.72), channel_id=1, source_target_pairs={{0,4},{1,5},{2,6},{3,7},{4,0},{5,1},{6,2},{7,3},{8,12},{9,13},{10,... | collective-permute-start | bytes 208904 | tf_op jit(solution)/shard_map/ppermute | solution.py:250
  117.2 22.9 %copy-start.1 = (f32[16,16,1024]{2,1,0:T(8,128)S(1)}, f32[16,16,1024]{2,1,0:T(8,128)}, u32[]{:S(2)}) copy-start(f32[16,16,1024]{2,1,0:T(8,128)} %state_ref.1) | copy-start | bytes 3145732
  117.2 22.9 %copy-start.9 = (bf16[16,2,1024]{2,1,0:T(2,128)(2,1)S(1)}, bf16[16,2,1024]{2,1,0:T(2,128)(2,1)}, u32[]{:S(2)}) copy-start(bf16[16,2,1024]{2,1,0:T(2,128)(2,1)} %gate_ref.1) | copy-start | bytes 196612
  117.2 22.9 %copy-start.11 = (s32[16]{0:T(128)S(1)}, s32[16]{0:T(128)}, u32[]{:S(2)}) copy-start(s32[16]{0:T(128)} %get-tuple-element.10.row_hbm) | copy-start | bytes 196
  124.5 1.3 copy-start.3
  125.9 1.0 copy-start.5
  126.8 1.0 copy-start.7
  140.1 1.6 %copy-start.4 = (f32[2,16,16,1024]{3,2,1,0:T(8,128)S(1)}, f32[2,16,16,1024]{3,2,1,0:T(8,128)}, u32[]{:S(2)}) copy-start(f32[2,16,16,1024]{3,2,1,0:T(8,128)} %copy-done.3) | copy-start | bytes 6291460
  141.7 1.2 copy-start.6
  142.9 1.2 copy-start.8

commit v6 on v3

--- a/solution.py
+++ b/solution.py
@@ -16,12 +16,11 @@
 CONV = 4
 
 
-def fetch(pairs, sems):
+def begin(pairs, sems):
     copies = [pltpu.make_async_copy(src, dst, sems.at[i]) for i, (src, dst) in enumerate(pairs)]
     for copy in copies:
         copy.start()
-    for copy in copies:
-        copy.wait()
+    return copies
 
 
 def pack_kernel(
@@ -29,7 +28,7 @@
     leaving_ref, offset_ref, row_ref, sums_ref,
     anchor_ref, target_ref, state_ref, conv_ref, taps_ref, slot_of, rank_of, source, sems,
 ):
-    fetch(
+    copies = begin(
         [
             (anchor_hbm, anchor_ref),
             (target_hbm, target_ref),
@@ -42,8 +41,13 @@
     slots = state_ref.shape[0]
     peers = leaving_ref.shape[0]
     me = me_ref[0]
+    for d in range(peers):
+        for q in range(CONV):
+            leaving_ref[d, 2 * TILES + q] = jnp.zeros((4, 128), jnp.float32)
     for o in range(peers):
         slot_of[o] = -1
+    for copy in copies[:2]:
+        copy.wait()
     for s in range(slots):
         slot_of[(target_ref[s] // slots - me + peers) % peers] = s
     rank = jnp.int32(0)
@@ -59,13 +63,13 @@
         offset = (me - anchor_ref[s] // slots + peers) % peers
         row_ref[s] = jnp.where(offset == 0, GROUPS + anchor_ref[s] % slots, rank_of[offset])
 
+    for copy in copies[2:4]:
+        copy.wait()
     old = [conv_ref[i] for i in range(3)]
     taps = [taps_ref[i : i + 1, :] for i in range(3)]
     sums_ref[0] = old[0] * taps[0] + old[1] * taps[1] + old[2] * taps[2]
     sums_ref[1] = old[1] * taps[0] + old[2] * taps[1]
-    for d in range(peers):
-        for q in range(CONV):
-            leaving_ref[d, 2 * TILES + q] = jnp.zeros((4, 128), jnp.float32)
+    copies[4].wait()
     for k in range(GROUPS):
         slot = source[k]
         for t in range(16):
@@ -137,44 +141,38 @@
 
 
 def update_kernel(
-    row_hbm, rest_hbm, moved_ref, state_ref, step_ref, x_ref, skip_ref, decay_ref, gate_ref,
-    mixed_ref, out_ref,
-    row_ref, rest_ref, held, y_ref, sems,
+    row_hbm, rest_ref, moved_ref, state_ref, step_ref, x_ref, skip_ref, decay_ref, gate_ref,
+    mixed_ref, out_hbm,
+    row_ref, out_ref, y_ref, row_sem, out_sems,
 ):
-    fetch([(row_hbm, row_ref), (rest_hbm, rest_ref)], sems)
+    for copy in begin([(row_hbm, row_ref)], row_sem):
+        copy.wait()
     slots, state_size, width = state_ref.shape
     steps = step_ref.shape[0]
+    copies = []
     for s in range(slots):
         r = row_ref[s]
-
-        @pl.when(r < GROUPS)
-        def _():
-            rank = jnp.minimum(r, GROUPS - 1)
-            base, group = rank % 4 * 16, rank // 4 * 2
-            for t in range(16):
-                rows, lanes = 8 * (t // 8), 128 * (t % 8)
-                held[s, rows : rows + 8, lanes : lanes + 128] = jnp.concatenate(
-                    [moved_ref[base + t, group], moved_ref[base + t, group + 1]]
-                )
-
-        @pl.when(r >= GROUPS)
-        def _():
-            held[s] = state_ref[jnp.maximum(r - GROUPS, 0)]
-
-    for s in range(slots):
         b = [rest_ref[i, :state_size, s : s + 1] for i in range(steps)]
         c = [rest_ref[i, state_size:, s : s + 1] for i in range(steps)]
-        for lanes in range(0, width, 128):
-            cut = slice(lanes, lanes + 128)
-            state = held[s, :, cut]
+        rank = jnp.clip(r, 0, GROUPS - 1)
+        base, group = rank % 4 * 16, rank // 4 * 2
+        slot = jnp.clip(r - GROUPS, 0, slots - 1)
+        for t in range(width // 128):
+            cut = slice(128 * t, 128 * t + 128)
+            came = [moved_ref[base + 8 * n + t, group + h] for n in range(2) for h in range(2)]
+            state = jnp.where(r < GROUPS, jnp.concatenate(came), state_ref[slot, :, cut])
             decay = decay_ref[:, cut]
             for i in range(steps):
                 step = step_ref[i, s : s + 1, cut]
                 state = jnp.exp(-step * decay) * state + (step * x_ref[i, s : s + 1, cut]) * b[i]
                 y_ref[s, i : i + 1, cut] = jnp.sum(c[i] * state, axis=0, keepdims=True)
             out_ref[s, :, cut] = state
+        copies.append(pltpu.make_async_copy(out_ref.at[s], out_hbm.at[s], out_sems.at[s]))
+        copies[-1].start()
         gate = gate_ref[s].astype(jnp.float32)
         mixed_ref[s] = ((y_ref[s] + skip_ref[s]) * jax.nn.silu(gate)).astype(mixed_ref.dtype)
+    for copy in copies:
+        copy.wait()
 
 
 def update(row, rest, moved, state, step, x, skip, decay, gate):
@@ -184,14 +182,14 @@
             jax.ShapeDtypeStruct(gate.shape, jnp.bfloat16),
             jax.ShapeDtypeStruct(state.shape, jnp.float32),
         ),
-        in_specs=[ANY, ANY] + [VMEM] * 7,
-        out_specs=(VMEM, VMEM),
+        in_specs=[ANY] + [VMEM] * 8,
+        out_specs=(VMEM, ANY),
         scratch_shapes=[
             pltpu.SMEM(row.shape, jnp.int32),
-            pltpu.VMEM(rest.shape, jnp.float32),
             pltpu.VMEM(state.shape, jnp.float32),
             pltpu.VMEM(gate.shape, jnp.float32),
-            pltpu.SemaphoreType.DMA((2,)),
+            pltpu.SemaphoreType.DMA((1,)),
+            pltpu.SemaphoreType.DMA((state.shape[0],)),
         ],
         compiler_params=pltpu.CompilerParams(vmem_limit_bytes=32 << 20),
         name="update",
@@ -203,20 +201,12 @@
 
 
 def sum_over_tp(part):
-    half = part.shape[0] // 2
     size = lax.axis_size("tp")
-    first = lax.axis_index("tp") % 2 == 0
-
-    def swap(array, bit):
-        return lax.ppermute(array, "tp", [(i, i ^ bit) for i in range(size)])
-
-    mine = jnp.where(first, part[:half], part[half:]) + swap(jnp.where(first, part[half:], part[:half]), 1)
-    bit = 2
+    bit = 1
     while bit < size:
-        mine = mine + swap(mine, bit)
+        part = part + lax.ppermute(part, "tp", [(i, i ^ bit) for i in range(size)])
         bit *= 2
-    other = swap(mine, 1)
-    return jnp.concatenate([jnp.where(first, mine, other), jnp.where(first, other, mine)])
+    return part
 
 
 def local(

time: 144 us -> 144 us (level)
  waiting for transfers between devices: 89.6 us -> 91.6 us
  starting transfers between devices: 34.7 us -> 32.9 us
    all_to_all x2, waiting for transfers between devices: 80.2 us -> 82.5 us  [exchange(): return lax.all_to_all(chunks, 'inst', 0, 0)]
    ppermute x4 -> x3, starting transfers between devices: 9.87 us -> 8.1 us  [sum_over_tp(): part = part + lax.ppermute(part, 'tp', [(i, i ^ bit) for i in range(size)])]
    ppermute x4 -> x3, waiting for transfers between devices: 9.37 us -> 9.19 us  [sum_over_tp(): part = part + lax.ppermute(part, 'tp', [(i, i ^ bit) for i in range(size)])]
  transfers between devices with their start and end apart: 6 -> 5, of which waited for: 6 -> 5; matrix products, arithmetic and copies ran while one was open for 6% -> 6% of each run, Pallas kernels for 0% -> 0%
where the time goes in v6:
time: 144 us; the launch traced here: 143 us
  waiting for transfers between devices  91.6 us (64%)
  starting transfers between devices  32.9 us (23%)
  Pallas kernels  7.06 us (5%)
  local copies, waits for them, and re-layouts  5.38 us (4%)
  other arithmetic  3.12 us (2%)
  matrix products  2.06 us (1%)
    all_to_all x2, waiting for transfers between devices, exchange(): return lax.all_to_all(chunks, 'inst', 0, 0)  82.5 us
    all_to_all x2, starting transfers between devices, exchange(): return lax.all_to_all(chunks, 'inst', 0, 0)  24.8 us
    ppermute x3, waiting for transfers between devices, sum_over_tp(): part = part + lax.ppermute(part, 'tp', [(i, i ^ bit) for i in range(size)])  9.19 us
    ppermute x3, starting transfers between devices, sum_over_tp(): part = part + lax.ppermute(part, 'tp', [(i, i ^ bit) for i in range(size)])  8.1 us
    pallas_call x1, Pallas kernels, update(): pl.pallas_call(update_kernel, out_shape=(jax.ShapeDtypeStruct(gate.shape,...  3.04 us
  transfers between devices with their start and end apart: 5, of which 5 were waited for; matrix products, arithmetic and copies ran while one was open for 6% of the time, Pallas kernels for 0%

profile of v6, /device:TPU:6, one launch (start us, length us, event | category | flops | bytes accessed | tf_op | source)
XLA Modules:
  0.0 143.2 jit_solution(14186139718680291715)
XLA Ops:
  0.7 2.8 %pack.1 = (f32[64,10,4,128]{3,2,1,0:T(4,128)}, s32[16]{0:T(128)}, s32[16]{0:T(128)}, f32[2,16,1024]{2,1,0:T(8,128)}) custom-call(s32[1]{0:T(128)} %bitcast.me_ref, s32[16]{0:T(128)} %anchor_hbm.1, s32[16]{0:T(128)} %target_hbm.1, f32[16,16,1024]{2,1,0:T(8,128)} %state_ref.1, f32[3,16,1024]{2,1,0:T(8,128)} %bitcast.24, f32[4,1024]{1,0:T(4,128)} %taps_hbm.1), custom_call_target="tpu_custom_call" | custom-call | tf_op jit(solution)/shard_map/pack/pallas_call | solution.py:91
  3.4 18.9 %all-to-all-start = ((f32[64,10,4,128]{3,2,1,0:T(4,128)}), f32[64,10,4,128]{3,2,1,0:T(4,128)S(1)}, u32[]{:S(2)}, u32[]{:S(2)}) async-start(f32[64,10,4,128]{3,2,1,0:T(4,128)} %get-tuple-element.8), calls=%async_computation | async-start | bytes 2621440 | tf_op jit(solution)/shard_map/all_to_all | solution.py:200
  22.4 0.1 copy.22
  22.5 66.4 %all-to-all-done.held_ref = f32[64,10,4,128]{3,2,1,0:T(4,128)S(1)} async-done(((f32[64,10,4,128]{3,2,1,0:T(4,128)}), f32[64,10,4,128]{3,2,1,0:T(4,128)S(1)}, u32[]{:S(2)}, u32[]{:S(2)}) %all-to-all-start) | async-done | bytes 1310752 | tf_op jit(solution)/shard_map/all_to_all | solution.py:200
  88.9 1.3 roll.1
  90.1 0.9 copy-done.2
  91.0 6.0 %all-to-all-start.1 = ((f32[64,6,4,128]{3,2,1,0:T(4,128)}), f32[64,6,4,128]{3,2,1,0:T(4,128)S(1)}, u32[]{:S(2)}, u32[]{:S(2)}) async-start(f32[64,6,4,128]{3,2,1,0:T(4,128)} %copy-done.2), calls=%async_computation.1 | async-start | bytes 1572864 | tf_op jit(solution)/shard_map/all_to_all | solution.py:200
  97.0 0.6 compare_and_fusion.1
  97.6 0.7 gather_fusion
  98.3 0.7 compare_select_fusion.1
  99.0 0.6 multiply_reduce_fusion
  99.6 0.7 compare_and_fusion
  100.3 0.8 slice.36
  101.2 1.5 %reshape.50 = f32[64,2,1024]{2,1,0:T(2,128)S(1)} reshape(f32[64,4,4,128]{3,2,1,0:T(4,128)} %slice.36) | data formatting | bytes 1048576 | tf_op jit(solution)/shard_map/reshape | solution.py:237
  102.6 0.7 gather_fusion.1
  103.4 0.2 select_select_fusion
  103.6 0.1 fusion.6
  103.7 0.1 multiply_convert_fusion.1
  103.8 0.4 fusion.5
  104.2 2.1 %collective-permute-start = (f32[32,544]{1,0:T(8,128)S(1)}, f32[32,544]{1,0:T(8,128)S(1)}, u32[]{:S(2)}, u32[]{:S(2)}) collective-permute-start(f32[32,544]{1,0:T(8,128)S(1)} %fusion.5), channel_id=1, source_target_pairs={{0,1},{1,0},{2,3},{3,2},{4,5},{5,4},{6,7},{7,6},{8,9},{9,8},{10,11... | collective-permute-start | bytes 208904 | tf_op jit(solution)/shard_map/ppermute | solution.py:207
  106.3 1.2 collective-permute-done
  107.5 2.7 %collective-permute-start.1 = (f32[32,544]{1,0:T(8,128)S(1)}, f32[32,544]{1,0:T(8,128)S(1)}, u32[]{:S(2)}, u32[]{:S(2)}) collective-permute-start(f32[32,544]{1,0:T(8,128)S(1)} %add.71), channel_id=1, source_target_pairs={{0,2},{1,3},{2,0},{3,1},{4,6},{5,7},{6,4},{7,5},{8,10},{9,11},{10,... | collective-permute-start | bytes 208904 | tf_op jit(solution)/shard_map/ppermute | solution.py:207
  110.4 3.6 %collective-permute-done.1 = f32[32,544]{1,0:T(8,128)S(1)} collective-permute-done((f32[32,544]{1,0:T(8,128)S(1)}, f32[32,544]{1,0:T(8,128)S(1)}, u32[]{:S(2)}, u32[]{:S(2)}) %collective-permute-start.1) | collective-permute-done | bytes 69664 | tf_op jit(solution)/shard_map/ppermute | solution.py:207
  114.0 3.3 %collective-permute-start.2 = (f32[32,544]{1,0:T(8,128)S(1)}, f32[32,544]{1,0:T(8,128)S(1)}, u32[]{:S(2)}, u32[]{:S(2)}) collective-permute-start(f32[32,544]{1,0:T(8,128)S(1)} %add.72), channel_id=1, source_target_pairs={{0,4},{1,5},{2,6},{3,7},{4,0},{5,1},{6,2},{7,3},{8,12},{9,13},{10,... | collective-permute-start | bytes 208904 | tf_op jit(solution)/shard_map/ppermute | solution.py:207
  117.3 0.1 fusion.skip_ref
  117.4 4.4 %collective-permute-done.2 = f32[32,544]{1,0:T(8,128)S(1)} collective-permute-done((f32[32,544]{1,0:T(8,128)S(1)}, f32[32,544]{1,0:T(8,128)S(1)}, u32[]{:S(2)}, u32[]{:S(2)}) %collective-permute-start.2) | collective-permute-done | bytes 69664 | tf_op jit(solution)/shard_map/ppermute | solution.py:207
  121.8 0.1 copy.25
  121.9 0.1 multiply_reduce_fusion.1
  122.0 0.4 copy-done.6
  122.5 1.6 %compare_select_fusion = f32[32,1024]{1,0:T(8,128)S(1)} fusion(bf16[512,1024]{1,0:T(8,128)(2,1)} %param.21, f32[1024]{0:T(1024)S(1)} %copy-done.13, f32[32,544]{1,0:T(8,128)} %copy-done.6, f32[512]{0:T(512)S(1)} %copy-done.14, f32[32]{0:T(128)S(1)} %add_rsqrt_fusion), kind=kOutput, calls=%fused_computation.3 | convolution fusion | flops 33832960 | bytes 1251456 | tf_op jit(solution)/shard_map/dot_general | solution.py:253
  124.1 16.1 %all-to-all-done.1.moved_ref = f32[64,6,4,128]{3,2,1,0:T(4,128)S(1)} async-done(((f32[64,6,4,128]{3,2,1,0:T(4,128)}), f32[64,6,4,128]{3,2,1,0:T(4,128)S(1)}, u32[]{:S(2)}, u32[]{:S(2)}) %all-to-all-start.1) | async-done | bytes 786464 | tf_op jit(solution)/shard_map/all_to_all | solution.py:200
  140.2 3.0 %update.1 = (bf16[16,2,1024]{2,1,0:T(2,128)(2,1)}, f32[16,16,1024]{2,1,0:T(8,128)}) custom-call(s32[16]{0:T(128)S(1)} %copy-done.4, f32[2,32,16]{2,1,0:T(8,128)S(1)} %bitcast.22, f32[64,6,4,128]{3,2,1,0:T(4,128)S(1)} %all-to-all-done.1.moved_ref, f32[16,16,1024]{2,1,0:T(8,128)S(1)} %copy-done.1, f32[2,16,1024]{2,1,0:T(8,128)S(1)} %bitcast.21, ...), custom_call_target="tpu_custom_call" | custom-call | tf_op jit(solution)/shard_map/update/pallas_call | solution.py:179
  (47 shorter events, 0.2 us)
Async XLA Ops:
  0.6 103.1 %copy-start = (bf16[1024,544]{0,1:T(8,128)(2,1)S(1)}, bf16[1024,544]{0,1:T(8,128)(2,1)}, u32[]{:S(2)}) copy-start(bf16[1024,544]{0,1:T(8,128)(2,1)} %param.20) | copy-start | bytes 3342340
  3.4 18.9 %copy-start.11 = (f32[4,1024]{1,0:T(4,128)S(1)}, f32[4,1024]{1,0:T(4,128)}, u32[]{:S(2)}) copy-start(f32[4,1024]{1,0:T(4,128)} %taps_hbm.1) | copy-start | bytes 49156
  3.4 18.9 %copy-start.9 = (f32[2,16,1024]{2,1,0:T(8,128)S(1)}, f32[2,16,1024]{2,1,0:T(8,128)}, u32[]{:S(2)}) copy-start(f32[2,16,1024]{2,1,0:T(8,128)} %get-tuple-element.7) | copy-start | bytes 393220
  3.4 85.4 %copy-start.5 = (s32[16]{0:T(128)S(1)}, s32[16]{0:T(128)}, u32[]{:S(2)}) copy-start(s32[16]{0:T(128)} %get-tuple-element.9.offset_ref) | copy-start | bytes 196
  3.4 85.4 %all-to-all-start = ((f32[64,10,4,128]{3,2,1,0:T(4,128)}), f32[64,10,4,128]{3,2,1,0:T(4,128)S(1)}, u32[]{:S(2)}, u32[]{:S(2)}) async-start(f32[64,10,4,128]{3,2,1,0:T(4,128)} %get-tuple-element.8), calls=%async_computation | async-start | bytes 2621440 | tf_op jit(solution)/shard_map/all_to_all | solution.py:200
  90.1 0.9 copy-start.2
  91.0 6.0 %copy-start.15 = (s32[16]{0:T(128)S(1)}, s32[16]{0:T(128)}, u32[]{:S(2)}) copy-start(s32[16]{0:T(128)} %anchor_hbm.1) | copy-start | bytes 196
  91.0 8.0 %copy-start.7 = (bf16[16,2,1024]{2,1,0:T(2,128)(2,1)S(1)}, bf16[16,2,1024]{2,1,0:T(2,128)(2,1)}, u32[]{:S(2)}) copy-start(bf16[16,2,1024]{2,1,0:T(2,128)(2,1)} %param.17) | copy-start | bytes 196612
  91.0 49.2 %all-to-all-start.1 = ((f32[64,6,4,128]{3,2,1,0:T(4,128)}), f32[64,6,4,128]{3,2,1,0:T(4,128)S(1)}, u32[]{:S(2)}, u32[]{:S(2)}) async-start(f32[64,6,4,128]{3,2,1,0:T(4,128)} %copy-done.2), calls=%async_computation.1 | async-start | bytes 1572864 | tf_op jit(solution)/shard_map/all_to_all | solution.py:200
  100.3 3.0 %copy-start.16 = (pred[16]{0:T(512)(128)(4,1)S(1)}, pred[16]{0:T(512)(128)(4,1)}, u32[]{:S(2)}) copy-start(pred[16]{0:T(512)(128)(4,1)} %get-tuple-element.12) | copy-start | bytes 52
  100.3 3.0 %copy-start.17 = (pred[16]{0:T(512)(128)(4,1)S(1)}, pred[16]{0:T(512)(128)(4,1)}, u32[]{:S(2)}) copy-start(pred[16]{0:T(512)(128)(4,1)} %get-tuple-element.16) | copy-start | bytes 52
  101.2 2.5 %copy-start.8 = (f32[16,1024]{1,0:T(8,128)S(1)}, f32[16,1024]{1,0:T(8,128)}, u32[]{:S(2)}) copy-start(f32[16,1024]{1,0:T(8,128)} %multiply_reduce_fusion) | copy-start | bytes 196612
  103.4 2.9 %copy-start.10 = (f32[16,1024]{1,0:T(8,128)S(1)}, f32[16,1024]{1,0:T(8,128)}, u32[]{:S(2)}) copy-start(f32[16,1024]{1,0:T(8,128)} %param.23) | copy-start | bytes 196612
  103.7 13.5 %copy-start.12 = (f32[1024]{0:T(1024)S(1)}, f32[1024]{0:T(1024)}, u32[]{:S(2)}) copy-start(f32[1024]{0:T(1024)} %param.24) | copy-start | bytes 12292
  104.2 18.3 %copy-start.13 = (f32[1024]{0:T(1024)S(1)}, f32[1024]{0:T(1024)}, u32[]{:S(2)}) copy-start(f32[1024]{0:T(1024)} %param.22) | copy-start | bytes 12292
  104.2 18.2 %copy-start.14 = (f32[512]{0:T(512)S(1)}, f32[512]{0:T(512)}, u32[]{:S(2)}) copy-start(f32[512]{0:T(512)} %param.25) | copy-start | bytes 6148
  104.2 3.3 %collective-permute-start = (f32[32,544]{1,0:T(8,128)S(1)}, f32[32,544]{1,0:T(8,128)S(1)}, u32[]{:S(2)}, u32[]{:S(2)}) collective-permute-start(f32[32,544]{1,0:T(8,128)S(1)} %fusion.5), channel_id=1, source_target_pairs={{0,1},{1,0},{2,3},{3,2},{4,5},{5,4},{6,7},{7,6},{8,9},{9,8},{10,11... | collective-permute-start | bytes 208904 | tf_op jit(solution)/shard_map/ppermute | solution.py:207
  107.5 6.4 %collective-permute-start.1 = (f32[32,544]{1,0:T(8,128)S(1)}, f32[32,544]{1,0:T(8,128)S(1)}, u32[]{:S(2)}, u32[]{:S(2)}) collective-permute-start(f32[32,544]{1,0:T(8,128)S(1)} %add.71), channel_id=1, source_target_pairs={{0,2},{1,3},{2,0},{3,1},{4,6},{5,7},{6,4},{7,5},{8,10},{9,11},{10,... | collective-permute-start | bytes 208904 | tf_op jit(solution)/shard_map/ppermute | solution.py:207
  110.3 29.9 %copy-start.1 = (f32[16,16,1024]{2,1,0:T(8,128)S(1)}, f32[16,16,1024]{2,1,0:T(8,128)}, u32[]{:S(2)}) copy-start(f32[16,16,1024]{2,1,0:T(8,128)} %state_ref.1) | copy-start | bytes 3145732
  110.3 29.9 %copy-start.3 = (bf16[16,2,1024]{2,1,0:T(2,128)(2,1)S(1)}, bf16[16,2,1024]{2,1,0:T(2,128)(2,1)}, u32[]{:S(2)}) copy-start(bf16[16,2,1024]{2,1,0:T(2,128)(2,1)} %gate_ref.1) | copy-start | bytes 196612
  110.3 29.8 %copy-start.4 = (s32[16]{0:T(128)S(1)}, s32[16]{0:T(128)}, u32[]{:S(2)}) copy-start(s32[16]{0:T(128)} %get-tuple-element.6.row_hbm) | copy-start | bytes 196
  114.0 7.8 %collective-permute-start.2 = (f32[32,544]{1,0:T(8,128)S(1)}, f32[32,544]{1,0:T(8,128)S(1)}, u32[]{:S(2)}, u32[]{:S(2)}) collective-permute-start(f32[32,544]{1,0:T(8,128)S(1)} %add.72), channel_id=1, source_target_pairs={{0,4},{1,5},{2,6},{3,7},{4,0},{5,1},{6,2},{7,3},{8,12},{9,13},{10,... | collective-permute-start | bytes 208904 | tf_op jit(solution)/shard_map/ppermute | solution.py:207
  121.8 0.6 copy-start.6

commit v7 on v6

--- a/solution.py
+++ b/solution.py
@@ -25,8 +25,8 @@
 
 def pack_kernel(
     me_ref, anchor_hbm, target_hbm, state_hbm, conv_hbm, taps_hbm,
-    leaving_ref, offset_ref, row_ref, sums_ref,
-    anchor_ref, target_ref, state_ref, conv_ref, taps_ref, slot_of, rank_of, source, sems,
+    leaving_hbm, offset_ref, row_ref, sums_ref,
+    leaving_ref, anchor_ref, target_ref, state_ref, conv_ref, taps_ref, slot_of, rank_of, source, sems, out_sems,
 ):
     copies = begin(
         [
@@ -69,21 +69,35 @@
     taps = [taps_ref[i : i + 1, :] for i in range(3)]
     sums_ref[0] = old[0] * taps[0] + old[1] * taps[1] + old[2] * taps[2]
     sums_ref[1] = old[1] * taps[0] + old[2] * taps[1]
-    copies[4].wait()
+    leaving = []
+
+    def send(low, high):
+        part = slice(low, high)
+        leaving.append(
+            pltpu.make_async_copy(leaving_ref.at[:, part], leaving_hbm.at[:, part], out_sems.at[len(leaving)])
+        )
+        leaving[-1].start()
+
     for k in range(GROUPS):
-        slot = source[k]
-        for t in range(16):
-            tile = 16 * k + t
-            rows, lanes = 8 * (t // 8), 128 * (t % 8)
-            block = state_ref[slot, rows : rows + 8, lanes : lanes + 128]
-            for h in range(2):
-                leaving_ref[tile % peers, 2 * (tile // peers) + h] = block[4 * h : 4 * h + 4]
         receiver = (me + offset_ref[k]) % peers
         for i in range(2):
-            sums = sums_ref[i, pl.ds(slot, 1), :]
+            sums = sums_ref[i, pl.ds(source[k], 1), :]
             for c in range(8):
                 r = 8 * i + c
                 leaving_ref[receiver, 2 * TILES + r // 4, r % 4 : r % 4 + 1, :] = sums[:, 128 * c : 128 * c + 128]
+    send(2 * TILES, 2 * TILES + CONV)
+    copies[4].wait()
+    for u in range(TILES):
+        for k in range(4 * u, 4 * u + 4):
+            slot = source[k]
+            for t in range(16):
+                rows, lanes = 8 * (t // 8), 128 * (t % 8)
+                block = state_ref[slot, rows : rows + 8, lanes : lanes + 128]
+                for h in range(2):
+                    leaving_ref[(16 * k + t) % peers, 2 * u + h] = block[4 * h : 4 * h + 4]
+        send(2 * u, 2 * u + 2)
+    for copy in leaving:
+        copy.wait()
 
 
 def pack(me, anchor, target, ssm_state, conv_state, conv_weight, peers):
@@ -97,8 +111,9 @@
             jax.ShapeDtypeStruct((2, slots, width), jnp.float32),
         ),
         in_specs=[SMEM] + [ANY] * 5,
-        out_specs=(VMEM, SMEM, SMEM, VMEM),
+        out_specs=(ANY, SMEM, SMEM, VMEM),
         scratch_shapes=[
+            pltpu.VMEM((peers, 2 * TILES + CONV, 4, 128), jnp.float32),
             pltpu.SMEM(anchor.shape, jnp.int32),
             pltpu.SMEM(target.shape, jnp.int32),
             pltpu.VMEM(ssm_state.shape, jnp.float32),
@@ -108,8 +123,9 @@
             pltpu.SMEM((peers,), jnp.int32),
             pltpu.SMEM((16,), jnp.int32),
             pltpu.SemaphoreType.DMA((5,)),
+            pltpu.SemaphoreType.DMA((TILES + 1,)),
         ],
-        compiler_params=pltpu.CompilerParams(vmem_limit_bytes=56 << 20),
+        compiler_params=pltpu.CompilerParams(vmem_limit_bytes=54 << 20),
         name="pack",
     )(me, anchor, target, ssm_state, conv_state, conv_weight)
 

time: 144 us -> 144 us (level)
  no operation moved by 1% of the time
where the time goes in v7:
time: 144 us
  waiting for transfers between devices  91.6 us (64%)
  starting transfers between devices  32.9 us (23%)
  Pallas kernels  7.51 us (5%)
  local copies, waits for them, and re-layouts  5.38 us (4%)
  other arithmetic  3.12 us (2%)
  matrix products  2.06 us (1%)
    all_to_all x2, waiting for transfers between devices, exchange(): return lax.all_to_all(chunks, 'inst', 0, 0)  82.5 us
    all_to_all x2, starting transfers between devices, exchange(): return lax.all_to_all(chunks, 'inst', 0, 0)  24.8 us
    ppermute x3, waiting for transfers between devices, sum_over_tp(): part = part + lax.ppermute(part, 'tp', [(i, i ^ bit) for i in range(size)])  9.19 us
    ppermute x3, starting transfers between devices, sum_over_tp(): part = part + lax.ppermute(part, 'tp', [(i, i ^ bit) for i in range(size)])  8.1 us
    pallas_call x1, Pallas kernels, pack(): pl.pallas_call(pack_kernel, out_shape=(jax.ShapeDtypeStruct((peers, 2 * T...  3.2 us
    pallas_call x1, Pallas kernels, update(): pl.pallas_call(update_kernel, out_shape=(jax.ShapeDtypeStruct(gate.shape,...  3.04 us
  transfers between devices with their start and end apart: 5, of which 5 were waited for; matrix products, arithmetic and copies ran while one was open for 6% of the time, Pallas kernels for 0%

profile of v7, /device:TPU:6, one launch (start us, length us, event | category | flops | bytes accessed | tf_op | source)
XLA Modules:
  0.0 143.7 jit_solution(2088964826545598085)
XLA Ops:
  0.7 3.2 %pack.1 = (f32[64,10,4,128]{3,2,1,0:T(4,128)}, s32[16]{0:T(128)}, s32[16]{0:T(128)}, f32[2,16,1024]{2,1,0:T(8,128)}) custom-call(s32[1]{0:T(128)} %bitcast.me_ref, s32[16]{0:T(128)} %anchor_hbm.1, s32[16]{0:T(128)} %target_hbm.1, f32[16,16,1024]{2,1,0:T(8,128)} %state_ref.1, f32[3,16,1024]{2,1,0:T(8,128)} %bitcast.24, f32[4,1024]{1,0:T(4,128)} %taps_hbm.1), custom_call_target="tpu_custom_call" | custom-call | tf_op jit(solution)/shard_map/pack/pallas_call | solution.py:105
  3.9 18.9 %all-to-all-start = ((f32[64,10,4,128]{3,2,1,0:T(4,128)}), f32[64,10,4,128]{3,2,1,0:T(4,128)S(1)}, u32[]{:S(2)}, u32[]{:S(2)}) async-start(f32[64,10,4,128]{3,2,1,0:T(4,128)} %get-tuple-element.8), calls=%async_computation | async-start | bytes 2621440 | tf_op jit(solution)/shard_map/all_to_all | solution.py:216
  22.8 0.1 copy.22
  22.9 66.4 %all-to-all-done.held_ref = f32[64,10,4,128]{3,2,1,0:T(4,128)S(1)} async-done(((f32[64,10,4,128]{3,2,1,0:T(4,128)}), f32[64,10,4,128]{3,2,1,0:T(4,128)S(1)}, u32[]{:S(2)}, u32[]{:S(2)}) %all-to-all-start) | async-done | bytes 1310752 | tf_op jit(solution)/shard_map/all_to_all | solution.py:216
  89.3 1.3 roll.1
  90.6 0.9 copy-done.2
  91.5 6.0 %all-to-all-start.1 = ((f32[64,6,4,128]{3,2,1,0:T(4,128)}), f32[64,6,4,128]{3,2,1,0:T(4,128)S(1)}, u32[]{:S(2)}, u32[]{:S(2)}) async-start(f32[64,6,4,128]{3,2,1,0:T(4,128)} %copy-done.2), calls=%async_computation.1 | async-start | bytes 1572864 | tf_op jit(solution)/shard_map/all_to_all | solution.py:216
  97.5 0.6 compare_and_fusion.1
  98.0 0.7 gather_fusion
  98.7 0.7 compare_select_fusion.1
  99.4 0.6 multiply_reduce_fusion
  100.1 0.7 compare_and_fusion
  100.8 0.8 slice.36
  101.6 1.5 %reshape.50 = f32[64,2,1024]{2,1,0:T(2,128)S(1)} reshape(f32[64,4,4,128]{3,2,1,0:T(4,128)} %slice.36) | data formatting | bytes 1048576 | tf_op jit(solution)/shard_map/reshape | solution.py:253
  103.1 0.7 gather_fusion.1
  103.8 0.2 select_select_fusion
  104.0 0.1 fusion.6
  104.1 0.1 multiply_convert_fusion.1
  104.2 0.4 fusion.5
  104.7 2.1 %collective-permute-start = (f32[32,544]{1,0:T(8,128)S(1)}, f32[32,544]{1,0:T(8,128)S(1)}, u32[]{:S(2)}, u32[]{:S(2)}) collective-permute-start(f32[32,544]{1,0:T(8,128)S(1)} %fusion.5), channel_id=1, source_target_pairs={{0,1},{1,0},{2,3},{3,2},{4,5},{5,4},{6,7},{7,6},{8,9},{9,8},{10,11... | collective-permute-start | bytes 208904 | tf_op jit(solution)/shard_map/ppermute | solution.py:223
  106.8 1.2 collective-permute-done
  108.0 2.7 %collective-permute-start.1 = (f32[32,544]{1,0:T(8,128)S(1)}, f32[32,544]{1,0:T(8,128)S(1)}, u32[]{:S(2)}, u32[]{:S(2)}) collective-permute-start(f32[32,544]{1,0:T(8,128)S(1)} %add.71), channel_id=1, source_target_pairs={{0,2},{1,3},{2,0},{3,1},{4,6},{5,7},{6,4},{7,5},{8,10},{9,11},{10,... | collective-permute-start | bytes 208904 | tf_op jit(solution)/shard_map/ppermute | solution.py:223
  110.8 3.6 %collective-permute-done.1 = f32[32,544]{1,0:T(8,128)S(1)} collective-permute-done((f32[32,544]{1,0:T(8,128)S(1)}, f32[32,544]{1,0:T(8,128)S(1)}, u32[]{:S(2)}, u32[]{:S(2)}) %collective-permute-start.1) | collective-permute-done | bytes 69664 | tf_op jit(solution)/shard_map/ppermute | solution.py:223
  114.4 3.3 %collective-permute-start.2 = (f32[32,544]{1,0:T(8,128)S(1)}, f32[32,544]{1,0:T(8,128)S(1)}, u32[]{:S(2)}, u32[]{:S(2)}) collective-permute-start(f32[32,544]{1,0:T(8,128)S(1)} %add.72), channel_id=1, source_target_pairs={{0,4},{1,5},{2,6},{3,7},{4,0},{5,1},{6,2},{7,3},{8,12},{9,13},{10,... | collective-permute-start | bytes 208904 | tf_op jit(solution)/shard_map/ppermute | solution.py:223
  117.7 0.1 fusion.skip_ref
  117.8 4.4 %collective-permute-done.2 = f32[32,544]{1,0:T(8,128)S(1)} collective-permute-done((f32[32,544]{1,0:T(8,128)S(1)}, f32[32,544]{1,0:T(8,128)S(1)}, u32[]{:S(2)}, u32[]{:S(2)}) %collective-permute-start.2) | collective-permute-done | bytes 69664 | tf_op jit(solution)/shard_map/ppermute | solution.py:223
  122.3 0.1 copy.25
  122.4 0.1 multiply_reduce_fusion.1
  122.5 0.4 copy-done.6
  122.9 1.6 %compare_select_fusion = f32[32,1024]{1,0:T(8,128)S(1)} fusion(bf16[512,1024]{1,0:T(8,128)(2,1)} %param.21, f32[1024]{0:T(1024)S(1)} %copy-done.13, f32[32,544]{1,0:T(8,128)} %copy-done.6, f32[512]{0:T(512)S(1)} %copy-done.14, f32[32]{0:T(128)S(1)} %add_rsqrt_fusion), kind=kOutput, calls=%fused_computation.3 | convolution fusion | flops 33832960 | bytes 1251456 | tf_op jit(solution)/shard_map/dot_general | solution.py:269
  124.5 16.1 %all-to-all-done.1.moved_ref = f32[64,6,4,128]{3,2,1,0:T(4,128)S(1)} async-done(((f32[64,6,4,128]{3,2,1,0:T(4,128)}), f32[64,6,4,128]{3,2,1,0:T(4,128)S(1)}, u32[]{:S(2)}, u32[]{:S(2)}) %all-to-all-start.1) | async-done | bytes 786464 | tf_op jit(solution)/shard_map/all_to_all | solution.py:216
  140.6 3.0 %update.1 = (bf16[16,2,1024]{2,1,0:T(2,128)(2,1)}, f32[16,16,1024]{2,1,0:T(8,128)}) custom-call(s32[16]{0:T(128)S(1)} %copy-done.4, f32[2,32,16]{2,1,0:T(8,128)S(1)} %bitcast.22, f32[64,6,4,128]{3,2,1,0:T(4,128)S(1)} %all-to-all-done.1.moved_ref, f32[16,16,1024]{2,1,0:T(8,128)S(1)} %copy-done.1, f32[2,16,1024]{2,1,0:T(8,128)S(1)} %bitcast.21, ...), custom_call_target="tpu_custom_call" | custom-call | tf_op jit(solution)/shard_map/update/pallas_call | solution.py:195
  (47 shorter events, 0.2 us)
Async XLA Ops:
  0.6 103.6 %copy-start = (bf16[1024,544]{0,1:T(8,128)(2,1)S(1)}, bf16[1024,544]{0,1:T(8,128)(2,1)}, u32[]{:S(2)}) copy-start(bf16[1024,544]{0,1:T(8,128)(2,1)} %param.20) | copy-start | bytes 3342340
  3.9 18.9 %copy-start.11 = (f32[4,1024]{1,0:T(4,128)S(1)}, f32[4,1024]{1,0:T(4,128)}, u32[]{:S(2)}) copy-start(f32[4,1024]{1,0:T(4,128)} %taps_hbm.1) | copy-start | bytes 49156
  3.9 18.9 %copy-start.9 = (f32[2,16,1024]{2,1,0:T(8,128)S(1)}, f32[2,16,1024]{2,1,0:T(8,128)}, u32[]{:S(2)}) copy-start(f32[2,16,1024]{2,1,0:T(8,128)} %get-tuple-element.7) | copy-start | bytes 393220
  3.9 85.4 %copy-start.5 = (s32[16]{0:T(128)S(1)}, s32[16]{0:T(128)}, u32[]{:S(2)}) copy-start(s32[16]{0:T(128)} %get-tuple-element.9.offset_ref) | copy-start | bytes 196
  3.9 85.4 %all-to-all-start = ((f32[64,10,4,128]{3,2,1,0:T(4,128)}), f32[64,10,4,128]{3,2,1,0:T(4,128)S(1)}, u32[]{:S(2)}, u32[]{:S(2)}) async-start(f32[64,10,4,128]{3,2,1,0:T(4,128)} %get-tuple-element.8), calls=%async_computation | async-start | bytes 2621440 | tf_op jit(solution)/shard_map/all_to_all | solution.py:216
  90.6 0.9 copy-start.2
  91.5 6.0 %copy-start.15 = (s32[16]{0:T(128)S(1)}, s32[16]{0:T(128)}, u32[]{:S(2)}) copy-start(s32[16]{0:T(128)} %anchor_hbm.1) | copy-start | bytes 196
  91.5 8.0 %copy-start.7 = (bf16[16,2,1024]{2,1,0:T(2,128)(2,1)S(1)}, bf16[16,2,1024]{2,1,0:T(2,128)(2,1)}, u32[]{:S(2)}) copy-start(bf16[16,2,1024]{2,1,0:T(2,128)(2,1)} %param.17) | copy-start | bytes 196612
  91.5 49.2 %all-to-all-start.1 = ((f32[64,6,4,128]{3,2,1,0:T(4,128)}), f32[64,6,4,128]{3,2,1,0:T(4,128)S(1)}, u32[]{:S(2)}, u32[]{:S(2)}) async-start(f32[64,6,4,128]{3,2,1,0:T(4,128)} %copy-done.2), calls=%async_computation.1 | async-start | bytes 1572864 | tf_op jit(solution)/shard_map/all_to_all | solution.py:216
  100.8 3.0 %copy-start.16 = (pred[16]{0:T(512)(128)(4,1)S(1)}, pred[16]{0:T(512)(128)(4,1)}, u32[]{:S(2)}) copy-start(pred[16]{0:T(512)(128)(4,1)} %get-tuple-element.12) | copy-start | bytes 52
  100.8 3.0 %copy-start.17 = (pred[16]{0:T(512)(128)(4,1)S(1)}, pred[16]{0:T(512)(128)(4,1)}, u32[]{:S(2)}) copy-start(pred[16]{0:T(512)(128)(4,1)} %get-tuple-element.16) | copy-start | bytes 52
  101.6 2.5 %copy-start.8 = (f32[16,1024]{1,0:T(8,128)S(1)}, f32[16,1024]{1,0:T(8,128)}, u32[]{:S(2)}) copy-start(f32[16,1024]{1,0:T(8,128)} %multiply_reduce_fusion) | copy-start | bytes 196612
  103.8 2.9 %copy-start.10 = (f32[16,1024]{1,0:T(8,128)S(1)}, f32[16,1024]{1,0:T(8,128)}, u32[]{:S(2)}) copy-start(f32[16,1024]{1,0:T(8,128)} %param.23) | copy-start | bytes 196612
  104.2 13.5 %copy-start.12 = (f32[1024]{0:T(1024)S(1)}, f32[1024]{0:T(1024)}, u32[]{:S(2)}) copy-start(f32[1024]{0:T(1024)} %param.24) | copy-start | bytes 12292
  104.6 18.3 %copy-start.13 = (f32[1024]{0:T(1024)S(1)}, f32[1024]{0:T(1024)}, u32[]{:S(2)}) copy-start(f32[1024]{0:T(1024)} %param.22) | copy-start | bytes 12292
  104.7 18.2 %copy-start.14 = (f32[512]{0:T(512)S(1)}, f32[512]{0:T(512)}, u32[]{:S(2)}) copy-start(f32[512]{0:T(512)} %param.25) | copy-start | bytes 6148
  104.7 3.3 %collective-permute-start = (f32[32,544]{1,0:T(8,128)S(1)}, f32[32,544]{1,0:T(8,128)S(1)}, u32[]{:S(2)}, u32[]{:S(2)}) collective-permute-start(f32[32,544]{1,0:T(8,128)S(1)} %fusion.5), channel_id=1, source_target_pairs={{0,1},{1,0},{2,3},{3,2},{4,5},{5,4},{6,7},{7,6},{8,9},{9,8},{10,11... | collective-permute-start | bytes 208904 | tf_op jit(solution)/shard_map/ppermute | solution.py:223
  108.0 6.4 %collective-permute-start.1 = (f32[32,544]{1,0:T(8,128)S(1)}, f32[32,544]{1,0:T(8,128)S(1)}, u32[]{:S(2)}, u32[]{:S(2)}) collective-permute-start(f32[32,544]{1,0:T(8,128)S(1)} %add.71), channel_id=1, source_target_pairs={{0,2},{1,3},{2,0},{3,1},{4,6},{5,7},{6,4},{7,5},{8,10},{9,11},{10,... | collective-permute-start | bytes 208904 | tf_op jit(solution)/shard_map/ppermute | solution.py:223
  110.8 29.9 %copy-start.1 = (f32[16,16,1024]{2,1,0:T(8,128)S(1)}, f32[16,16,1024]{2,1,0:T(8,128)}, u32[]{:S(2)}) copy-start(f32[16,16,1024]{2,1,0:T(8,128)} %state_ref.1) | copy-start | bytes 3145732
  110.8 29.9 %copy-start.3 = (bf16[16,2,1024]{2,1,0:T(2,128)(2,1)S(1)}, bf16[16,2,1024]{2,1,0:T(2,128)(2,1)}, u32[]{:S(2)}) copy-start(bf16[16,2,1024]{2,1,0:T(2,128)(2,1)} %gate_ref.1) | copy-start | bytes 196612
  110.8 29.8 %copy-start.4 = (s32[16]{0:T(128)S(1)}, s32[16]{0:T(128)}, u32[]{:S(2)}) copy-start(s32[16]{0:T(128)} %get-tuple-element.6.row_hbm) | copy-start | bytes 196
  114.4 7.8 %collective-permute-start.2 = (f32[32,544]{1,0:T(8,128)S(1)}, f32[32,544]{1,0:T(8,128)S(1)}, u32[]{:S(2)}, u32[]{:S(2)}) collective-permute-start(f32[32,544]{1,0:T(8,128)S(1)} %add.72), channel_id=1, source_target_pairs={{0,4},{1,5},{2,6},{3,7},{4,0},{5,1},{6,2},{7,3},{8,12},{9,13},{10,... | collective-permute-start | bytes 208904 | tf_op jit(solution)/shard_map/ppermute | solution.py:223
  122.3 0.6 copy-start.6

commit v8 on v6

--- a/solution.py
+++ b/solution.py
@@ -142,13 +142,16 @@
 
 def update_kernel(
     row_hbm, rest_ref, moved_ref, state_ref, step_ref, x_ref, skip_ref, decay_ref, gate_ref,
-    mixed_ref, out_hbm,
-    row_ref, out_ref, y_ref, row_sem, out_sems,
+    mixed_hbm, out_hbm,
+    row_ref, out_ref, y_ref, gated_ref, mixed_ref, row_sem, out_sems,
 ):
-    for copy in begin([(row_hbm, row_ref)], row_sem):
-        copy.wait()
+    arriving = begin([(row_hbm, row_ref)], row_sem)
     slots, state_size, width = state_ref.shape
     steps = step_ref.shape[0]
+    for s in range(slots):
+        gated_ref[s] = jax.nn.silu(gate_ref[s].astype(jnp.float32))
+    for copy in arriving:
+        copy.wait()
     copies = []
     for s in range(slots):
         r = row_ref[s]
@@ -169,8 +172,9 @@
             out_ref[s, :, cut] = state
         copies.append(pltpu.make_async_copy(out_ref.at[s], out_hbm.at[s], out_sems.at[s]))
         copies[-1].start()
-        gate = gate_ref[s].astype(jnp.float32)
-        mixed_ref[s] = ((y_ref[s] + skip_ref[s]) * jax.nn.silu(gate)).astype(mixed_ref.dtype)
+        mixed_ref[s] = ((y_ref[s] + skip_ref[s]) * gated_ref[s]).astype(mixed_ref.dtype)
+    copies.append(pltpu.make_async_copy(mixed_ref, mixed_hbm, out_sems.at[slots]))
+    copies[-1].start()
     for copy in copies:
         copy.wait()
 
@@ -183,13 +187,15 @@
             jax.ShapeDtypeStruct(state.shape, jnp.float32),
         ),
         in_specs=[ANY] + [VMEM] * 8,
-        out_specs=(VMEM, ANY),
+        out_specs=(ANY, ANY),
         scratch_shapes=[
             pltpu.SMEM(row.shape, jnp.int32),
             pltpu.VMEM(state.shape, jnp.float32),
             pltpu.VMEM(gate.shape, jnp.float32),
+            pltpu.VMEM(gate.shape, jnp.float32),
+            pltpu.VMEM(gate.shape, jnp.bfloat16),
             pltpu.SemaphoreType.DMA((1,)),
-            pltpu.SemaphoreType.DMA((state.shape[0],)),
+            pltpu.SemaphoreType.DMA((state.shape[0] + 1,)),
         ],
         compiler_params=pltpu.CompilerParams(vmem_limit_bytes=32 << 20),
         name="update",

time: 144 us -> 143 us (level)
  no operation moved by 1% of the time
where the time goes in v8:
time: 143 us
  waiting for transfers between devices  91.6 us (64%)
  starting transfers between devices  32.9 us (23%)
  Pallas kernels  6.45 us (5%)
  local copies, waits for them, and re-layouts  5.38 us (4%)
  other arithmetic  3.12 us (2%)
  matrix products  2.06 us (1%)
    all_to_all x2, waiting for transfers between devices, exchange(): return lax.all_to_all(chunks, 'inst', 0, 0)  82.5 us
    all_to_all x2, starting transfers between devices, exchange(): return lax.all_to_all(chunks, 'inst', 0, 0)  24.8 us
    ppermute x3, waiting for transfers between devices, sum_over_tp(): part = part + lax.ppermute(part, 'tp', [(i, i ^ bit) for i in range(size)])  9.19 us
    ppermute x3, starting transfers between devices, sum_over_tp(): part = part + lax.ppermute(part, 'tp', [(i, i ^ bit) for i in range(size)])  8.1 us
  transfers between devices with their start and end apart: 5, of which 5 were waited for; matrix products, arithmetic and copies ran while one was open for 6% of the time, Pallas kernels for 0%

profile of v8, /device:TPU:6, one launch (start us, length us, event | category | flops | bytes accessed | tf_op | source)
XLA Modules:
  0.0 142.6 jit_solution(2544711508973425496)
XLA Ops:
  0.7 2.8 %pack.1 = (f32[64,10,4,128]{3,2,1,0:T(4,128)}, s32[16]{0:T(128)}, s32[16]{0:T(128)}, f32[2,16,1024]{2,1,0:T(8,128)}) custom-call(s32[1]{0:T(128)} %bitcast.me_ref, s32[16]{0:T(128)} %anchor_hbm.1, s32[16]{0:T(128)} %target_hbm.1, f32[16,16,1024]{2,1,0:T(8,128)} %state_ref.1, f32[3,16,1024]{2,1,0:T(8,128)} %bitcast.24, f32[4,1024]{1,0:T(4,128)} %taps_hbm.1), custom_call_target="tpu_custom_call" | custom-call | tf_op jit(solution)/shard_map/pack/pallas_call | solution.py:91
  3.4 18.9 %all-to-all-start = ((f32[64,10,4,128]{3,2,1,0:T(4,128)}), f32[64,10,4,128]{3,2,1,0:T(4,128)S(1)}, u32[]{:S(2)}, u32[]{:S(2)}) async-start(f32[64,10,4,128]{3,2,1,0:T(4,128)} %get-tuple-element.8), calls=%async_computation | async-start | bytes 2621440 | tf_op jit(solution)/shard_map/all_to_all | solution.py:206
  22.4 0.1 copy.22
  22.5 66.4 %all-to-all-done.held_ref = f32[64,10,4,128]{3,2,1,0:T(4,128)S(1)} async-done(((f32[64,10,4,128]{3,2,1,0:T(4,128)}), f32[64,10,4,128]{3,2,1,0:T(4,128)S(1)}, u32[]{:S(2)}, u32[]{:S(2)}) %all-to-all-start) | async-done | bytes 1310752 | tf_op jit(solution)/shard_map/all_to_all | solution.py:206
  88.9 1.3 roll.1
  90.1 0.9 copy-done.2
  91.0 6.0 %all-to-all-start.1 = ((f32[64,6,4,128]{3,2,1,0:T(4,128)}), f32[64,6,4,128]{3,2,1,0:T(4,128)S(1)}, u32[]{:S(2)}, u32[]{:S(2)}) async-start(f32[64,6,4,128]{3,2,1,0:T(4,128)} %copy-done.2), calls=%async_computation.1 | async-start | bytes 1572864 | tf_op jit(solution)/shard_map/all_to_all | solution.py:206
  97.0 0.6 compare_and_fusion.1
  97.6 0.7 gather_fusion
  98.3 0.7 compare_select_fusion.1
  99.0 0.6 multiply_reduce_fusion
  99.6 0.7 compare_and_fusion
  100.3 0.8 slice.36
  101.2 1.5 %reshape.50 = f32[64,2,1024]{2,1,0:T(2,128)S(1)} reshape(f32[64,4,4,128]{3,2,1,0:T(4,128)} %slice.36) | data formatting | bytes 1048576 | tf_op jit(solution)/shard_map/reshape | solution.py:243
  102.6 0.7 gather_fusion.1
  103.4 0.2 select_select_fusion
  103.6 0.1 fusion.6
  103.7 0.1 multiply_convert_fusion.1
  103.8 0.4 fusion.5
  104.2 2.1 %collective-permute-start = (f32[32,544]{1,0:T(8,128)S(1)}, f32[32,544]{1,0:T(8,128)S(1)}, u32[]{:S(2)}, u32[]{:S(2)}) collective-permute-start(f32[32,544]{1,0:T(8,128)S(1)} %fusion.5), channel_id=1, source_target_pairs={{0,1},{1,0},{2,3},{3,2},{4,5},{5,4},{6,7},{7,6},{8,9},{9,8},{10,11... | collective-permute-start | bytes 208904 | tf_op jit(solution)/shard_map/ppermute | solution.py:213
  106.3 1.2 collective-permute-done
  107.5 2.7 %collective-permute-start.1 = (f32[32,544]{1,0:T(8,128)S(1)}, f32[32,544]{1,0:T(8,128)S(1)}, u32[]{:S(2)}, u32[]{:S(2)}) collective-permute-start(f32[32,544]{1,0:T(8,128)S(1)} %add.71), channel_id=1, source_target_pairs={{0,2},{1,3},{2,0},{3,1},{4,6},{5,7},{6,4},{7,5},{8,10},{9,11},{10,... | collective-permute-start | bytes 208904 | tf_op jit(solution)/shard_map/ppermute | solution.py:213
  110.4 3.6 %collective-permute-done.1 = f32[32,544]{1,0:T(8,128)S(1)} collective-permute-done((f32[32,544]{1,0:T(8,128)S(1)}, f32[32,544]{1,0:T(8,128)S(1)}, u32[]{:S(2)}, u32[]{:S(2)}) %collective-permute-start.1) | collective-permute-done | bytes 69664 | tf_op jit(solution)/shard_map/ppermute | solution.py:213
  114.0 3.3 %collective-permute-start.2 = (f32[32,544]{1,0:T(8,128)S(1)}, f32[32,544]{1,0:T(8,128)S(1)}, u32[]{:S(2)}, u32[]{:S(2)}) collective-permute-start(f32[32,544]{1,0:T(8,128)S(1)} %add.72), channel_id=1, source_target_pairs={{0,4},{1,5},{2,6},{3,7},{4,0},{5,1},{6,2},{7,3},{8,12},{9,13},{10,... | collective-permute-start | bytes 208904 | tf_op jit(solution)/shard_map/ppermute | solution.py:213
  117.3 0.1 fusion.skip_ref
  117.4 4.4 %collective-permute-done.2 = f32[32,544]{1,0:T(8,128)S(1)} collective-permute-done((f32[32,544]{1,0:T(8,128)S(1)}, f32[32,544]{1,0:T(8,128)S(1)}, u32[]{:S(2)}, u32[]{:S(2)}) %collective-permute-start.2) | collective-permute-done | bytes 69664 | tf_op jit(solution)/shard_map/ppermute | solution.py:213
  121.8 0.1 copy.25
  121.9 0.1 multiply_reduce_fusion.1
  122.0 0.4 copy-done.6
  122.5 1.6 %compare_select_fusion = f32[32,1024]{1,0:T(8,128)S(1)} fusion(bf16[512,1024]{1,0:T(8,128)(2,1)} %param.21, f32[1024]{0:T(1024)S(1)} %copy-done.13, f32[32,544]{1,0:T(8,128)} %copy-done.6, f32[512]{0:T(512)S(1)} %copy-done.14, f32[32]{0:T(128)S(1)} %add_rsqrt_fusion), kind=kOutput, calls=%fused_computation.3 | convolution fusion | flops 33832960 | bytes 1251456 | tf_op jit(solution)/shard_map/dot_general | solution.py:259
  124.1 16.1 %all-to-all-done.1.moved_ref = f32[64,6,4,128]{3,2,1,0:T(4,128)S(1)} async-done(((f32[64,6,4,128]{3,2,1,0:T(4,128)}), f32[64,6,4,128]{3,2,1,0:T(4,128)S(1)}, u32[]{:S(2)}, u32[]{:S(2)}) %all-to-all-start.1) | async-done | bytes 786464 | tf_op jit(solution)/shard_map/all_to_all | solution.py:206
  140.2 2.4 %update.1 = (bf16[16,2,1024]{2,1,0:T(2,128)(2,1)}, f32[16,16,1024]{2,1,0:T(8,128)}) custom-call(s32[16]{0:T(128)S(1)} %copy-done.4, f32[2,32,16]{2,1,0:T(8,128)S(1)} %bitcast.22, f32[64,6,4,128]{3,2,1,0:T(4,128)S(1)} %all-to-all-done.1.moved_ref, f32[16,16,1024]{2,1,0:T(8,128)S(1)} %copy-done.1, f32[2,16,1024]{2,1,0:T(8,128)S(1)} %bitcast.21, ...), custom_call_target="tpu_custom_call" | custom-call | tf_op jit(solution)/shard_map/update/pallas_call | solution.py:183
  (47 shorter events, 0.2 us)
Async XLA Ops:
  0.6 103.1 %copy-start = (bf16[1024,544]{0,1:T(8,128)(2,1)S(1)}, bf16[1024,544]{0,1:T(8,128)(2,1)}, u32[]{:S(2)}) copy-start(bf16[1024,544]{0,1:T(8,128)(2,1)} %param.20) | copy-start | bytes 3342340
  3.4 18.9 %copy-start.11 = (f32[4,1024]{1,0:T(4,128)S(1)}, f32[4,1024]{1,0:T(4,128)}, u32[]{:S(2)}) copy-start(f32[4,1024]{1,0:T(4,128)} %taps_hbm.1) | copy-start | bytes 49156
  3.4 18.9 %copy-start.9 = (f32[2,16,1024]{2,1,0:T(8,128)S(1)}, f32[2,16,1024]{2,1,0:T(8,128)}, u32[]{:S(2)}) copy-start(f32[2,16,1024]{2,1,0:T(8,128)} %get-tuple-element.7) | copy-start | bytes 393220
  3.4 85.4 %copy-start.5 = (s32[16]{0:T(128)S(1)}, s32[16]{0:T(128)}, u32[]{:S(2)}) copy-start(s32[16]{0:T(128)} %get-tuple-element.9.offset_ref) | copy-start | bytes 196
  3.4 85.4 %all-to-all-start = ((f32[64,10,4,128]{3,2,1,0:T(4,128)}), f32[64,10,4,128]{3,2,1,0:T(4,128)S(1)}, u32[]{:S(2)}, u32[]{:S(2)}) async-start(f32[64,10,4,128]{3,2,1,0:T(4,128)} %get-tuple-element.8), calls=%async_computation | async-start | bytes 2621440 | tf_op jit(solution)/shard_map/all_to_all | solution.py:206
  90.1 0.9 copy-start.2
  91.0 6.0 %copy-start.15 = (s32[16]{0:T(128)S(1)}, s32[16]{0:T(128)}, u32[]{:S(2)}) copy-start(s32[16]{0:T(128)} %anchor_hbm.1) | copy-start | bytes 196
  91.0 8.0 %copy-start.7 = (bf16[16,2,1024]{2,1,0:T(2,128)(2,1)S(1)}, bf16[16,2,1024]{2,1,0:T(2,128)(2,1)}, u32[]{:S(2)}) copy-start(bf16[16,2,1024]{2,1,0:T(2,128)(2,1)} %param.17) | copy-start | bytes 196612
  91.0 49.2 %all-to-all-start.1 = ((f32[64,6,4,128]{3,2,1,0:T(4,128)}), f32[64,6,4,128]{3,2,1,0:T(4,128)S(1)}, u32[]{:S(2)}, u32[]{:S(2)}) async-start(f32[64,6,4,128]{3,2,1,0:T(4,128)} %copy-done.2), calls=%async_computation.1 | async-start | bytes 1572864 | tf_op jit(solution)/shard_map/all_to_all | solution.py:206
  100.3 3.0 %copy-start.16 = (pred[16]{0:T(512)(128)(4,1)S(1)}, pred[16]{0:T(512)(128)(4,1)}, u32[]{:S(2)}) copy-start(pred[16]{0:T(512)(128)(4,1)} %get-tuple-element.12) | copy-start | bytes 52
  100.3 3.0 %copy-start.17 = (pred[16]{0:T(512)(128)(4,1)S(1)}, pred[16]{0:T(512)(128)(4,1)}, u32[]{:S(2)}) copy-start(pred[16]{0:T(512)(128)(4,1)} %get-tuple-element.16) | copy-start | bytes 52
  101.2 2.5 %copy-start.8 = (f32[16,1024]{1,0:T(8,128)S(1)}, f32[16,1024]{1,0:T(8,128)}, u32[]{:S(2)}) copy-start(f32[16,1024]{1,0:T(8,128)} %multiply_reduce_fusion) | copy-start | bytes 196612
  103.4 2.9 %copy-start.10 = (f32[16,1024]{1,0:T(8,128)S(1)}, f32[16,1024]{1,0:T(8,128)}, u32[]{:S(2)}) copy-start(f32[16,1024]{1,0:T(8,128)} %param.23) | copy-start | bytes 196612
  103.7 13.5 %copy-start.12 = (f32[1024]{0:T(1024)S(1)}, f32[1024]{0:T(1024)}, u32[]{:S(2)}) copy-start(f32[1024]{0:T(1024)} %param.24) | copy-start | bytes 12292
  104.2 18.3 %copy-start.13 = (f32[1024]{0:T(1024)S(1)}, f32[1024]{0:T(1024)}, u32[]{:S(2)}) copy-start(f32[1024]{0:T(1024)} %param.22) | copy-start | bytes 12292
  104.2 18.2 %copy-start.14 = (f32[512]{0:T(512)S(1)}, f32[512]{0:T(512)}, u32[]{:S(2)}) copy-start(f32[512]{0:T(512)} %param.25) | copy-start | bytes 6148
  104.2 3.3 %collective-permute-start = (f32[32,544]{1,0:T(8,128)S(1)}, f32[32,544]{1,0:T(8,128)S(1)}, u32[]{:S(2)}, u32[]{:S(2)}) collective-permute-start(f32[32,544]{1,0:T(8,128)S(1)} %fusion.5), channel_id=1, source_target_pairs={{0,1},{1,0},{2,3},{3,2},{4,5},{5,4},{6,7},{7,6},{8,9},{9,8},{10,11... | collective-permute-start | bytes 208904 | tf_op jit(solution)/shard_map/ppermute | solution.py:213
  107.5 6.4 %collective-permute-start.1 = (f32[32,544]{1,0:T(8,128)S(1)}, f32[32,544]{1,0:T(8,128)S(1)}, u32[]{:S(2)}, u32[]{:S(2)}) collective-permute-start(f32[32,544]{1,0:T(8,128)S(1)} %add.71), channel_id=1, source_target_pairs={{0,2},{1,3},{2,0},{3,1},{4,6},{5,7},{6,4},{7,5},{8,10},{9,11},{10,... | collective-permute-start | bytes 208904 | tf_op jit(solution)/shard_map/ppermute | solution.py:213
  110.3 29.9 %copy-start.1 = (f32[16,16,1024]{2,1,0:T(8,128)S(1)}, f32[16,16,1024]{2,1,0:T(8,128)}, u32[]{:S(2)}) copy-start(f32[16,16,1024]{2,1,0:T(8,128)} %state_ref.1) | copy-start | bytes 3145732
  110.3 29.9 %copy-start.3 = (bf16[16,2,1024]{2,1,0:T(2,128)(2,1)S(1)}, bf16[16,2,1024]{2,1,0:T(2,128)(2,1)}, u32[]{:S(2)}) copy-start(bf16[16,2,1024]{2,1,0:T(2,128)(2,1)} %gate_ref.1) | copy-start | bytes 196612
  110.3 29.8 %copy-start.4 = (s32[16]{0:T(128)S(1)}, s32[16]{0:T(128)}, u32[]{:S(2)}) copy-start(s32[16]{0:T(128)} %get-tuple-element.6.row_hbm) | copy-start | bytes 196
  114.0 7.8 %collective-permute-start.2 = (f32[32,544]{1,0:T(8,128)S(1)}, f32[32,544]{1,0:T(8,128)S(1)}, u32[]{:S(2)}, u32[]{:S(2)}) collective-permute-start(f32[32,544]{1,0:T(8,128)S(1)} %add.72), channel_id=1, source_target_pairs={{0,4},{1,5},{2,6},{3,7},{4,0},{5,1},{6,2},{7,3},{8,12},{9,13},{10,... | collective-permute-start | bytes 208904 | tf_op jit(solution)/shard_map/ppermute | solution.py:213
  121.8 0.6 copy-start.6

commit v9 on v7

--- a/solution.py
+++ b/solution.py
@@ -25,8 +25,8 @@
 
 def pack_kernel(
     me_ref, anchor_hbm, target_hbm, state_hbm, conv_hbm, taps_hbm,
-    leaving_hbm, offset_ref, row_ref, sums_ref,
-    leaving_ref, anchor_ref, target_ref, state_ref, conv_ref, taps_ref, slot_of, rank_of, source, sems, out_sems,
+    leaving_hbm, offset_hbm, row_hbm, sums_hbm,
+    leaving_ref, offset_ref, row_ref, sums_ref, anchor_ref, target_ref, state_ref, conv_ref, taps_ref, slot_of, rank_of, source, sems, out_sems,
 ):
     copies = begin(
         [
@@ -69,7 +69,13 @@
     taps = [taps_ref[i : i + 1, :] for i in range(3)]
     sums_ref[0] = old[0] * taps[0] + old[1] * taps[1] + old[2] * taps[2]
     sums_ref[1] = old[1] * taps[0] + old[2] * taps[1]
-    leaving = []
+    leaving = [
+        pltpu.make_async_copy(offset_ref, offset_hbm, out_sems.at[0]),
+        pltpu.make_async_copy(row_ref, row_hbm, out_sems.at[1]),
+        pltpu.make_async_copy(sums_ref, sums_hbm, out_sems.at[2]),
+    ]
+    for copy in leaving:
+        copy.start()
 
     def send(low, high):
         part = slice(low, high)
@@ -111,9 +117,12 @@
             jax.ShapeDtypeStruct((2, slots, width), jnp.float32),
         ),
         in_specs=[SMEM] + [ANY] * 5,
-        out_specs=(ANY, SMEM, SMEM, VMEM),
+        out_specs=(ANY,) * 4,
         scratch_shapes=[
             pltpu.VMEM((peers, 2 * TILES + CONV, 4, 128), jnp.float32),
+            pltpu.SMEM((16,), jnp.int32),
+            pltpu.SMEM((16,), jnp.int32),
+            pltpu.VMEM((2, slots, width), jnp.float32),
             pltpu.SMEM(anchor.shape, jnp.int32),
             pltpu.SMEM(target.shape, jnp.int32),
             pltpu.VMEM(ssm_state.shape, jnp.float32),
@@ -123,9 +132,9 @@
             pltpu.SMEM((peers,), jnp.int32),
             pltpu.SMEM((16,), jnp.int32),
             pltpu.SemaphoreType.DMA((5,)),
-            pltpu.SemaphoreType.DMA((TILES + 1,)),
+            pltpu.SemaphoreType.DMA((TILES + 4,)),
         ],
-        compiler_params=pltpu.CompilerParams(vmem_limit_bytes=54 << 20),
+        compiler_params=pltpu.CompilerParams(vmem_limit_bytes=56 << 20),
         name="pack",
     )(me, anchor, target, ssm_state, conv_state, conv_weight)
 
@@ -158,13 +167,16 @@
 
 def update_kernel(
     row_hbm, rest_ref, moved_ref, state_ref, step_ref, x_ref, skip_ref, decay_ref, gate_ref,
-    mixed_ref, out_hbm,
-    row_ref, out_ref, y_ref, row_sem, out_sems,
+    mixed_hbm, out_hbm,
+    row_ref, out_ref, y_ref, gated_ref, mixed_ref, row_sem, out_sems,
 ):
-    for copy in begin([(row_hbm, row_ref)], row_sem):
-        copy.wait()
+    arriving = begin([(row_hbm, row_ref)], row_sem)
     slots, state_size, width = state_ref.shape
     steps = step_ref.shape[0]
+    for s in range(slots):
+        gated_ref[s] = jax.nn.silu(gate_ref[s].astype(jnp.float32))
+    for copy in arriving:
+        copy.wait()
     copies = []
     for s in range(slots):
         r = row_ref[s]
@@ -185,8 +197,9 @@
             out_ref[s, :, cut] = state
         copies.append(pltpu.make_async_copy(out_ref.at[s], out_hbm.at[s], out_sems.at[s]))
         copies[-1].start()
-        gate = gate_ref[s].astype(jnp.float32)
-        mixed_ref[s] = ((y_ref[s] + skip_ref[s]) * jax.nn.silu(gate)).astype(mixed_ref.dtype)
+        mixed_ref[s] = ((y_ref[s] + skip_ref[s]) * gated_ref[s]).astype(mixed_ref.dtype)
+    copies.append(pltpu.make_async_copy(mixed_ref, mixed_hbm, out_sems.at[slots]))
+    copies[-1].start()
     for copy in copies:
         copy.wait()
 
@@ -199,13 +212,15 @@
             jax.ShapeDtypeStruct(state.shape, jnp.float32),
         ),
         in_specs=[ANY] + [VMEM] * 8,
-        out_specs=(VMEM, ANY),
+        out_specs=(ANY, ANY),
         scratch_shapes=[
             pltpu.SMEM(row.shape, jnp.int32),
             pltpu.VMEM(state.shape, jnp.float32),
             pltpu.VMEM(gate.shape, jnp.float32),
+            pltpu.VMEM(gate.shape, jnp.float32),
+            pltpu.VMEM(gate.shape, jnp.bfloat16),
             pltpu.SemaphoreType.DMA((1,)),
-            pltpu.SemaphoreType.DMA((state.shape[0],)),
+            pltpu.SemaphoreType.DMA((state.shape[0] + 1,)),
         ],
         compiler_params=pltpu.CompilerParams(vmem_limit_bytes=32 << 20),
         name="update",

time: 144 us -> 143 us (level)
  no operation moved by 1% of the time
where the time goes in v9:
time: 143 us; the launch traced here: 142 us
  waiting for transfers between devices  91.6 us (64%)
  starting transfers between devices  32.9 us (23%)
  Pallas kernels  6.26 us (4%)
  local copies, waits for them, and re-layouts  5.38 us (4%)
  other arithmetic  3.12 us (2%)
  matrix products  2.06 us (1%)
    all_to_all x2, waiting for transfers between devices, exchange(): return lax.all_to_all(chunks, 'inst', 0, 0)  82.5 us
    all_to_all x2, starting transfers between devices, exchange(): return lax.all_to_all(chunks, 'inst', 0, 0)  24.8 us
    ppermute x3, waiting for transfers between devices, sum_over_tp(): part = part + lax.ppermute(part, 'tp', [(i, i ^ bit) for i in range(size)])  9.19 us
    ppermute x3, starting transfers between devices, sum_over_tp(): part = part + lax.ppermute(part, 'tp', [(i, i ^ bit) for i in range(size)])  8.1 us
  transfers between devices with their start and end apart: 5, of which 5 were waited for; matrix products, arithmetic and copies ran while one was open for 6% of the time, Pallas kernels for 0%

profile of v9, /device:TPU:6, one launch (start us, length us, event | category | flops | bytes accessed | tf_op | source)
XLA Modules:
  0.0 142.4 jit_solution(6734685197095866293)
XLA Ops:
  0.7 2.6 %pack.1 = (f32[64,10,4,128]{3,2,1,0:T(4,128)}, s32[16]{0:T(128)}, s32[16]{0:T(128)}, f32[2,16,1024]{2,1,0:T(8,128)}) custom-call(s32[1]{0:T(128)} %bitcast.me_ref, s32[16]{0:T(128)} %anchor_hbm.1, s32[16]{0:T(128)} %target_hbm.1, f32[16,16,1024]{2,1,0:T(8,128)} %state_ref.1, f32[3,16,1024]{2,1,0:T(8,128)} %bitcast.24, f32[4,1024]{1,0:T(4,128)} %taps_hbm.1), custom_call_target="tpu_custom_call" | custom-call | tf_op jit(solution)/shard_map/pack/pallas_call | solution.py:111
  3.3 18.9 %all-to-all-start = ((f32[64,10,4,128]{3,2,1,0:T(4,128)}), f32[64,10,4,128]{3,2,1,0:T(4,128)S(1)}, u32[]{:S(2)}, u32[]{:S(2)}) async-start(f32[64,10,4,128]{3,2,1,0:T(4,128)} %get-tuple-element.8), calls=%async_computation | async-start | bytes 2621440 | tf_op jit(solution)/shard_map/all_to_all | solution.py:231
  22.2 0.1 copy.22
  22.3 66.4 %all-to-all-done.held_ref = f32[64,10,4,128]{3,2,1,0:T(4,128)S(1)} async-done(((f32[64,10,4,128]{3,2,1,0:T(4,128)}), f32[64,10,4,128]{3,2,1,0:T(4,128)S(1)}, u32[]{:S(2)}, u32[]{:S(2)}) %all-to-all-start) | async-done | bytes 1310752 | tf_op jit(solution)/shard_map/all_to_all | solution.py:231
  88.7 1.3 roll.1
  90.0 0.9 copy-done.2
  90.8 6.0 %all-to-all-start.1 = ((f32[64,6,4,128]{3,2,1,0:T(4,128)}), f32[64,6,4,128]{3,2,1,0:T(4,128)S(1)}, u32[]{:S(2)}, u32[]{:S(2)}) async-start(f32[64,6,4,128]{3,2,1,0:T(4,128)} %copy-done.2), calls=%async_computation.1 | async-start | bytes 1572864 | tf_op jit(solution)/shard_map/all_to_all | solution.py:231
  96.8 0.6 compare_and_fusion.1
  97.4 0.7 gather_fusion
  98.1 0.7 compare_select_fusion.1
  98.8 0.6 multiply_reduce_fusion
  99.4 0.7 compare_and_fusion
  100.1 0.8 slice.36
  101.0 1.5 %reshape.50 = f32[64,2,1024]{2,1,0:T(2,128)S(1)} reshape(f32[64,4,4,128]{3,2,1,0:T(4,128)} %slice.36) | data formatting | bytes 1048576 | tf_op jit(solution)/shard_map/reshape | solution.py:268
  102.5 0.7 gather_fusion.1
  103.2 0.2 select_select_fusion
  103.4 0.1 fusion.6
  103.5 0.1 multiply_convert_fusion.1
  103.6 0.4 fusion.5
  104.0 2.1 %collective-permute-start = (f32[32,544]{1,0:T(8,128)S(1)}, f32[32,544]{1,0:T(8,128)S(1)}, u32[]{:S(2)}, u32[]{:S(2)}) collective-permute-start(f32[32,544]{1,0:T(8,128)S(1)} %fusion.5), channel_id=1, source_target_pairs={{0,1},{1,0},{2,3},{3,2},{4,5},{5,4},{6,7},{7,6},{8,9},{9,8},{10,11... | collective-permute-start | bytes 208904 | tf_op jit(solution)/shard_map/ppermute | solution.py:238
  106.1 1.2 collective-permute-done
  107.4 2.7 %collective-permute-start.1 = (f32[32,544]{1,0:T(8,128)S(1)}, f32[32,544]{1,0:T(8,128)S(1)}, u32[]{:S(2)}, u32[]{:S(2)}) collective-permute-start(f32[32,544]{1,0:T(8,128)S(1)} %add.71), channel_id=1, source_target_pairs={{0,2},{1,3},{2,0},{3,1},{4,6},{5,7},{6,4},{7,5},{8,10},{9,11},{10,... | collective-permute-start | bytes 208904 | tf_op jit(solution)/shard_map/ppermute | solution.py:238
  110.2 3.6 %collective-permute-done.1 = f32[32,544]{1,0:T(8,128)S(1)} collective-permute-done((f32[32,544]{1,0:T(8,128)S(1)}, f32[32,544]{1,0:T(8,128)S(1)}, u32[]{:S(2)}, u32[]{:S(2)}) %collective-permute-start.1) | collective-permute-done | bytes 69664 | tf_op jit(solution)/shard_map/ppermute | solution.py:238
  113.8 3.3 %collective-permute-start.2 = (f32[32,544]{1,0:T(8,128)S(1)}, f32[32,544]{1,0:T(8,128)S(1)}, u32[]{:S(2)}, u32[]{:S(2)}) collective-permute-start(f32[32,544]{1,0:T(8,128)S(1)} %add.72), channel_id=1, source_target_pairs={{0,4},{1,5},{2,6},{3,7},{4,0},{5,1},{6,2},{7,3},{8,12},{9,13},{10,... | collective-permute-start | bytes 208904 | tf_op jit(solution)/shard_map/ppermute | solution.py:238
  117.1 0.1 fusion.skip_ref
  117.2 4.4 %collective-permute-done.2 = f32[32,544]{1,0:T(8,128)S(1)} collective-permute-done((f32[32,544]{1,0:T(8,128)S(1)}, f32[32,544]{1,0:T(8,128)S(1)}, u32[]{:S(2)}, u32[]{:S(2)}) %collective-permute-start.2) | collective-permute-done | bytes 69664 | tf_op jit(solution)/shard_map/ppermute | solution.py:238
  121.6 0.1 copy.25
  121.7 0.1 multiply_reduce_fusion.1
  121.8 0.4 copy-done.6
  122.3 1.6 %compare_select_fusion = f32[32,1024]{1,0:T(8,128)S(1)} fusion(bf16[512,1024]{1,0:T(8,128)(2,1)} %param.21, f32[1024]{0:T(1024)S(1)} %copy-done.13, f32[32,544]{1,0:T(8,128)} %copy-done.6, f32[512]{0:T(512)S(1)} %copy-done.14, f32[32]{0:T(128)S(1)} %add_rsqrt_fusion), kind=kOutput, calls=%fused_computation.3 | convolution fusion | flops 33832960 | bytes 1251456 | tf_op jit(solution)/shard_map/dot_general | solution.py:284
  123.9 16.1 %all-to-all-done.1.moved_ref = f32[64,6,4,128]{3,2,1,0:T(4,128)S(1)} async-done(((f32[64,6,4,128]{3,2,1,0:T(4,128)}), f32[64,6,4,128]{3,2,1,0:T(4,128)S(1)}, u32[]{:S(2)}, u32[]{:S(2)}) %all-to-all-start.1) | async-done | bytes 786464 | tf_op jit(solution)/shard_map/all_to_all | solution.py:231
  140.0 2.4 %update.1 = (bf16[16,2,1024]{2,1,0:T(2,128)(2,1)}, f32[16,16,1024]{2,1,0:T(8,128)}) custom-call(s32[16]{0:T(128)S(1)} %copy-done.4, f32[2,32,16]{2,1,0:T(8,128)S(1)} %bitcast.22, f32[64,6,4,128]{3,2,1,0:T(4,128)S(1)} %all-to-all-done.1.moved_ref, f32[16,16,1024]{2,1,0:T(8,128)S(1)} %copy-done.1, f32[2,16,1024]{2,1,0:T(8,128)S(1)} %bitcast.21, ...), custom_call_target="tpu_custom_call" | custom-call | tf_op jit(solution)/shard_map/update/pallas_call | solution.py:208
  (47 shorter events, 0.2 us)
Async XLA Ops:
  0.6 102.9 %copy-start = (bf16[1024,544]{0,1:T(8,128)(2,1)S(1)}, bf16[1024,544]{0,1:T(8,128)(2,1)}, u32[]{:S(2)}) copy-start(bf16[1024,544]{0,1:T(8,128)(2,1)} %param.20) | copy-start | bytes 3342340
  3.2 18.9 %copy-start.11 = (f32[4,1024]{1,0:T(4,128)S(1)}, f32[4,1024]{1,0:T(4,128)}, u32[]{:S(2)}) copy-start(f32[4,1024]{1,0:T(4,128)} %taps_hbm.1) | copy-start | bytes 49156
  3.2 18.9 %copy-start.9 = (f32[2,16,1024]{2,1,0:T(8,128)S(1)}, f32[2,16,1024]{2,1,0:T(8,128)}, u32[]{:S(2)}) copy-start(f32[2,16,1024]{2,1,0:T(8,128)} %get-tuple-element.7) | copy-start | bytes 393220
  3.2 85.4 %copy-start.5 = (s32[16]{0:T(128)S(1)}, s32[16]{0:T(128)}, u32[]{:S(2)}) copy-start(s32[16]{0:T(128)} %get-tuple-element.9.offset_ref) | copy-start | bytes 196
  3.3 85.4 %all-to-all-start = ((f32[64,10,4,128]{3,2,1,0:T(4,128)}), f32[64,10,4,128]{3,2,1,0:T(4,128)S(1)}, u32[]{:S(2)}, u32[]{:S(2)}) async-start(f32[64,10,4,128]{3,2,1,0:T(4,128)} %get-tuple-element.8), calls=%async_computation | async-start | bytes 2621440 | tf_op jit(solution)/shard_map/all_to_all | solution.py:231
  89.9 0.9 copy-start.2
  90.8 6.0 %copy-start.15 = (s32[16]{0:T(128)S(1)}, s32[16]{0:T(128)}, u32[]{:S(2)}) copy-start(s32[16]{0:T(128)} %anchor_hbm.1) | copy-start | bytes 196
  90.8 8.0 %copy-start.7 = (bf16[16,2,1024]{2,1,0:T(2,128)(2,1)S(1)}, bf16[16,2,1024]{2,1,0:T(2,128)(2,1)}, u32[]{:S(2)}) copy-start(bf16[16,2,1024]{2,1,0:T(2,128)(2,1)} %param.17) | copy-start | bytes 196612
  90.8 49.2 %all-to-all-start.1 = ((f32[64,6,4,128]{3,2,1,0:T(4,128)}), f32[64,6,4,128]{3,2,1,0:T(4,128)S(1)}, u32[]{:S(2)}, u32[]{:S(2)}) async-start(f32[64,6,4,128]{3,2,1,0:T(4,128)} %copy-done.2), calls=%async_computation.1 | async-start | bytes 1572864 | tf_op jit(solution)/shard_map/all_to_all | solution.py:231
  100.1 3.0 %copy-start.16 = (pred[16]{0:T(512)(128)(4,1)S(1)}, pred[16]{0:T(512)(128)(4,1)}, u32[]{:S(2)}) copy-start(pred[16]{0:T(512)(128)(4,1)} %get-tuple-element.12) | copy-start | bytes 52
  100.1 3.0 %copy-start.17 = (pred[16]{0:T(512)(128)(4,1)S(1)}, pred[16]{0:T(512)(128)(4,1)}, u32[]{:S(2)}) copy-start(pred[16]{0:T(512)(128)(4,1)} %get-tuple-element.16) | copy-start | bytes 52
  101.0 2.5 %copy-start.8 = (f32[16,1024]{1,0:T(8,128)S(1)}, f32[16,1024]{1,0:T(8,128)}, u32[]{:S(2)}) copy-start(f32[16,1024]{1,0:T(8,128)} %multiply_reduce_fusion) | copy-start | bytes 196612
  103.2 2.9 %copy-start.10 = (f32[16,1024]{1,0:T(8,128)S(1)}, f32[16,1024]{1,0:T(8,128)}, u32[]{:S(2)}) copy-start(f32[16,1024]{1,0:T(8,128)} %param.23) | copy-start | bytes 196612
  103.6 13.5 %copy-start.12 = (f32[1024]{0:T(1024)S(1)}, f32[1024]{0:T(1024)}, u32[]{:S(2)}) copy-start(f32[1024]{0:T(1024)} %param.24) | copy-start | bytes 12292
  104.0 18.3 %copy-start.13 = (f32[1024]{0:T(1024)S(1)}, f32[1024]{0:T(1024)}, u32[]{:S(2)}) copy-start(f32[1024]{0:T(1024)} %param.22) | copy-start | bytes 12292
  104.0 18.2 %copy-start.14 = (f32[512]{0:T(512)S(1)}, f32[512]{0:T(512)}, u32[]{:S(2)}) copy-start(f32[512]{0:T(512)} %param.25) | copy-start | bytes 6148
  104.0 3.3 %collective-permute-start = (f32[32,544]{1,0:T(8,128)S(1)}, f32[32,544]{1,0:T(8,128)S(1)}, u32[]{:S(2)}, u32[]{:S(2)}) collective-permute-start(f32[32,544]{1,0:T(8,128)S(1)} %fusion.5), channel_id=1, source_target_pairs={{0,1},{1,0},{2,3},{3,2},{4,5},{5,4},{6,7},{7,6},{8,9},{9,8},{10,11... | collective-permute-start | bytes 208904 | tf_op jit(solution)/shard_map/ppermute | solution.py:238
  107.4 6.4 %collective-permute-start.1 = (f32[32,544]{1,0:T(8,128)S(1)}, f32[32,544]{1,0:T(8,128)S(1)}, u32[]{:S(2)}, u32[]{:S(2)}) collective-permute-start(f32[32,544]{1,0:T(8,128)S(1)} %add.71), channel_id=1, source_target_pairs={{0,2},{1,3},{2,0},{3,1},{4,6},{5,7},{6,4},{7,5},{8,10},{9,11},{10,... | collective-permute-start | bytes 208904 | tf_op jit(solution)/shard_map/ppermute | solution.py:238
  110.1 29.9 %copy-start.1 = (f32[16,16,1024]{2,1,0:T(8,128)S(1)}, f32[16,16,1024]{2,1,0:T(8,128)}, u32[]{:S(2)}) copy-start(f32[16,16,1024]{2,1,0:T(8,128)} %state_ref.1) | copy-start | bytes 3145732
  110.1 29.9 %copy-start.3 = (bf16[16,2,1024]{2,1,0:T(2,128)(2,1)S(1)}, bf16[16,2,1024]{2,1,0:T(2,128)(2,1)}, u32[]{:S(2)}) copy-start(bf16[16,2,1024]{2,1,0:T(2,128)(2,1)} %gate_ref.1) | copy-start | bytes 196612
  110.2 29.8 %copy-start.4 = (s32[16]{0:T(128)S(1)}, s32[16]{0:T(128)}, u32[]{:S(2)}) copy-start(s32[16]{0:T(128)} %get-tuple-element.6.row_hbm) | copy-start | bytes 196
  113.8 7.8 %collective-permute-start.2 = (f32[32,544]{1,0:T(8,128)S(1)}, f32[32,544]{1,0:T(8,128)S(1)}, u32[]{:S(2)}, u32[]{:S(2)}) collective-permute-start(f32[32,544]{1,0:T(8,128)S(1)} %add.72), channel_id=1, source_target_pairs={{0,4},{1,5},{2,6},{3,7},{4,0},{5,1},{6,2},{7,3},{8,12},{9,13},{10,... | collective-permute-start | bytes 208904 | tf_op jit(solution)/shard_map/ppermute | solution.py:238
  121.6 0.6 copy-start.6
